TPU v7x, 32 devices: a whole 2x2x4 slice. The times are simulated.
32 devices in a mesh: worker: 8 (over y, x, core), fsdp: 4 (over z).
Axes of the slice: x: 2, y: 2, z: 4, core: 2. Of those that a mesh axis runs over, the one named last changes fastest.
Arguments:
- tokens: bfloat16 [2048, 8192], P('worker', 'fsdp'), may hold values from -6 to 6
- inner_weight: bfloat16 [8, 8192, 512], P('worker', 'fsdp'), may hold values from -0.0625 to 0.0625
- key_grad: bfloat16 [2048, 512], P(('worker', 'fsdp')), may hold values from -6 to 6
- anchor: float32 [8192, 512], P('fsdp'), may hold values from -0.0625 to 0.0625
- momentum: float32 [8192, 512], P('fsdp'), may hold values from -0.06 to 0.06
- stale_delta: bfloat16 [8, 8192, 512], P('worker', 'fsdp'), may hold values from -0.29882812 to 0.29882812
Outputs:
- keys: bfloat16 [2048, 512], P(('worker', 'fsdp'))
- input_grad: bfloat16 [2048, 8192], P('worker', 'fsdp')
- new_params: bfloat16 [8, 8192, 512], P('worker', 'fsdp')
- new_momentum: float32 [8192, 512], P(('fsdp', 'worker'))
- fresh_delta: bfloat16 [8, 8192, 512], P('worker', 'fsdp')
All inputs are finite; a program needn't handle non-finite values.
Results may differ from a plain program's by a relative error of at most 0.001.
Values may be sent and summed in bfloat16 or wider, within the bound.
No kernel may reach another device: no remote copies, remote signals or barrier semaphores. Data moves between devices by JAX's collectives and lax.ppermute only.
A program may use at most 64 MiB of HBM per device.

v0:
```python
import jax
import jax.numpy as jnp
from jax import lax
from jax.sharding import PartitionSpec as P

inner_rate = 0.0005
outer_rate = 0.7
outer_momentum = 0.9


def local(tokens, inner_weight, key_grad, anchor, momentum, stale_delta):
    weights = inner_weight[0]
    inputs = tokens
    key_out = lax.psum_scatter(
        jnp.dot(inputs, weights, preferred_element_type=jnp.float32),
        "fsdp",
        scatter_dimension=0,
        tiled=True,
    ).astype(jnp.bfloat16)
    portion = lax.all_gather(key_grad, "fsdp", axis=0, tiled=True)
    inputs = tokens
    grad_weight = lax.dot_general(
        inputs, portion, (((0,), (0,)), ((), ())), preferred_element_type=jnp.float32
    )
    product = lax.dot_general(
        portion, weights, (((1,), (1,)), ((), ())), preferred_element_type=jnp.float32
    )
    grad_input = product
    grad_weight, grad_input = (grad_weight, grad_input)
    fresh_term = anchor - (weights.astype(jnp.float32) - inner_rate * grad_weight)
    stale_value = stale_delta[0].astype(jnp.float32)
    workers = lax.axis_size("worker")
    share_rows = anchor.shape[0] // workers
    worker_index = lax.axis_index("worker")
    summed = lax.psum(stale_value, "worker")
    average = summed / workers
    moment_full = outer_momentum * momentum + average
    common_term = average + outer_momentum * moment_full
    new_moment = lax.dynamic_slice_in_dim(moment_full, worker_index * share_rows, share_rows, 0)
    updated = anchor - outer_rate * (common_term + (fresh_term - stale_value) / workers)
    fresh_out = fresh_term[None].astype(jnp.bfloat16)
    return (
        key_out,
        grad_input.astype(jnp.bfloat16),
        updated[None].astype(jnp.bfloat16),
        new_moment,
        fresh_out,
    )


def solution(mesh):
    in_specs = (
        P("worker", "fsdp"),
        P("worker", "fsdp", None),
        P(("worker", "fsdp"), None),
        P("fsdp", None),
        P("fsdp", None),
        P("worker", "fsdp", None),
    )
    out_specs = (
        P(("worker", "fsdp"), None),
        P("worker", "fsdp"),
        P("worker", "fsdp", None),
        P(("fsdp", "worker"), None),
        P("worker", "fsdp", None),
    )
    return jax.shard_map(local, mesh=mesh, in_specs=in_specs, out_specs=out_specs, check_vma=False)
```

profile of v0, /device:TPU:0, one launch (start us, length us, event | category | flops | bytes accessed | tf_op | source)
XLA Modules:
  0.0 115.4 jit_solution(13689509371087794594)
XLA Ops:
  8.0 0.0 copy-start
  8.0 0.0 copy-start.1
  8.0 0.0 reduce-scatter.2.cloned.1.call-start
  8.1 1.2 %copy-done = bf16[256,2048]{1,0:T(8,128)(2,1)S(1)} copy-done((bf16[256,2048]{1,0:T(8,128)(2,1)S(1)}, bf16[256,2048]{1,0:T(8,128)(2,1)}, u32[]{:S(2)}) %copy-start) | copy-done | bytes 1048600
  9.2 3.1 %fusion.2 = f32[256,512]{1,0:T(8,128)} fusion(bf16[256,2048]{1,0:T(8,128)(2,1)S(1)} %copy-done, bf16[1,2048,512]{2,1,0:T(8,128)(2,1)} %param.7), kind=kOutput, calls=%fused_computation.7 | convolution fusion | flops 536870912 | bytes 3670016 | tf_op jit(solution)/shard_map/dot_general | solution.py:15
  12.3 0.0 reduce-scatter.2.cloned.1.call-update
  12.3 0.0 copy-start.2
  12.4 0.0 all-reduce.2.cloned.1.call-start
  12.4 0.0 copy-done.1
  12.4 2.6 %bitcast_convert_fusion = f32[2048,512]{1,0:T(8,128)} fusion(bf16[1,2048,512]{2,1,0:T(8,128)(2,1)S(1)} %copy-done.1), kind=kLoop, calls=%fused_computation.5 | loop fusion | flops 1048576 | bytes 6291456 | tf_op jit(solution)/shard_map/convert_element_type | solution.py:31
  15.0 0.0 all-reduce.2.cloned.1.call-update
  15.0 0.0 copy-done.2
  15.0 17.7 %all_gather.3 = bf16[256,512]{1,0:T(8,128)(2,1)S(1)} all-gather(bf16[64,512]{1,0:T(8,128)(2,1)S(1)} %copy-done.2), channel_id=1, replica_groups=mesh['worker'=8,'fsdp'=4] {'fsdp'}, dimensions={0}, use_global_device_ids=true | all-gather | bytes 327680 | tf_op jit(solution)/shard_map/all_gather | solution.py:20
  32.7 3.4 %convolution_convert_fusion = bf16[256,2048]{1,0:T(8,128)(2,1)} fusion(bf16[256,512]{1,0:T(8,128)(2,1)S(1)} %all_gather.3, bf16[1,2048,512]{2,1,0:T(8,128)(2,1)} %param.7), kind=kOutput, calls=%fused_computation.3 | convolution fusion | flops 537395200 | bytes 3407872 | tf_op jit(solution)/shard_map/dot_general | solution.py:25
  36.1 1.4 %reduce-scatter.2.cloned.1.call-done = f32[64,512]{1,0:T(8,128)} async-done(((f32[256,512]{1,0:T(8,128)}), f32[64,512]{1,0:T(8,128)}) %reduce-scatter.2.cloned.1.call-update) | async-done | bytes 131088 | tf_op jit(solution)/shard_map/reduce_scatter | solution.py:14
  37.5 1.5 %convert_element_type.27 = bf16[64,512]{1,0:T(8,128)(2,1)} convert(f32[64,512]{1,0:T(8,128)} %reduce-scatter.2.cloned.1.call-done) | non-fusion elementwise | flops 32768 | bytes 196608 | tf_op jit(solution)/shard_map/convert_element_type | solution.py:19
  39.1 60.3 %all-reduce.2.cloned.1.call-done = f32[2048,512]{1,0:T(8,128)} async-done(((f32[2048,512]{1,0:T(8,128)}), f32[2048,512]{1,0:T(8,128)}) %all-reduce.2.cloned.1.call-update) | async-done | bytes 4194320 | tf_op jit(solution)/shard_map/psum | solution.py:35
  99.4 7.8 %multiply_add_fusion = (f32[2048,512]{1,0:T(8,128)S(1)}, bf16[1,2048,512]{2,1,0:T(8,128)(2,1)}, bf16[1,2048,512]{2,1,0:T(8,128)(2,1)}) fusion(f32[2048,512]{1,0:T(8,128)} %param.10, f32[2048,512]{1,0:T(8,128)} %all-reduce.2.cloned.1.call-done, f32[2048,512]{1,0:T(8,128)} %param.9, bf16[1,2048,512]{2,1,0:T(8,128)(2,1)S(1)} %copy-done.1, ...), kind=kOutput, calls=%fused_computation.2 | convolution fusion | flops 554696704 | bytes 26476544 | tf_op jit(solution)/shard_map/dot_general | solution.py:22
  107.2 0.8 constant_dynamic-slice_fusion
Async XLA Ops:
  8.0 1.2 %copy-start = (bf16[256,2048]{1,0:T(8,128)(2,1)S(1)}, bf16[256,2048]{1,0:T(8,128)(2,1)}, u32[]{:S(2)}) copy-start(bf16[256,2048]{1,0:T(8,128)(2,1)} %param.6) | copy-start | bytes 3145732
  8.0 4.4 %copy-start.1 = (bf16[1,2048,512]{2,1,0:T(8,128)(2,1)S(1)}, bf16[1,2048,512]{2,1,0:T(8,128)(2,1)}, u32[]{:S(2)}) copy-start(bf16[1,2048,512]{2,1,0:T(8,128)(2,1)} %param.11) | copy-start | bytes 6291460
  8.0 29.5 %reduce-scatter.2.cloned.1.call-start = ((), (), s32[]{:S(2)}) async-start(), calls=%async_computation.1 | async-start | bytes 655360 | tf_op jit(solution)/shard_map/reduce_scatter | solution.py:14
  12.3 2.7 %copy-start.2 = (bf16[64,512]{1,0:T(8,128)(2,1)S(1)}, bf16[64,512]{1,0:T(8,128)(2,1)}, u32[]{:S(2)}) copy-start(bf16[64,512]{1,0:T(8,128)(2,1)} %param.8) | copy-start | bytes 196612
  12.4 87.1 %all-reduce.2.cloned.1.call-start = ((), (), s32[]{:S(2)}) async-start(), calls=%async_computation.2 | async-start | bytes 8388608 | tf_op jit(solution)/shard_map/psum | solution.py:35
Sparse Core Ops, SparseCore 0:
  12.5 25.0 reduce-scatter.1
Sparse Core Ops, SparseCore 1:
  16.1 83.3 all-reduce.1
where the time goes:
time: 116 us; the launch traced here: 115 us
  waiting for transfers between devices  61.8 us (53%)
  blocking collectives  17.7 us (15%)
  between operations  15.5 us (13%)
  matrix products  14.2 us (12%)
  other arithmetic  4.11 us (4%)
  local copies, waits for them, and re-layouts  2.01 us (2%)
    psum x1, waiting for transfers between devices, local(): summed = lax.psum(stale_value, 'worker')  60.3 us
    all_gather x1, blocking collectives, local(): portion = lax.all_gather(key_grad, 'fsdp', axis=0, tiled=True)  17.7 us
    dot_general x1, matrix products, local(): lax.dot_general(inputs, portion, (((0,), (0,)), ((), ())), preferred_elem...  7.76 us
    dot_general x1, matrix products, local(): lax.dot_general(portion, weights, (((1,), (1,)), ((), ())), preferred_ele...  3.37 us
    dot_general x1, matrix products, local(): jnp.dot(inputs, weights, preferred_element_type=jnp.float32)  3.09 us
    convert_element_type x1, other arithmetic, local(): stale_value = stale_delta[0].astype(jnp.float32)  2.56 us
  transfers between devices with their start and end apart: 2, of which 2 were waited for; matrix products, arithmetic and copies ran while one was open for 6% of the time, Pallas kernels for 0%

commit v1 on v0

v1 whole, which is shorter than its diff:
```python
import functools
import math

import jax
import jax.numpy as jnp
from jax import lax
from jax.experimental import pallas as pl
from jax.experimental.pallas import tpu as pltpu
from jax.sharding import PartitionSpec as P

inner_rate = 0.0005
outer_rate = 0.7
outer_momentum = 0.9

stale_bound = 0.29882812
floor = 2.0**-14
power = 250.0 / math.log2(1.0 + stale_bound / floor)


def encode(value, count):
    grown = jnp.log(jnp.abs(value) * (1.0 / (floor * count)) + 1.0)
    code = jnp.exp2(grown * (power / math.log(2.0)) - 125.0)
    return jnp.where(value < 0, -code, code).astype(jnp.bfloat16)


def decode(code, count):
    code = code.astype(jnp.float32)
    grown = jnp.exp2(jnp.log(jnp.abs(code)) * (1.0 / (power * math.log(2.0))) + 125.0 / power)
    value = (grown - 1.0) * (floor * count)
    return jnp.where(code < 0, -value, value)


def place(me):
    core, low, high = me % 2, (me // 2) % 2, me // 4
    return core, jnp.where(core == 0, low, high), jnp.where(core == 0, high, low)


def block(region, half, sub):
    return jnp.where(region == 0, 4 * sub + 2 * half, 4 * half + 2 * sub + 1)


def call(kernel, me, grid, ins, outs, scratch=(), aliases=None, flops=0, vmem=None):
    def spec(shape, index):
        if shape is None:
            return pl.BlockSpec(memory_space=pl.ANY)
        return pl.BlockSpec(shape, lambda i, me_ref: index(i, me_ref[0]))

    moved = sum(math.prod(s) * 4 * grid for _, s, _ in ins if s is not None)
    moved += sum(math.prod(s) * 4 * grid for _, _, s, _ in outs)
    return pl.pallas_call(
        kernel,
        grid_spec=pltpu.PrefetchScalarGridSpec(
            num_scalar_prefetch=1,
            grid=(grid,),
            in_specs=[spec(s, f) for _, s, f in ins],
            out_specs=[spec(s, f) for _, _, s, f in outs],
            scratch_shapes=scratch,
        ),
        out_shape=[jax.ShapeDtypeStruct(shape, dtype) for shape, dtype, _, _ in outs],
        input_output_aliases=aliases or {},
        cost_estimate=pl.CostEstimate(flops=flops, bytes_accessed=moved, transcendentals=0),
        compiler_params=pltpu.CompilerParams(vmem_limit_bytes=vmem or 32 * 2**20),
    )(me, *[a for a, _, _ in ins])


def copy_kernel(me_ref, value, out):
    out[...] = value[...]


def pair_kernel(me_ref, send_own, keep_own, send_other, keep_other, code, keep):
    f32 = jnp.float32
    code[...] = encode(send_own[...].astype(f32) + send_other[...].astype(f32), 2)
    keep[...] = keep_own[...].astype(f32) + keep_other[...].astype(f32)


def add_kernel(held, total, me_ref, value, received, out, code):
    summed = value[...] + decode(received[...], held)
    out[...] = summed
    code[...] = encode(summed, total)


def keys_kernel(parts, me_ref, tokens, weights, *rest):
    outs, total = rest[:parts], rest[parts]
    step = pl.program_id(0)
    product = jnp.dot(tokens[...], weights[...], preferred_element_type=jnp.float32)

    @pl.when(step == 0)
    def _():
        total[...] = product

    @pl.when(step > 0)
    def _():
        total[...] += product

    @pl.when(step == pl.num_programs(0) - 1)
    def _():
        rows = total.shape[0] // parts
        for d in range(parts):
            at = pl.multiple_of((me_ref[1] ^ d) * rows, rows)
            outs[d][...] = total[pl.ds(at, rows), :]


def fresh_kernel(parts, workers, filled, me_ref, tokens, weights, anchor, momentum, stale, *rest):
    grads, rest = rest[:parts], rest[parts:]
    if filled:
        rest = rest[3:]
    fresh_out, base_out, grad_out, portion = rest

    @pl.when(pl.program_id(0) == 0)
    def _():
        rows = grads[0].shape[0]
        for d in range(parts):
            at = pl.multiple_of((me_ref[1] ^ d) * rows, rows)
            portion[pl.ds(at, rows), :] = grads[d][...]

    grad_weight = lax.dot_general(
        tokens[...], portion[...], (((0,), (0,)), ((), ())), preferred_element_type=jnp.float32
    )
    grad_out[...] = lax.dot_general(
        portion[...], weights[...], (((1,), (1,)), ((), ())), preferred_element_type=jnp.float32
    ).astype(jnp.bfloat16)
    fresh = anchor[...] - (weights[...].astype(jnp.float32) - inner_rate * grad_weight)
    fresh_out[...] = fresh.astype(jnp.bfloat16)
    base_out[...] = anchor[...] - outer_rate * (
        outer_momentum * outer_momentum * momentum[...] + (fresh - stale[...].astype(jnp.float32)) / workers
    )


def final_kernel(subs, workers, kinds, filled, me_ref, base, *rest):
    pieces = rest[: len(kinds)]
    out = rest[-1]
    for at in range(len(kinds)):

        @pl.when(pl.program_id(0) // subs == at)
        def _(at=at):
            total = pieces[at][...]
            if kinds[at] != "own":
                total = decode(total, workers)
            out[...] = (base[...] - (outer_rate * (1.0 + outer_momentum) / workers) * total).astype(jnp.bfloat16)


chunk_subs = ((0,), (1,))


def fast(tokens, inner_weight, key_grad, anchor, momentum, stale_delta):
    workers, shards = lax.axis_size("worker"), lax.axis_size("fsdp")
    f32, bf16 = jnp.float32, jnp.bfloat16
    weights, stale = inner_weight[0], stale_delta[0]
    rows, columns = stale.shape
    size = rows // workers
    window = (size, columns)
    worker = lax.axis_index("worker")
    me = jnp.stack([worker, lax.axis_index("fsdp")]).astype(jnp.int32)

    def swap(value, flips):
        return lax.ppermute(value, "worker", [(i, i ^ flips[i % 2]) for i in range(workers)])

    beside, first, last = (1, 1), (2, 4), (4, 2)

    grads = [key_grad] + [
        lax.ppermute(key_grad, "fsdp", [(i, i ^ d) for i in range(shards)]) for d in range(1, shards)
    ]

    chunks = []
    for subs in chunk_subs:
        n, base = len(subs), subs[0]

        def other(i, me):
            core, _, _ = place(me)
            return block(1 - core, i // n, base + i % n), 0

        def mine(flip):
            def index(i, me):
                core, f, _ = place(me)
                return block(core, f ^ flip, base + i), 0

            return index

        def half(flip):
            def index(i, me):
                _, f, _ = place(me)
                return (f ^ flip) * n + i, 0

            return index

        straight = lambda i, me: (i, 0)
        (sent,) = call(
            copy_kernel, me, 2 * n, [(stale, window, other)], [((2 * n * size, columns), bf16, window, straight)]
        )
        received = swap(sent, beside)
        code, keep = call(
            pair_kernel,
            me,
            n,
            [
                (stale, window, mine(1)),
                (stale, window, mine(0)),
                (received, window, half(1)),
                (received, window, half(0)),
            ],
            [((n * size, columns), bf16, window, straight), ((n * size, columns), f32, window, straight)],
        )
        for held, total, flips in ((2, 4, first), (4, 8, last)):
            got = swap(code, flips)
            keep, code = call(
                functools.partial(add_kernel, held, total),
                me,
                n,
                [(keep, window, straight), (got, window, straight)],
                [((n * size, columns), f32, window, straight), ((n * size, columns), bf16, window, straight)],
            )
        near = swap(code, first)
        across = swap(code, beside)
        far = swap(near, beside)
        chunks.append((subs, keep, near, across, far))

    key_rows = tokens.shape[0] // shards
    partial = call(
        functools.partial(keys_kernel, shards),
        me,
        workers,
        [
            (tokens, (tokens.shape[0], size), lambda i, me: (0, i)),
            (weights, window, lambda i, me: (i, 0)),
        ],
        [((key_rows, columns), f32, (key_rows, columns), lambda i, me: (0, 0))] * shards,
        scratch=[pltpu.VMEM((tokens.shape[0], columns), f32)],
        flops=2 * tokens.shape[0] * rows * columns,
    )
    key_out = partial[0]
    for d in range(1, shards):
        key_out = key_out + lax.ppermute(partial[d], "fsdp", [(i, i ^ d) for i in range(shards)])
    key_out = key_out.astype(bf16)

    outs = None
    calls = 4
    per = workers // calls
    for at in range(calls):
        across_rows = lambda i, me, at=at: (at * per + i, 0)
        across_columns = lambda i, me, at=at: (0, at * per + i)
        ins = [
            (tokens, (tokens.shape[0], size), across_columns),
            (weights, window, across_rows),
            (anchor, window, across_rows),
            (momentum, window, across_rows),
            (stale, window, across_rows),
        ] + [(g, g.shape, lambda i, me: (0, 0)) for g in grads]
        aliases = {}
        if outs is not None:
            aliases = {1 + len(ins) + k: k for k in range(3)}
            ins += [(o, None, None) for o in outs]
        outs = call(
            functools.partial(fresh_kernel, shards, workers, outs is not None),
            me,
            per,
            ins,
            [
                ((rows, columns), bf16, window, across_rows),
                ((rows, columns), f32, window, across_rows),
                ((tokens.shape[0], rows), bf16, (tokens.shape[0], size), across_columns),
            ],
            scratch=[pltpu.VMEM((tokens.shape[0], columns), bf16)],
            aliases=aliases,
            flops=4 * tokens.shape[0] * rows * columns // calls,
        )
    fresh_out, base, grad_input = outs

    updated = None
    for at, (subs, keep, near, across, far) in enumerate(chunks):
        groups = [(("own", keep), ("across", across), ("near", near), ("far", far))]
        if at == len(chunks) - 1:
            groups = [(("own", keep), ("across", across)), (("near", near), ("far", far))]
        for group in groups:
            kinds = [k for k, _ in group]
            n = len(subs)

            def rows_of(i, me, kinds=kinds, n=n, subs=subs):
                core, f, l = place(me)
                spots = {"own": (core, f), "near": (core, 1 - f), "across": (1 - core, l), "far": (1 - core, 1 - l)}
                region, half = spots[kinds[0]]
                for k, kind in enumerate(kinds[1:], 1):
                    region = jnp.where(i // n == k, spots[kind][0], region)
                    half = jnp.where(i // n == k, spots[kind][1], half)
                return block(region, half, subs[0] + i % n), 0

            ins = [(base, window, rows_of)] + [
                (p, window, lambda i, me, k=k, n=n: (jnp.clip(i - k * n, 0, n - 1), 0))
                for k, (_, p) in enumerate(group)
            ]
            aliases = {}
            if updated is not None:
                aliases = {1 + len(ins): 0}
                ins.append((updated, None, None))
            (updated,) = call(
                functools.partial(final_kernel, n, workers, kinds, updated is not None),
                me,
                n * len(kinds),
                ins,
                [((rows, columns), bf16, window, rows_of)],
                aliases=aliases,
            )

    totals = jnp.concatenate([c[1] for c in chunks], 0).reshape(2, size, columns)
    _, _, l = place(worker)
    average = jnp.where(l == 0, totals[0], totals[1]) / workers
    new_moment = outer_momentum * lax.dynamic_slice_in_dim(momentum, worker * size, size, 0) + average
    return key_out, grad_input, updated[None], new_moment, fresh_out[None]


def plain(tokens, inner_weight, key_grad, anchor, momentum, stale_delta):
    weights = inner_weight[0]
    key_out = lax.psum_scatter(
        jnp.dot(tokens, weights, preferred_element_type=jnp.float32), "fsdp", scatter_dimension=0, tiled=True
    ).astype(jnp.bfloat16)
    portion = lax.all_gather(key_grad, "fsdp", axis=0, tiled=True)
    grad_weight = lax.dot_general(tokens, portion, (((0,), (0,)), ((), ())), preferred_element_type=jnp.float32)
    grad_input = lax.dot_general(portion, weights, (((1,), (1,)), ((), ())), preferred_element_type=jnp.float32)
    fresh_term = anchor - (weights.astype(jnp.float32) - inner_rate * grad_weight)
    stale_value = stale_delta[0].astype(jnp.float32)
    workers = lax.axis_size("worker")
    average = lax.psum(stale_value, "worker") / workers
    moment_full = outer_momentum * momentum + average
    common_term = average + outer_momentum * moment_full
    share_rows = anchor.shape[0] // workers
    new_moment = lax.dynamic_slice_in_dim(moment_full, lax.axis_index("worker") * share_rows, share_rows, 0)
    updated = anchor - outer_rate * (common_term + (fresh_term - stale_value) / workers)
    return (
        key_out,
        grad_input.astype(jnp.bfloat16),
        updated[None].astype(jnp.bfloat16),
        new_moment,
        fresh_term[None].astype(jnp.bfloat16),
    )


def local(*args):
    tokens, inner_weight = args[:2]
    workers, shards = lax.axis_size("worker"), lax.axis_size("fsdp")
    size = inner_weight.shape[1] // workers
    fits = workers == 2**3 and shards & (shards - 1) == 0
    fits = fits and size % 128 == 0 and tokens.shape[0] // shards % 16 == 0
    return (fast if fits else plain)(*args)


def solution(mesh):
    in_specs = (
        P("worker", "fsdp"),
        P("worker", "fsdp", None),
        P(("worker", "fsdp"), None),
        P("fsdp", None),
        P("fsdp", None),
        P("worker", "fsdp", None),
    )
    out_specs = (
        P(("worker", "fsdp"), None),
        P("worker", "fsdp"),
        P("worker", "fsdp", None),
        P(("fsdp", "worker"), None),
        P("worker", "fsdp", None),
    )
    return jax.shard_map(local, mesh=mesh, in_specs=in_specs, out_specs=out_specs, check_vma=False)
```

time: 116 us -> 64.9 us (0.56)
  waiting for transfers between devices: 61.8 us -> 5.7 us
  Pallas kernels: 0 us -> 29.5 us
  blocking collectives: 17.7 us -> 0 us
  starting transfers between devices: 0.08 us -> 17.5 us
  between operations: 15.5 us -> 0.76 us
  matrix products: 14.2 us -> 0 us
  local copies, waits for them, and re-layouts: 2.01 us -> 8.38 us
  other arithmetic: 4.11 us -> 2.74 us
    psum x1 -> x0, waiting for transfers between devices: 60.3 us -> none  [local(): summed = lax.psum(stale_value, 'worker')]
    pallas_call x0 -> x16, Pallas kernels: none -> 29.5 us  [call(): pl.pallas_call(kernel, grid_spec=pltpu.PrefetchScalarGridSpec(num_scalar_...]
    all_gather x1 -> x0, blocking collectives: 17.7 us -> none  [local(): portion = lax.all_gather(key_grad, 'fsdp', axis=0, tiled=True)]
    ppermute x0 -> x18, starting transfers between devices: none -> 17.5 us  [the longest x12 8.7 us: swap(): lax.ppermute(value, 'worker', [(i, i ^ flips[i % 2]) for i in range(worke...]
    dot_general x3 -> x0, matrix products: 14.2 us -> none  [the longest x1 7.76 us: local(): lax.dot_general(inputs, portion, (((0,), (0,)), ((), ())), preferred_elem...]
    unnamed x6 -> x24, local copies, waits for them, and re-layouts: 1.18 us -> 8.38 us
    ppermute x0 -> x18, waiting for transfers between devices: none -> 5.7 us  [the longest x12 5.69 us: swap(): lax.ppermute(value, 'worker', [(i, i ^ flips[i % 2]) for i in range(worke...]
    convert_element_type x2 -> x1, other arithmetic: 4.11 us -> 1.7 us  [fast(): key_out = key_out.astype(bf16)]
  transfers between devices with their start and end apart: 2 -> 18, of which waited for: 2 -> 3; matrix products, arithmetic and copies ran while one was open for 6% -> 4% of each run, Pallas kernels for 0% -> 42%
where the time goes in v1:
time: 64.9 us; the launch traced here: 64.5 us
  Pallas kernels  29.5 us (45%)
  starting transfers between devices  17.5 us (27%)
  local copies, waits for them, and re-layouts  8.38 us (13%)
  waiting for transfers between devices  5.7 us (9%)
  other arithmetic  2.74 us (4%)
  between operations  0.76 us (1%)
    pallas_call x16, Pallas kernels, call(): pl.pallas_call(kernel, grid_spec=pltpu.PrefetchScalarGridSpec(num_scalar_...  29.5 us
    ppermute x12, starting transfers between devices, swap(): lax.ppermute(value, 'worker', [(i, i ^ flips[i % 2]) for i in range(worke...  8.7 us
    unnamed x24, local copies, waits for them, and re-layouts  8.38 us
    ppermute x12, waiting for transfers between devices, swap(): lax.ppermute(value, 'worker', [(i, i ^ flips[i % 2]) for i in range(worke...  5.69 us
    ppermute x3, starting transfers between devices, fast(): lax.ppermute(partial[d], 'fsdp', [(i, i ^ d) for i in range(shards)])  4.39 us
    ppermute x3, starting transfers between devices, fast(): lax.ppermute(key_grad, 'fsdp', [(i, i ^ d) for i in range(shards)])  4.39 us
    convert_element_type x1, other arithmetic, fast(): key_out = key_out.astype(bf16)  1.7 us
  transfers between devices with their start and end apart: 18, of which 3 were waited for; matrix products, arithmetic and copies ran while one was open for 4% of the time, Pallas kernels for 42%

profile of v1, /device:TPU:0, one launch (start us, length us, event | category | flops | bytes accessed | tf_op | source)
XLA Modules:
  0.0 64.5 jit_solution(2172031884593796929)
XLA Ops:
  0.7 1.6 %copy-done = bf16[1,2048,512]{2,1,0:T(8,128)(2,1)S(1)} copy-done((bf16[1,2048,512]{2,1,0:T(8,128)(2,1)S(1)}, bf16[1,2048,512]{2,1,0:T(8,128)(2,1)}, u32[]{:S(2)}) %copy-start) | copy-done | bytes 2097176
  2.3 0.6 shard_map.110
  4.2 0.8 %collective-permute-done.12.send_other.keep_other = bf16[512,512]{1,0:T(8,128)(2,1)S(1)} collective-permute-done((bf16[512,512]{1,0:T(8,128)(2,1)S(1)}, bf16[512,512]{1,0:T(8,128)(2,1)S(1)}, u32[]{:S(2)}, u32[]{:S(2)}) %collective-permute-start.12) | collective-permute-done | bytes 524320 | tf_op jit(solution)/shard_map/ppermute | solution.py:156
  5.0 0.9 %shard_map.111 = (bf16[256,512]{1,0:T(8,128)(2,1)S(1)}, f32[256,512]{1,0:T(8,128)S(1)}) custom-call(s32[2]{0:T(128)S(1)} %pad_add_fusion.me_ref, bf16[2048,512]{1,0:T(8,128)(2,1)S(1)} %bitcast.8, bf16[2048,512]{1,0:T(8,128)(2,1)S(1)} %bitcast.9, bf16[512,512]{1,0:T(8,128)(2,1)S(1)} %collective-permute-done.12.send_other.keep_other, ...), custom_call_target="tpu_custom_call" | custom-call | bytes 3145728 | tf_op jit(solution)/shard_map/pallas_call | solution.py:50
  5.9 2.9 %collective-permute-start.13 = (bf16[256,512]{1,0:T(8,128)(2,1)S(1)}, bf16[256,512]{1,0:T(8,128)(2,1)S(1)}, u32[]{:S(2)}, u32[]{:S(2)}) collective-permute-start(bf16[256,512]{1,0:T(8,128)(2,1)S(1)} %get-tuple-element.55), channel_id=1, source_target_pairs={{0,8},{4,20},{8,0},{12,28},{16,24},{20,4},{24,16},{28,12},{1,9},{5... | collective-permute-start | bytes 786440 | tf_op jit(solution)/shard_map/ppermute | solution.py:156
  8.8 0.9 %shard_map.107 = (bf16[256,512]{1,0:T(8,128)(2,1)S(1)}, f32[256,512]{1,0:T(8,128)S(1)}) custom-call(s32[2]{0:T(128)S(1)} %pad_add_fusion.me_ref, bf16[2048,512]{1,0:T(8,128)(2,1)S(1)} %bitcast.10, bf16[2048,512]{1,0:T(8,128)(2,1)S(1)} %bitcast.11, bf16[512,512]{1,0:T(8,128)(2,1)S(1)} %collective-permute-done.6.send_other.keep_other, ...), custom_call_target="tpu_custom_call" | custom-call | bytes 3145728 | tf_op jit(solution)/shard_map/pallas_call | solution.py:50
  9.8 3.4 %collective-permute-done.13.received = bf16[256,512]{1,0:T(8,128)(2,1)S(1)} collective-permute-done((bf16[256,512]{1,0:T(8,128)(2,1)S(1)}, bf16[256,512]{1,0:T(8,128)(2,1)S(1)}, u32[]{:S(2)}, u32[]{:S(2)}) %collective-permute-start.13) | collective-permute-done | bytes 262176 | tf_op jit(solution)/shard_map/ppermute | solution.py:156
  13.2 1.7 %shard_map.112 = (f32[256,512]{1,0:T(8,128)S(1)}, bf16[256,512]{1,0:T(8,128)(2,1)}) custom-call(s32[2]{0:T(128)S(1)} %pad_add_fusion.me_ref, f32[256,512]{1,0:T(8,128)S(1)} %get-tuple-element.54.value, bf16[256,512]{1,0:T(8,128)(2,1)S(1)} %collective-permute-done.13.received), custom_call_target="tpu_custom_call" | custom-call | bytes 2097152 | tf_op jit(solution)/shard_map/pallas_call | solution.py:50
  14.8 0.8 %copy-done.8 = f32[256,512]{1,0:T(8,128)} copy-done((f32[256,512]{1,0:T(8,128)}, f32[256,512]{1,0:T(8,128)S(1)}, u32[]{:S(2)}) %copy-start.8) | copy-done | bytes 524312
  15.6 2.0 %collective-permute-start.14 = (bf16[256,512]{1,0:T(8,128)(2,1)}, bf16[256,512]{1,0:T(8,128)(2,1)}, u32[]{:S(2)}, u32[]{:S(2)}) collective-permute-start(bf16[256,512]{1,0:T(8,128)(2,1)} %get-tuple-element.57), channel_id=1, source_target_pairs={{0,16},{4,12},{8,24},{12,4},{16,0},{20,28},{24,8},{28,20},{1,17},{... | collective-permute-start | bytes 786440 | tf_op jit(solution)/shard_map/ppermute | solution.py:156
  17.7 1.7 %shard_map.108 = (f32[256,512]{1,0:T(8,128)S(1)}, bf16[256,512]{1,0:T(8,128)(2,1)}) custom-call(s32[2]{0:T(128)S(1)} %pad_add_fusion.me_ref, f32[256,512]{1,0:T(8,128)S(1)} %get-tuple-element.48.value, bf16[256,512]{1,0:T(8,128)(2,1)S(1)} %collective-permute-done.7.received), custom_call_target="tpu_custom_call" | custom-call | bytes 2097152 | tf_op jit(solution)/shard_map/pallas_call | solution.py:50
  19.7 1.8 %collective-permute-start.3 = (bf16[64,512]{1,0:T(8,128)(2,1)S(1)}, bf16[64,512]{1,0:T(8,128)(2,1)S(1)}, u32[]{:S(2)}, u32[]{:S(2)}) collective-permute-start(bf16[64,512]{1,0:T(8,128)(2,1)S(1)} %copy-done.7), channel_id=1, source_target_pairs={{0,1},{1,0},{2,3},{3,2},{4,5},{5,4},{6,7},{7,6},{8,9},{9,8},{10,11... | collective-permute-start | bytes 196616 | tf_op jit(solution)/shard_map/ppermute | solution.py:161
  21.5 2.6 %collective-permute-start.4 = (bf16[64,512]{1,0:T(8,128)(2,1)S(1)}, bf16[64,512]{1,0:T(8,128)(2,1)S(1)}, u32[]{:S(2)}, u32[]{:S(2)}) collective-permute-start(bf16[64,512]{1,0:T(8,128)(2,1)S(1)} %copy-done.7), channel_id=1, source_target_pairs={{0,2},{1,3},{2,0},{3,1},{4,6},{5,7},{6,4},{7,5},{8,10},{9,11},{10,... | collective-permute-start | bytes 196616 | tf_op jit(solution)/shard_map/ppermute | solution.py:161
  24.1 3.9 %shard_map.101 = (f32[64,512]{1,0:T(8,128)S(1)}, f32[64,512]{1,0:T(8,128)}, f32[64,512]{1,0:T(8,128)}, f32[64,512]{1,0:T(8,128)}) custom-call(s32[2]{0:T(128)S(1)} %pad_add_fusion.me_ref, bf16[256,2048]{1,0:T(8,128)(2,1)S(1)} %copy-done.6, bf16[2048,512]{1,0:T(8,128)(2,1)S(1)} %bitcast.16), custom_call_target="tpu_custom_call" | custom-call | flops 536870912 | bytes 10485760 | tf_op jit(solution)/shard_map/pallas_call | solution.py:50
  28.0 0.9 %collective-permute-start = (f32[64,512]{1,0:T(8,128)}, f32[64,512]{1,0:T(8,128)}, u32[]{:S(2)}, u32[]{:S(2)}) collective-permute-start(f32[64,512]{1,0:T(8,128)} %get-tuple-element.34), channel_id=1, source_target_pairs={{0,1},{1,0},{2,3},{3,2},{4,5},{5,4},{6,7},{7,6},{8,9},{9,8},{10,11... | collective-permute-start | bytes 393224 | tf_op jit(solution)/shard_map/ppermute | solution.py:232
  28.8 3.5 %collective-permute-start.1 = (f32[64,512]{1,0:T(8,128)}, f32[64,512]{1,0:T(8,128)}, u32[]{:S(2)}, u32[]{:S(2)}) collective-permute-start(f32[64,512]{1,0:T(8,128)} %get-tuple-element.35), channel_id=1, source_target_pairs={{0,2},{1,3},{2,0},{3,1},{4,6},{5,7},{6,4},{7,5},{8,10},{9,11},{10,... | collective-permute-start | bytes 393224 | tf_op jit(solution)/shard_map/ppermute | solution.py:232
  32.4 2.2 %copy-done.2 = f32[2048,512]{1,0:T(8,128)S(1)} copy-done((f32[2048,512]{1,0:T(8,128)S(1)}, f32[2048,512]{1,0:T(8,128)}, u32[]{:S(2)}) %copy-start.2) | copy-done | bytes 4194328
  34.6 2.2 %copy-done.3 = f32[2048,512]{1,0:T(8,128)S(1)} copy-done((f32[2048,512]{1,0:T(8,128)S(1)}, f32[2048,512]{1,0:T(8,128)}, u32[]{:S(2)}) %copy-start.3) | copy-done | bytes 4194328
  36.8 1.6 %copy-done.5 = bf16[1,2048,512]{2,1,0:T(8,128)(2,1)S(1)} copy-done((bf16[1,2048,512]{2,1,0:T(8,128)(2,1)S(1)}, bf16[1,2048,512]{2,1,0:T(8,128)(2,1)}, u32[]{:S(2)}) %copy-start.5) | copy-done | bytes 2097176
  38.4 2.3 %shard_map.102 = (bf16[2048,512]{1,0:T(8,128)(2,1)}, f32[2048,512]{1,0:T(8,128)S(1)}, bf16[256,2048]{1,0:T(8,128)(2,1)}) custom-call(s32[2]{0:T(128)S(1)} %pad_add_fusion.me_ref, bf16[256,2048]{1,0:T(8,128)(2,1)S(1)} %copy-done.6, bf16[2048,512]{1,0:T(8,128)(2,1)S(1)} %bitcast.17, f32[2048,512]{1,0:T(8,128)S(1)} %copy-done.3, f32[2048,512]{1,0:T(8,128)S(1)} %copy-done.2, ...), custom_call_target="tpu_custom_call" | custom-call | flops 268435456 | bytes 8388608 | tf_op jit(solution)/shard_map/pallas_call | solution.py:50
  40.6 2.3 %shard_map.103 = (bf16[2048,512]{1,0:T(8,128)(2,1)}, f32[2048,512]{1,0:T(8,128)S(1)}, bf16[256,2048]{1,0:T(8,128)(2,1)}) custom-call(s32[2]{0:T(128)S(1)} %pad_add_fusion.me_ref, bf16[256,2048]{1,0:T(8,128)(2,1)S(1)} %copy-done.6, bf16[2048,512]{1,0:T(8,128)(2,1)S(1)} %bitcast.18, ...), custom_call_target="tpu_custom_call", output_to_operand_aliasing={{0}: (10, {}), {1}: (11, {}), {2}: (12, {})} | custom-call | flops 268435456 | bytes 8388608 | tf_op jit(solution)/shard_map/pallas_call | solution.py:50
  42.9 2.3 %shard_map.104 = (bf16[2048,512]{1,0:T(8,128)(2,1)}, f32[2048,512]{1,0:T(8,128)S(1)}, bf16[256,2048]{1,0:T(8,128)(2,1)}) custom-call(s32[2]{0:T(128)S(1)} %pad_add_fusion.me_ref, bf16[256,2048]{1,0:T(8,128)(2,1)S(1)} %copy-done.6, bf16[2048,512]{1,0:T(8,128)(2,1)S(1)} %bitcast.19, ...), custom_call_target="tpu_custom_call", output_to_operand_aliasing={{0}: (10, {}), {1}: (11, {}), {2}: (12, {})} | custom-call | flops 268435456 | bytes 8388608 | tf_op jit(solution)/shard_map/pallas_call | solution.py:50
  45.1 1.9 %shard_map.113 = (f32[256,512]{1,0:T(8,128)S(1)}, bf16[256,512]{1,0:T(8,128)(2,1)S(1)}) custom-call(s32[2]{0:T(128)S(1)} %pad_add_fusion.me_ref, f32[256,512]{1,0:T(8,128)S(1)} %copy-done.9, bf16[256,512]{1,0:T(8,128)(2,1)} %collective-permute-done.14.received), custom_call_target="tpu_custom_call" | custom-call | bytes 2097152 | tf_op jit(solution)/shard_map/pallas_call | solution.py:50
  47.1 1.7 %collective-permute-start.16 = (bf16[256,512]{1,0:T(8,128)(2,1)S(1)}, bf16[256,512]{1,0:T(8,128)(2,1)S(1)}, u32[]{:S(2)}, u32[]{:S(2)}) collective-permute-start(bf16[256,512]{1,0:T(8,128)(2,1)S(1)} %get-tuple-element.59), channel_id=1, source_target_pairs={{0,8},{4,20},{8,0},{12,28},{16,24},{20,4},{24,16},{28,12},{1,9},{5... | collective-permute-start | bytes 786440 | tf_op jit(solution)/shard_map/ppermute | solution.py:156
  48.8 1.9 %shard_map.109 = (f32[256,512]{1,0:T(8,128)S(1)}, bf16[256,512]{1,0:T(8,128)(2,1)S(1)}) custom-call(s32[2]{0:T(128)S(1)} %pad_add_fusion.me_ref, f32[256,512]{1,0:T(8,128)S(1)} %copy-done.11, bf16[256,512]{1,0:T(8,128)(2,1)} %collective-permute-done.8.received), custom_call_target="tpu_custom_call" | custom-call | bytes 2097152 | tf_op jit(solution)/shard_map/pallas_call | solution.py:50
  51.2 2.3 %shard_map.105 = (bf16[2048,512]{1,0:T(8,128)(2,1)}, f32[2048,512]{1,0:T(8,128)S(1)}, bf16[256,2048]{1,0:T(8,128)(2,1)}) custom-call(s32[2]{0:T(128)S(1)} %pad_add_fusion.me_ref, bf16[256,2048]{1,0:T(8,128)(2,1)S(1)} %copy-done.6, bf16[2048,512]{1,0:T(8,128)(2,1)S(1)} %bitcast.20, ...), custom_call_target="tpu_custom_call", output_to_operand_aliasing={{0}: (10, {}), {1}: (11, {}), {2}: (12, {})} | custom-call | flops 268435456 | bytes 8388608 | tf_op jit(solution)/shard_map/pallas_call | solution.py:50
  53.4 1.7 %add_convert_fusion = bf16[64,512]{1,0:T(8,128)(2,1)} fusion(f32[64,512]{1,0:T(8,128)} %collective-permute-done.2, f32[64,512]{1,0:T(8,128)} %collective-permute-done.1, f32[64,512]{1,0:T(8,128)S(1)} %get-tuple-element.33, f32[64,512]{1,0:T(8,128)} %collective-permute-done), kind=kLoop, calls=%fused_computation.1 | loop fusion | flops 131072 | bytes 589824 | tf_op jit(solution)/shard_map/convert_element_type | solution.py:233
  55.7 1.5 %collective-permute-done.9.rest_0_ = bf16[256,512]{1,0:T(8,128)(2,1)S(1)} collective-permute-done((bf16[256,512]{1,0:T(8,128)(2,1)S(1)}, bf16[256,512]{1,0:T(8,128)(2,1)S(1)}, u32[]{:S(2)}, u32[]{:S(2)}) %collective-permute-start.9) | collective-permute-done | bytes 262176 | tf_op jit(solution)/shard_map/ppermute | solution.py:156
  57.2 1.0 %multiply_add_fusion = f32[256,512]{1,0:T(8,128)} fusion(f32[256,512]{1,0:T(8,128)S(1)} %get-tuple-element.58.rest_0_, f32[256,512]{1,0:T(8,128)S(1)} %get-tuple-element.53.rest_0_, f32[2048,512]{1,0:T(8,128)S(1)} %copy-done.2, s32[]{:T(128)S(6)} %select_n.32, pred[]{:T(512)S(6)} %eq.10), kind=kLoop, calls=%fused_computation | loop fusion | flops 524288 | bytes 2097157 | tf_op jit(solution)/shard_map/add | solution.py:306
  58.2 2.7 %shard_map.114.rest_2_ = bf16[2048,512]{1,0:T(8,128)(2,1)} custom-call(s32[2]{0:T(128)S(1)} %pad_add_fusion.me_ref, f32[2048,512]{1,0:T(8,128)S(1)} %get-tuple-element.47.base, f32[256,512]{1,0:T(8,128)S(1)} %get-tuple-element.58.rest_0_, bf16[256,512]{1,0:T(8,128)(2,1)S(1)} %collective-permute-done.15.rest_1_, ...), custom_call_target="tpu_custom_call" | custom-call | bytes 12582912 | tf_op jit(solution)/shard_map/pallas_call | solution.py:50
  60.9 1.7 %shard_map.115.rest_2_ = bf16[2048,512]{1,0:T(8,128)(2,1)} custom-call(s32[2]{0:T(128)S(1)} %pad_add_fusion.me_ref, f32[2048,512]{1,0:T(8,128)S(1)} %get-tuple-element.47.base, f32[256,512]{1,0:T(8,128)S(1)} %get-tuple-element.53.rest_0_, bf16[256,512]{1,0:T(8,128)(2,1)S(1)} %collective-permute-done.11.rest_1_, ...), custom_call_target="tpu_custom_call", output_to_operand_aliasing={{}: (4, {})} | custom-call | bytes 4194304 | tf_op jit(solution)/shard_map/pallas_call | solution.py:50
  62.6 1.9 %shard_map.116 = bf16[2048,512]{1,0:T(8,128)(2,1)} custom-call(s32[2]{0:T(128)S(1)} %pad_add_fusion.me_ref, f32[2048,512]{1,0:T(8,128)S(1)} %get-tuple-element.47.base, bf16[256,512]{1,0:T(8,128)(2,1)S(1)} %collective-permute-done.9.rest_0_, bf16[256,512]{1,0:T(8,128)(2,1)S(1)} %collective-permute-done.10.rest_1_, ...), custom_call_target="tpu_custom_call", output_to_operand_aliasing={{}: (4, {})} | custom-call | bytes 4194304 | tf_op jit(solution)/shard_map/pallas_call | solution.py:50
  (47 shorter events, 2.9 us)
Async XLA Ops:
  0.7 1.6 %copy-start = (bf16[1,2048,512]{2,1,0:T(8,128)(2,1)S(1)}, bf16[1,2048,512]{2,1,0:T(8,128)(2,1)}, u32[]{:S(2)}) copy-start(bf16[1,2048,512]{2,1,0:T(8,128)(2,1)} %param.11) | copy-start | bytes 6291460
  2.9 2.1 %collective-permute-start.12 = (bf16[512,512]{1,0:T(8,128)(2,1)S(1)}, bf16[512,512]{1,0:T(8,128)(2,1)S(1)}, u32[]{:S(2)}, u32[]{:S(2)}) collective-permute-start(bf16[512,512]{1,0:T(8,128)(2,1)S(1)} %shard_map.110), channel_id=1, source_target_pairs={{0,4},{4,0},{8,12},{12,8},{16,20},{20,16},{24,28},{28,24},{1,5},{5... | collective-permute-start | bytes 1572872 | tf_op jit(solution)/shard_map/ppermute | solution.py:156
  4.1 4.7 %collective-permute-start.6 = (bf16[512,512]{1,0:T(8,128)(2,1)S(1)}, bf16[512,512]{1,0:T(8,128)(2,1)S(1)}, u32[]{:S(2)}, u32[]{:S(2)}) collective-permute-start(bf16[512,512]{1,0:T(8,128)(2,1)S(1)} %shard_map.106), channel_id=1, source_target_pairs={{0,4},{4,0},{8,12},{12,8},{16,20},{20,16},{24,28},{28,24},{1,5},{5... | collective-permute-start | bytes 1572872 | tf_op jit(solution)/shard_map/ppermute | solution.py:156
  5.9 13.8 %copy-start.7 = (bf16[64,512]{1,0:T(8,128)(2,1)S(1)}, bf16[64,512]{1,0:T(8,128)(2,1)}, u32[]{:S(2)}) copy-start(bf16[64,512]{1,0:T(8,128)(2,1)} %rest_0_.7) | copy-start | bytes 196612
  5.9 7.3 %collective-permute-start.13 = (bf16[256,512]{1,0:T(8,128)(2,1)S(1)}, bf16[256,512]{1,0:T(8,128)(2,1)S(1)}, u32[]{:S(2)}, u32[]{:S(2)}) collective-permute-start(bf16[256,512]{1,0:T(8,128)(2,1)S(1)} %get-tuple-element.55), channel_id=1, source_target_pairs={{0,8},{4,20},{8,0},{12,28},{16,24},{20,4},{24,16},{28,12},{1,9},{5... | collective-permute-start | bytes 786440 | tf_op jit(solution)/shard_map/ppermute | solution.py:156
  8.8 15.3 %copy-start.4 = (bf16[1,2048,512]{2,1,0:T(8,128)(2,1)S(1)}, bf16[1,2048,512]{2,1,0:T(8,128)(2,1)}, u32[]{:S(2)}) copy-start(bf16[1,2048,512]{2,1,0:T(8,128)(2,1)} %param.7) | copy-start | bytes 6291460
  9.7 14.4 %copy-start.6 = (bf16[256,2048]{1,0:T(8,128)(2,1)S(1)}, bf16[256,2048]{1,0:T(8,128)(2,1)}, u32[]{:S(2)}) copy-start(bf16[256,2048]{1,0:T(8,128)(2,1)} %tokens.9) | copy-start | bytes 3145732
  9.7 8.0 %collective-permute-start.7 = (bf16[256,512]{1,0:T(8,128)(2,1)S(1)}, bf16[256,512]{1,0:T(8,128)(2,1)S(1)}, u32[]{:S(2)}, u32[]{:S(2)}) collective-permute-start(bf16[256,512]{1,0:T(8,128)(2,1)S(1)} %get-tuple-element.49), channel_id=1, source_target_pairs={{0,8},{4,20},{8,0},{12,28},{16,24},{20,4},{24,16},{28,12},{1,9},{5... | collective-permute-start | bytes 786440 | tf_op jit(solution)/shard_map/ppermute | solution.py:156
  14.8 0.8 %copy-start.8 = (f32[256,512]{1,0:T(8,128)}, f32[256,512]{1,0:T(8,128)S(1)}, u32[]{:S(2)}) copy-start(f32[256,512]{1,0:T(8,128)S(1)} %get-tuple-element.56.value) | copy-start | bytes 1572868
  15.6 16.7 %copy-start.1 = (bf16[1,2048,512]{2,1,0:T(8,128)(2,1)S(1)}, bf16[1,2048,512]{2,1,0:T(8,128)(2,1)}, u32[]{:S(2)}) copy-start(bf16[1,2048,512]{2,1,0:T(8,128)(2,1)} %param.11) | copy-start | bytes 6291460
  15.6 29.5 %collective-permute-start.14 = (bf16[256,512]{1,0:T(8,128)(2,1)}, bf16[256,512]{1,0:T(8,128)(2,1)}, u32[]{:S(2)}, u32[]{:S(2)}) collective-permute-start(bf16[256,512]{1,0:T(8,128)(2,1)} %get-tuple-element.57), channel_id=1, source_target_pairs={{0,16},{4,12},{8,24},{12,4},{16,0},{20,28},{24,8},{28,20},{1,17},{... | collective-permute-start | bytes 786440 | tf_op jit(solution)/shard_map/ppermute | solution.py:156
  19.4 12.9 %copy-start.10 = (f32[256,512]{1,0:T(8,128)}, f32[256,512]{1,0:T(8,128)S(1)}, u32[]{:S(2)}) copy-start(f32[256,512]{1,0:T(8,128)S(1)} %get-tuple-element.50.value) | copy-start | bytes 1572868
  19.4 29.4 %collective-permute-start.8 = (bf16[256,512]{1,0:T(8,128)(2,1)}, bf16[256,512]{1,0:T(8,128)(2,1)}, u32[]{:S(2)}, u32[]{:S(2)}) collective-permute-start(bf16[256,512]{1,0:T(8,128)(2,1)} %get-tuple-element.51), channel_id=1, source_target_pairs={{0,16},{4,12},{8,24},{12,4},{16,0},{20,28},{24,8},{28,20},{1,17},{... | collective-permute-start | bytes 786440 | tf_op jit(solution)/shard_map/ppermute | solution.py:156
  19.7 8.3 %collective-permute-start.3 = (bf16[64,512]{1,0:T(8,128)(2,1)S(1)}, bf16[64,512]{1,0:T(8,128)(2,1)S(1)}, u32[]{:S(2)}, u32[]{:S(2)}) collective-permute-start(bf16[64,512]{1,0:T(8,128)(2,1)S(1)} %copy-done.7), channel_id=1, source_target_pairs={{0,1},{1,0},{2,3},{3,2},{4,5},{5,4},{6,7},{7,6},{8,9},{9,8},{10,11... | collective-permute-start | bytes 196616 | tf_op jit(solution)/shard_map/ppermute | solution.py:161
  21.5 7.4 %collective-permute-start.4 = (bf16[64,512]{1,0:T(8,128)(2,1)S(1)}, bf16[64,512]{1,0:T(8,128)(2,1)S(1)}, u32[]{:S(2)}, u32[]{:S(2)}) collective-permute-start(bf16[64,512]{1,0:T(8,128)(2,1)S(1)} %copy-done.7), channel_id=1, source_target_pairs={{0,2},{1,3},{2,0},{3,1},{4,6},{5,7},{6,4},{7,5},{8,10},{9,11},{10,... | collective-permute-start | bytes 196616 | tf_op jit(solution)/shard_map/ppermute | solution.py:161
  24.1 8.3 %collective-permute-start.5 = (bf16[64,512]{1,0:T(8,128)(2,1)S(1)}, bf16[64,512]{1,0:T(8,128)(2,1)S(1)}, u32[]{:S(2)}, u32[]{:S(2)}) collective-permute-start(bf16[64,512]{1,0:T(8,128)(2,1)S(1)} %copy-done.7), channel_id=1, source_target_pairs={{0,3},{1,2},{2,1},{3,0},{4,7},{5,6},{6,5},{7,4},{8,11},{9,10},{10,... | collective-permute-start | bytes 196616 | tf_op jit(solution)/shard_map/ppermute | solution.py:161
  28.0 25.5 %collective-permute-start = (f32[64,512]{1,0:T(8,128)}, f32[64,512]{1,0:T(8,128)}, u32[]{:S(2)}, u32[]{:S(2)}) collective-permute-start(f32[64,512]{1,0:T(8,128)} %get-tuple-element.34), channel_id=1, source_target_pairs={{0,1},{1,0},{2,3},{3,2},{4,5},{5,4},{6,7},{7,6},{8,9},{9,8},{10,11... | collective-permute-start | bytes 393224 | tf_op jit(solution)/shard_map/ppermute | solution.py:232
  28.8 24.6 %collective-permute-start.1 = (f32[64,512]{1,0:T(8,128)}, f32[64,512]{1,0:T(8,128)}, u32[]{:S(2)}, u32[]{:S(2)}) collective-permute-start(f32[64,512]{1,0:T(8,128)} %get-tuple-element.35), channel_id=1, source_target_pairs={{0,2},{1,3},{2,0},{3,1},{4,6},{5,7},{6,4},{7,5},{8,10},{9,11},{10,... | collective-permute-start | bytes 393224 | tf_op jit(solution)/shard_map/ppermute | solution.py:232
  32.3 21.1 %collective-permute-start.2 = (f32[64,512]{1,0:T(8,128)}, f32[64,512]{1,0:T(8,128)}, u32[]{:S(2)}, u32[]{:S(2)}) collective-permute-start(f32[64,512]{1,0:T(8,128)} %get-tuple-element.36), channel_id=1, source_target_pairs={{0,3},{1,2},{2,1},{3,0},{4,7},{5,6},{6,5},{7,4},{8,11},{9,10},{10,... | collective-permute-start | bytes 393224 | tf_op jit(solution)/shard_map/ppermute | solution.py:232
  32.4 2.2 %copy-start.2 = (f32[2048,512]{1,0:T(8,128)S(1)}, f32[2048,512]{1,0:T(8,128)}, u32[]{:S(2)}) copy-start(f32[2048,512]{1,0:T(8,128)} %momentum.7) | copy-start | bytes 12582916
  34.6 2.2 %copy-start.3 = (f32[2048,512]{1,0:T(8,128)S(1)}, f32[2048,512]{1,0:T(8,128)}, u32[]{:S(2)}) copy-start(f32[2048,512]{1,0:T(8,128)} %anchor.7) | copy-start | bytes 12582916
  36.8 1.6 %copy-start.5 = (bf16[1,2048,512]{2,1,0:T(8,128)(2,1)S(1)}, bf16[1,2048,512]{2,1,0:T(8,128)(2,1)}, u32[]{:S(2)}) copy-start(bf16[1,2048,512]{2,1,0:T(8,128)(2,1)} %param.7) | copy-start | bytes 6291460
  42.9 2.3 %copy-start.9 = (f32[256,512]{1,0:T(8,128)S(1)}, f32[256,512]{1,0:T(8,128)}, u32[]{:S(2)}) copy-start(f32[256,512]{1,0:T(8,128)} %copy-done.8) | copy-start | bytes 1572868
  42.9 5.9 %copy-start.11 = (f32[256,512]{1,0:T(8,128)S(1)}, f32[256,512]{1,0:T(8,128)}, u32[]{:S(2)}) copy-start(f32[256,512]{1,0:T(8,128)} %copy-done.10) | copy-start | bytes 1572868
  47.1 8.6 %collective-permute-start.16 = (bf16[256,512]{1,0:T(8,128)(2,1)S(1)}, bf16[256,512]{1,0:T(8,128)(2,1)S(1)}, u32[]{:S(2)}, u32[]{:S(2)}) collective-permute-start(bf16[256,512]{1,0:T(8,128)(2,1)S(1)} %get-tuple-element.59), channel_id=1, source_target_pairs={{0,8},{4,20},{8,0},{12,28},{16,24},{20,4},{24,16},{28,12},{1,9},{5... | collective-permute-start | bytes 786440 | tf_op jit(solution)/shard_map/ppermute | solution.py:156
  50.7 6.4 %collective-permute-start.9 = (bf16[256,512]{1,0:T(8,128)(2,1)S(1)}, bf16[256,512]{1,0:T(8,128)(2,1)S(1)}, u32[]{:S(2)}, u32[]{:S(2)}) collective-permute-start(bf16[256,512]{1,0:T(8,128)(2,1)S(1)} %get-tuple-element.52), channel_id=1, source_target_pairs={{0,8},{4,20},{8,0},{12,28},{16,24},{20,4},{24,16},{28,12},{1,9},{5... | collective-permute-start | bytes 786440 | tf_op jit(solution)/shard_map/ppermute | solution.py:156
  55.1 3.0 %collective-permute-start.15 = (bf16[256,512]{1,0:T(8,128)(2,1)S(1)}, bf16[256,512]{1,0:T(8,128)(2,1)S(1)}, u32[]{:S(2)}, u32[]{:S(2)}) collective-permute-start(bf16[256,512]{1,0:T(8,128)(2,1)S(1)} %get-tuple-element.59), channel_id=1, source_target_pairs={{0,4},{4,0},{8,12},{12,8},{16,20},{20,16},{24,28},{28,24},{1,5},{5... | collective-permute-start | bytes 786440 | tf_op jit(solution)/shard_map/ppermute | solution.py:156
  55.1 5.7 %collective-permute-start.11 = (bf16[256,512]{1,0:T(8,128)(2,1)S(1)}, bf16[256,512]{1,0:T(8,128)(2,1)S(1)}, u32[]{:S(2)}, u32[]{:S(2)}) collective-permute-start(bf16[256,512]{1,0:T(8,128)(2,1)S(1)} %get-tuple-element.52), channel_id=1, source_target_pairs={{0,4},{4,0},{8,12},{12,8},{16,20},{20,16},{24,28},{28,24},{1,5},{5... | collective-permute-start | bytes 786440 | tf_op jit(solution)/shard_map/ppermute | solution.py:156
  55.7 2.5 %collective-permute-start.17 = (bf16[256,512]{1,0:T(8,128)(2,1)S(1)}, bf16[256,512]{1,0:T(8,128)(2,1)S(1)}, u32[]{:S(2)}, u32[]{:S(2)}) collective-permute-start(bf16[256,512]{1,0:T(8,128)(2,1)S(1)} %collective-permute-done.16.rest_2_), channel_id=1, source_target_pairs={{0,4},{4,0},{8,12},{12,8},{16,20},{20,16},{24,28},{28,24},{1,5},{5... | collective-permute-start | bytes 786440 | tf_op jit(solution)/shard_map/ppermute | solution.py:156
  57.2 5.4 %collective-permute-start.10 = (bf16[256,512]{1,0:T(8,128)(2,1)S(1)}, bf16[256,512]{1,0:T(8,128)(2,1)S(1)}, u32[]{:S(2)}, u32[]{:S(2)}) collective-permute-start(bf16[256,512]{1,0:T(8,128)(2,1)S(1)} %collective-permute-done.9.rest_0_), channel_id=1, source_target_pairs={{0,4},{4,0},{8,12},{12,8},{16,20},{20,16},{24,28},{28,24},{1,5},{5... | collective-permute-start | bytes 786440 | tf_op jit(solution)/shard_map/ppermute | solution.py:156

commit v2 on v0

v2 whole, which is shorter than its diff:
```python
import functools
import math

import jax
import jax.numpy as jnp
from jax import lax
from jax.experimental import pallas as pl
from jax.experimental.pallas import tpu as pltpu
from jax.sharding import PartitionSpec as P

inner_rate = 0.0005
outer_rate = 0.7
outer_momentum = 0.9

stale_bound = 0.29882812
floor = 2.0**-14
power = 250.0 / math.log2(1.0 + stale_bound / floor)


def encode(value, count):
    grown = jnp.log(jnp.abs(value) * (1.0 / (floor * count)) + 1.0)
    code = jnp.exp2(grown * (power / math.log(2.0)) - 125.0)
    return jnp.where(value < 0, -code, code).astype(jnp.bfloat16)


def decode(code, count):
    code = code.astype(jnp.float32)
    grown = jnp.exp2(jnp.log(jnp.abs(code)) * (1.0 / (power * math.log(2.0))) + 125.0 / power)
    value = (grown - 1.0) * (floor * count)
    return jnp.where(code < 0, -value, value)


pace = 3.3e9


def place(me):
    core, low, high = me % 2, (me // 2) % 2, me // 4
    return core, jnp.where(core == 0, low, high), jnp.where(core == 0, high, low)


def block(region, half, sub):
    return jnp.where(region == 0, 4 * sub + 2 * half, 4 * half + 2 * sub + 1)


SMEM, VMEM, HBM, ANY = pltpu.SMEM, pltpu.VMEM, pltpu.HBM, pl.ANY


def call(kernel, ins, outs, scratch=(), after=(), aliases=None, micros=1.0, vmem=12):
    late = len(after)

    def body(*refs):
        kernel(*refs[: len(ins)], *refs[len(ins) + late :])

    def placed(array, space):
        return pltpu.with_memory_space_constraint(array, space) if space in (HBM, VMEM) else array

    return pl.pallas_call(
        body,
        in_specs=[pl.BlockSpec(memory_space=s) for _, s in ins] + [pl.BlockSpec(memory_space=ANY)] * late,
        out_specs=[pl.BlockSpec(memory_space=s) for _, _, s in outs],
        out_shape=[s(shape, dtype) for shape, dtype, s in outs],
        scratch_shapes=scratch,
        input_output_aliases=aliases or {},
        cost_estimate=pl.CostEstimate(flops=int(micros * pace), bytes_accessed=0, transcendentals=0),
        compiler_params=pltpu.CompilerParams(vmem_limit_bytes=vmem * 2**20),
    )(*[placed(a, s) for a, s in ins], *after)


def rows(ref, at, size):
    return ref.at[pl.ds(pl.multiple_of(at * size, size), size), :]


def pair_kernel(size, sub, me_ref, stale, other, code, keep):
    core, first, _ = place(me_ref[0])

    def summed(half):
        at = block(core, half, sub)
        return rows(stale, at, size)[...].astype(jnp.float32) + rows(other, at, size)[...].astype(jnp.float32)

    code[...] = encode(summed(1 - first), 2)
    keep[...] = summed(first)


def add_kernel(held, total, value, received, out, code):
    summed = value[...] + decode(received[...], held)
    out[...] = summed
    code[...] = encode(summed, total)


def keys_kernel(me_ref, tokens, weights, sent, own, later, total):
    total[...] = jnp.dot(tokens[...], weights[...], preferred_element_type=jnp.float32)
    size = own.shape[0]
    shard = me_ref[1]
    sent[:size, :] = rows(total, shard ^ 1, size)[...]
    sent[size:, :] = rows(total, shard ^ 3, size)[...]
    own[...] = rows(total, shard, size)[...]
    later[...] = rows(total, shard ^ 2, size)[...]


def keys_add_kernel(received, own, later, own_out, later_out):
    size = own.shape[0]
    own_out[...] = own[...] + received[:size, :]
    later_out[...] = later[...] + received[size:, :]


def spots(me):
    core, first, last = place(me)
    return {
        "own": (core, first),
        "near": (core, 1 - first),
        "across": (1 - core, last),
        "far": (1 - core, 1 - last),
    }


def fresh_kernel(parts, workers, kinds, finish, me_ref, tokens, weights, anchor, momentum, stale, *rest):
    count = len(kinds)
    grads, rest = rest[:parts], rest[parts:]
    if finish:
        sums, partial, rest = rest[:count], rest[count : count + 2], rest[count + 4 :]
        fresh_out, grad_out, param_out, moment_out, key_out = rest[:5]
        param_buf, moment_buf, key_buf, rest = rest[5], rest[6], rest[7], rest[8:]
    else:
        fresh_out, grad_out, bases, rest = rest[0], rest[1], rest[2 : 2 + count], rest[2 + count :]
    portion, fresh_buf, grad_buf, sem = rest
    size = weights.shape[0] // workers
    known = spots(me_ref[0])
    spans = [pl.ds(pl.multiple_of(block(*known[kind], sub) * size, size), size) for kind, sub in kinds]
    departures = []

    def send(source, target):
        copy = pltpu.make_async_copy(source, target, sem.at[len(departures)])
        copy.start()
        departures.append(copy)

    if finish:
        key_buf[...] = (partial[0][...] + partial[1][...]).astype(jnp.bfloat16)
        send(key_buf, key_out)
        _, _, last = place(me_ref[0])
        average = jnp.where(last == 0, sums[0][...], sums[1][...]) / workers
        moment_buf[...] = outer_momentum * rows(momentum, me_ref[0], size)[...] + average
        send(moment_buf, moment_out)
    held = grads[0].shape[0]
    for d in range(parts):
        rows(portion, me_ref[1] ^ d, held)[...] = grads[d][...]
    for k, span in enumerate(spans):
        weight = weights[span, :]
        grad_weight = lax.dot_general(
            tokens[:, span], portion[...], (((0,), (0,)), ((), ())), preferred_element_type=jnp.float32
        )
        grad_buf[k] = lax.dot_general(
            portion[...], weight, (((1,), (1,)), ((), ())), preferred_element_type=jnp.float32
        ).astype(jnp.bfloat16)
        send(grad_buf.at[k], grad_out.at[:, span])
        value = anchor[span, :]
        fresh = value - (weight.astype(jnp.float32) - inner_rate * grad_weight)
        fresh_buf[k] = fresh.astype(jnp.bfloat16)
        send(fresh_buf.at[k], fresh_out.at[span, :])
        base = value - outer_rate * (
            outer_momentum * outer_momentum * momentum[span, :]
            + (fresh - stale[span, :].astype(jnp.float32)) / workers
        )
        if finish:
            param_buf[k] = finished(kinds[k][0], workers, base, sums[k])
            send(param_buf.at[k], param_out.at[span, :])
        else:
            bases[k][...] = base
    for copy in departures:
        copy.wait()


def finished(kind, workers, base, piece):
    total = piece[...]
    if kind != "own":
        total = decode(total, workers)
    return (base - (outer_rate * (1.0 + outer_momentum) / workers) * total).astype(jnp.bfloat16)


def update_kernel(workers, kinds, me_ref, *rest):
    count = len(kinds)
    bases, pieces, (_, out, out_buf, sem) = rest[:count], rest[count : 2 * count], rest[2 * count :]
    size = out.shape[0] // workers
    known = spots(me_ref[0])
    copies = []
    for k, (kind, sub) in enumerate(kinds):
        out_buf[k] = finished(kind, workers, bases[k][...], pieces[k])
        copies.append(pltpu.make_async_copy(out_buf.at[k], rows(out, block(*known[kind], sub), size), sem.at[k]))
        copies[-1].start()
    for copy in copies:
        copy.wait()


def fast(tokens, inner_weight, key_grad, anchor, momentum, stale_delta):
    workers, shards = lax.axis_size("worker"), lax.axis_size("fsdp")
    f32, bf16 = jnp.float32, jnp.bfloat16
    DMA = pltpu.SemaphoreType.DMA
    weights, stale = inner_weight[0], stale_delta[0]
    height, columns = stale.shape
    batch = tokens.shape[0]
    size = height // workers
    me = jnp.stack([lax.axis_index("worker"), lax.axis_index("fsdp")]).astype(jnp.int32)
    window = (size, columns)

    def swap(value, flips):
        return lax.ppermute(value, "worker", [(i, i ^ flips[i % 2]) for i in range(workers)])

    def across_shards(value, distance):
        return lax.ppermute(value, "fsdp", [(i, i ^ distance) for i in range(shards)])

    beside, first, last = (1, 1), (2, 4), (4, 2)
    chunks = range(2)

    key_rows = batch // shards
    other = swap(stale, beside)
    grad_near = across_shards(key_grad, 1)
    block_of_keys = (key_rows, columns)
    sent, own_keys, later_keys = call(
        keys_kernel,
        [(me, SMEM), (tokens, VMEM), (weights, VMEM)],
        [((2 * key_rows, columns), f32, VMEM), (block_of_keys, f32, VMEM), (block_of_keys, f32, VMEM)],
        scratch=[pltpu.VMEM((batch, columns), f32)],
        micros=0.8,
    )

    codes, keeps = [], []
    for c in chunks:
        code, keep = call(
            functools.partial(pair_kernel, size, c),
            [(me, SMEM), (stale, VMEM), (other, VMEM)],
            [(window, bf16, VMEM), (window, f32, VMEM)],
            after=[sent, grad_near] if c == 0 else [keeps[0]],
            micros=0.9,
        )
        codes.append(code)
        keeps.append(keep)
    got = [swap(codes[c], first) for c in chunks]

    key_near = across_shards(sent, 1)
    grads = [key_grad, grad_near, across_shards(key_grad, 2), across_shards(grad_near, 2)]

    def added(held, total, after):
        for c in chunks:
            keeps[c], codes[c] = call(
                functools.partial(add_kernel, held, total),
                [(keeps[c], VMEM), (got[c], VMEM)],
                [(window, f32, VMEM), (window, bf16, VMEM)],
                after=after if c == 0 else [keeps[0], *after],
                micros=0.5,
            )

    def fresh(kinds, after, finish=None):
        n = len(kinds)
        ins = [(me, SMEM), (tokens, VMEM), (weights, VMEM), (anchor, VMEM), (momentum, VMEM), (stale, VMEM)]
        ins += [(g, VMEM) for g in grads]
        outs = [((height, columns), bf16, HBM), ((batch, height), bf16, HBM)]
        scratch = [
            pltpu.VMEM((batch, columns), bf16),
            pltpu.VMEM((n, *window), bf16),
            pltpu.VMEM((n, batch, size), bf16),
            DMA((3 * n + 2,)),
        ]
        aliases = {}
        if finish is None:
            outs += [(window, f32, VMEM)] * n
        else:
            sums, filled = finish
            ins += [(p, VMEM) for p in [*sums, own_keys, key_far]]
            aliases = {len(ins) + k: k for k in range(2)}
            ins += [(o, HBM) for o in filled]
            outs += [((height, columns), bf16, HBM), (window, f32, HBM), ((key_rows, columns), bf16, HBM)]
            scratch = [
                pltpu.VMEM((n, *window), bf16),
                pltpu.VMEM(window, f32),
                pltpu.VMEM((key_rows, columns), bf16),
            ] + scratch
        return call(
            functools.partial(fresh_kernel, shards, workers, kinds, finish is not None),
            ins,
            outs,
            scratch=scratch,
            after=after,
            aliases=aliases,
            micros=3.0,
        )

    added(2, 4, [])
    got = [swap(codes[c], last) for c in chunks]
    late_kinds = [("near", 0), ("far", 0), ("near", 1), ("far", 1)]
    own_keys, later_keys = call(
        keys_add_kernel,
        [(key_near, VMEM), (own_keys, VMEM), (later_keys, VMEM)],
        [(block_of_keys, f32, VMEM), (block_of_keys, f32, VMEM)],
        after=[keeps[1]],
        micros=0.4,
    )
    key_far = across_shards(later_keys, 2)
    fresh_out, grad_input, *bases = fresh(late_kinds, [keeps[1]])
    added(4, 8, [bases[0]])
    near = [swap(codes[c], first) for c in chunks]
    across = [swap(codes[c], beside) for c in chunks]
    far = [swap(near[c], beside) for c in chunks]
    soon_kinds = [("own", 0), ("own", 1), ("across", 0), ("across", 1)]
    fresh_out, grad_input, updated, new_moment, key_out = fresh(
        soon_kinds, [], ([*keeps, *across], [fresh_out, grad_input])
    )

    for which in ((0, 1, 2), (3,)):
        kinds = [late_kinds[w] for w in which]
        pieces = [near[0], far[0], near[1], far[1]]
        ins = [(me, SMEM)] + [(bases[w], VMEM) for w in which] + [(pieces[w], VMEM) for w in which] + [(updated, HBM)]
        (updated,) = call(
            functools.partial(update_kernel, workers, kinds),
            ins,
            [((height, columns), bf16, HBM)],
            scratch=[pltpu.VMEM((len(which), *window), bf16), DMA((len(which),))],
            aliases={len(ins) - 1: 0},
            micros=1.8,
        )
    return key_out, grad_input, updated[None], new_moment, fresh_out[None]


def plain(tokens, inner_weight, key_grad, anchor, momentum, stale_delta):
    weights = inner_weight[0]
    key_out = lax.psum_scatter(
        jnp.dot(tokens, weights, preferred_element_type=jnp.float32), "fsdp", scatter_dimension=0, tiled=True
    ).astype(jnp.bfloat16)
    portion = lax.all_gather(key_grad, "fsdp", axis=0, tiled=True)
    grad_weight = lax.dot_general(tokens, portion, (((0,), (0,)), ((), ())), preferred_element_type=jnp.float32)
    grad_input = lax.dot_general(portion, weights, (((1,), (1,)), ((), ())), preferred_element_type=jnp.float32)
    fresh_term = anchor - (weights.astype(jnp.float32) - inner_rate * grad_weight)
    stale_value = stale_delta[0].astype(jnp.float32)
    workers = lax.axis_size("worker")
    average = lax.psum(stale_value, "worker") / workers
    moment_full = outer_momentum * momentum + average
    common_term = average + outer_momentum * moment_full
    share_rows = anchor.shape[0] // workers
    new_moment = lax.dynamic_slice_in_dim(moment_full, lax.axis_index("worker") * share_rows, share_rows, 0)
    updated = anchor - outer_rate * (common_term + (fresh_term - stale_value) / workers)
    return (
        key_out,
        grad_input.astype(jnp.bfloat16),
        updated[None].astype(jnp.bfloat16),
        new_moment,
        fresh_term[None].astype(jnp.bfloat16),
    )


def local(*args):
    tokens, inner_weight = args[:2]
    workers, shards = lax.axis_size("worker"), lax.axis_size("fsdp")
    size = inner_weight.shape[1] // workers
    fits = workers == 2**3 and shards == 2**2
    fits = fits and size % 128 == 0 and tokens.shape[0] // shards % 16 == 0
    return (fast if fits else plain)(*args)


def solution(mesh):
    in_specs = (
        P("worker", "fsdp"),
        P("worker", "fsdp", None),
        P(("worker", "fsdp"), None),
        P("fsdp", None),
        P("fsdp", None),
        P("worker", "fsdp", None),
    )
    out_specs = (
        P(("worker", "fsdp"), None),
        P("worker", "fsdp"),
        P("worker", "fsdp", None),
        P(("fsdp", "worker"), None),
        P("worker", "fsdp", None),
    )
    return jax.shard_map(local, mesh=mesh, in_specs=in_specs, out_specs=out_specs, check_vma=False)
```

time: 116 us -> 46.6 us (0.40)
  waiting for transfers between devices: 61.8 us -> 10.1 us
  blocking collectives: 17.7 us -> 0 us
  starting transfers between devices: 0.08 us -> 17.7 us
  between operations: 15.5 us -> 0.76 us
  Pallas kernels: 0 us -> 14.6 us
  matrix products: 14.2 us -> 0 us
  other arithmetic: 4.11 us -> 0.07 us
    psum x1 -> x0, waiting for transfers between devices: 60.3 us -> none  [local(): summed = lax.psum(stale_value, 'worker')]
    ppermute x0 -> x16, starting transfers between devices: none -> 17.7 us  [the longest x5 9.21 us: across_shards(): lax.ppermute(value, 'fsdp', [(i, i ^ distance) for i in range(shards)])]
    all_gather x1 -> x0, blocking collectives: 17.7 us -> none  [local(): portion = lax.all_gather(key_grad, 'fsdp', axis=0, tiled=True)]
    pallas_call x0 -> x12, Pallas kernels: none -> 14.6 us  [call(): pl.pallas_call(body, in_specs=[pl.BlockSpec(memory_space=s) for _, s in i...]
    dot_general x3 -> x0, matrix products: 14.2 us -> none  [the longest x1 7.76 us: local(): lax.dot_general(inputs, portion, (((0,), (0,)), ((), ())), preferred_elem...]
    ppermute x0 -> x16, waiting for transfers between devices: none -> 10.1 us  [the longest x5 5.98 us: across_shards(): lax.ppermute(value, 'fsdp', [(i, i ^ distance) for i in range(shards)])]
    convert_element_type x2 -> x0, other arithmetic: 4.11 us -> none  [the longest x1 2.56 us: local(): stale_value = stale_delta[0].astype(jnp.float32)]
    unnamed x6 -> x16, local copies, waits for them, and re-layouts: 1.18 us -> 3.12 us
  transfers between devices with their start and end apart: 2 -> 16, of which waited for: 2 -> 5; matrix products, arithmetic and copies ran while one was open for 6% -> 0% of each run, Pallas kernels for 0% -> 26%
where the time goes in v2:
time: 46.6 us; the launch traced here: 46.4 us
  starting transfers between devices  17.7 us (38%)
  Pallas kernels  14.6 us (31%)
  waiting for transfers between devices  10.1 us (22%)
  local copies, waits for them, and re-layouts  3.12 us (7%)
  between operations  0.76 us (2%)
    pallas_call x12, Pallas kernels, call(): pl.pallas_call(body, in_specs=[pl.BlockSpec(memory_space=s) for _, s in i...  14.6 us
    ppermute x5, starting transfers between devices, across_shards(): lax.ppermute(value, 'fsdp', [(i, i ^ distance) for i in range(shards)])  9.21 us
    ppermute x11, starting transfers between devices, swap(): lax.ppermute(value, 'worker', [(i, i ^ flips[i % 2]) for i in range(worke...  8.52 us
    ppermute x5, waiting for transfers between devices, across_shards(): lax.ppermute(value, 'fsdp', [(i, i ^ distance) for i in range(shards)])  5.98 us
    ppermute x11, waiting for transfers between devices, swap(): lax.ppermute(value, 'worker', [(i, i ^ flips[i % 2]) for i in range(worke...  4.08 us
    unnamed x16, local copies, waits for them, and re-layouts  3.12 us
  transfers between devices with their start and end apart: 16, of which 5 were waited for; matrix products, arithmetic and copies ran while one was open for 0% of the time, Pallas kernels for 26%

profile of v2, /device:TPU:0, one launch (start us, length us, event | category | flops | bytes accessed | tf_op | source)
XLA Modules:
  0.0 46.4 jit_solution(6115898688432292705)
XLA Ops:
  0.6 0.5 %collective-permute-start.3 = (bf16[2048,512]{1,0:T(8,128)(2,1)}, bf16[2048,512]{1,0:T(8,128)(2,1)S(1)}, u32[]{:S(2)}, u32[]{:S(2)}) collective-permute-start(bf16[2048,512]{1,0:T(8,128)(2,1)} %bitcast.9), channel_id=1, source_target_pairs={{0,4},{4,0},{8,12},{12,8},{16,20},{20,16},{24,28},{28,24},{1,5},{5... | collective-permute-start | bytes 6291464 | tf_op jit(solution)/shard_map/ppermute | solution.py:205
  1.1 2.7 %collective-permute-start = (bf16[64,512]{1,0:T(8,128)(2,1)}, bf16[64,512]{1,0:T(8,128)(2,1)S(1)}, u32[]{:S(2)}, u32[]{:S(2)}) collective-permute-start(bf16[64,512]{1,0:T(8,128)(2,1)} %refs_6_.3), channel_id=1, source_target_pairs={{0,1},{1,0},{2,3},{3,2},{4,5},{5,4},{6,7},{7,6},{8,9},{9,8},{10,11... | collective-permute-start | bytes 196616 | tf_op jit(solution)/shard_map/ppermute | solution.py:208
  3.8 0.1 pad_add_fusion.refs_0_
  3.9 1.6 %copy-done.2 = bf16[1,2048,512]{2,1,0:T(8,128)(2,1)S(1)} copy-done((bf16[1,2048,512]{2,1,0:T(8,128)(2,1)S(1)}, bf16[1,2048,512]{2,1,0:T(8,128)(2,1)}, u32[]{:S(2)}) %copy-start.2) | copy-done | bytes 2097176
  5.5 1.2 %copy-done.5 = bf16[256,2048]{1,0:T(8,128)(2,1)S(1)} copy-done((bf16[256,2048]{1,0:T(8,128)(2,1)S(1)}, bf16[256,2048]{1,0:T(8,128)(2,1)}, u32[]{:S(2)}) %copy-start.5) | copy-done | bytes 1048600
  6.7 1.3 %shard_map.101 = (f32[128,512]{1,0:T(8,128)S(1)}, f32[64,512]{1,0:T(8,128)S(1)}, f32[64,512]{1,0:T(8,128)S(1)}) custom-call(s32[2]{0:T(128)S(1)} %pad_add_fusion.refs_0_, bf16[256,2048]{1,0:T(8,128)(2,1)S(1)} %copy-done.5, bf16[2048,512]{1,0:T(8,128)(2,1)S(1)} %bitcast.6), custom_call_target="tpu_custom_call" | custom-call | flops 2640000000 | tf_op jit(solution)/shard_map/pallas_call | solution.py:57
  8.0 0.3 copy-done.4
  8.3 0.9 %shard_map.102 = (bf16[256,512]{1,0:T(8,128)(2,1)S(1)}, f32[256,512]{1,0:T(8,128)S(1)}) custom-call(s32[2]{0:T(128)S(1)} %pad_add_fusion.refs_0_, bf16[2048,512]{1,0:T(8,128)(2,1)S(1)} %bitcast.10, bf16[2048,512]{1,0:T(8,128)(2,1)S(1)} %collective-permute-done.3.refs_2_, f32[128,512]{1,0:T(8,128)S(1)} %get-tuple-element.33.refs_3_, ...), custom_call_target="tpu_custom_call" | custom-call | flops 2969999872 | tf_op jit(solution)/shard_map/pallas_call | solution.py:57
  9.1 1.6 %collective-permute-start.4 = (bf16[256,512]{1,0:T(8,128)(2,1)S(1)}, bf16[256,512]{1,0:T(8,128)(2,1)S(1)}, u32[]{:S(2)}, u32[]{:S(2)}) collective-permute-start(bf16[256,512]{1,0:T(8,128)(2,1)S(1)} %get-tuple-element.35), channel_id=1, source_target_pairs={{0,8},{4,20},{8,0},{12,28},{16,24},{20,4},{24,16},{28,12},{1,9},{5... | collective-permute-start | bytes 786440 | tf_op jit(solution)/shard_map/ppermute | solution.py:205
  10.7 0.9 %shard_map.104 = (bf16[256,512]{1,0:T(8,128)(2,1)S(1)}, f32[256,512]{1,0:T(8,128)S(1)}) custom-call(s32[2]{0:T(128)S(1)} %pad_add_fusion.refs_0_, bf16[2048,512]{1,0:T(8,128)(2,1)S(1)} %bitcast.11, bf16[2048,512]{1,0:T(8,128)(2,1)S(1)} %collective-permute-done.3.refs_2_, f32[256,512]{1,0:T(8,128)S(1)} %get-tuple-element.34.refs_0_.refs_3_), custom_call_target="tpu_custom_call" | custom-call | flops 2969999872 | tf_op jit(solution)/shard_map/pallas_call | solution.py:57
  11.6 0.6 %collective-permute-start.6 = (bf16[256,512]{1,0:T(8,128)(2,1)S(1)}, bf16[256,512]{1,0:T(8,128)(2,1)S(1)}, u32[]{:S(2)}, u32[]{:S(2)}) collective-permute-start(bf16[256,512]{1,0:T(8,128)(2,1)S(1)} %get-tuple-element.39), channel_id=1, source_target_pairs={{0,8},{4,20},{8,0},{12,28},{16,24},{20,4},{24,16},{28,12},{1,9},{5... | collective-permute-start | bytes 786440 | tf_op jit(solution)/shard_map/ppermute | solution.py:205
  12.2 2.6 %collective-permute-start.1 = (bf16[64,512]{1,0:T(8,128)(2,1)S(1)}, bf16[64,512]{1,0:T(8,128)(2,1)S(1)}, u32[]{:S(2)}, u32[]{:S(2)}) collective-permute-start(bf16[64,512]{1,0:T(8,128)(2,1)S(1)} %copy-done.7), channel_id=1, source_target_pairs={{0,2},{1,3},{2,0},{3,1},{4,6},{5,7},{6,4},{7,5},{8,10},{9,11},{10,... | collective-permute-start | bytes 196616 | tf_op jit(solution)/shard_map/ppermute | solution.py:208
  14.8 0.4 collective-permute-start.10
  15.3 0.3 collective-permute-done.4.refs_1_
  15.6 0.4 shard_map.103
  16.0 1.6 %collective-permute-start.5 = (bf16[256,512]{1,0:T(8,128)(2,1)S(1)}, bf16[256,512]{1,0:T(8,128)(2,1)S(1)}, u32[]{:S(2)}, u32[]{:S(2)}) collective-permute-start(bf16[256,512]{1,0:T(8,128)(2,1)S(1)} %get-tuple-element.37), channel_id=1, source_target_pairs={{0,16},{4,12},{8,24},{12,4},{16,0},{20,28},{24,8},{28,20},{1,17},{... | collective-permute-start | bytes 786440 | tf_op jit(solution)/shard_map/ppermute | solution.py:205
  17.6 1.1 %collective-permute-done.6.refs_1_ = bf16[256,512]{1,0:T(8,128)(2,1)S(1)} collective-permute-done((bf16[256,512]{1,0:T(8,128)(2,1)S(1)}, bf16[256,512]{1,0:T(8,128)(2,1)S(1)}, u32[]{:S(2)}, u32[]{:S(2)}) %collective-permute-start.6) | collective-permute-done | bytes 262176 | tf_op jit(solution)/shard_map/ppermute | solution.py:205
  18.7 0.4 shard_map.105
  19.2 1.6 %collective-permute-start.7 = (bf16[256,512]{1,0:T(8,128)(2,1)S(1)}, bf16[256,512]{1,0:T(8,128)(2,1)S(1)}, u32[]{:S(2)}, u32[]{:S(2)}) collective-permute-start(bf16[256,512]{1,0:T(8,128)(2,1)S(1)} %get-tuple-element.43), channel_id=1, source_target_pairs={{0,16},{4,12},{8,24},{12,4},{16,0},{20,28},{24,8},{28,20},{1,17},{... | collective-permute-start | bytes 786440 | tf_op jit(solution)/shard_map/ppermute | solution.py:205
  20.8 2.1 %collective-permute-done.2.refs_9_ = bf16[64,512]{1,0:T(8,128)(2,1)S(1)} collective-permute-done((bf16[64,512]{1,0:T(8,128)(2,1)S(1)}, bf16[64,512]{1,0:T(8,128)(2,1)S(1)}, u32[]{:S(2)}, u32[]{:S(2)}) %collective-permute-start.2) | collective-permute-done | bytes 65568 | tf_op jit(solution)/shard_map/ppermute | solution.py:208
  22.9 2.7 %shard_map.106 = (bf16[2048,512]{1,0:T(8,128)(2,1)}, bf16[256,2048]{1,0:T(8,128)(2,1)}, f32[256,512]{1,0:T(8,128)S(1)}, f32[256,512]{1,0:T(8,128)S(1)}, f32[256,512]{1,0:T(8,128)S(1)}, /*index=5*/f32[256,512]{1,0:T(8,128)S(1)}) custom-call(s32[2]{0:T(128)S(1)} %pad_add_fusion.refs_0_, bf16[256,2048]{1,0:T(8,128)(2,1)S(1)} %copy-done.6, ...), custom_call_target="tpu_custom_call" | custom-call | flops 9900000256 | tf_op jit(solution)/shard_map/pallas_call | solution.py:57
  25.7 0.4 shard_map.107
  26.1 1.6 %collective-permute-start.14 = (bf16[256,512]{1,0:T(8,128)(2,1)S(1)}, bf16[256,512]{1,0:T(8,128)(2,1)S(1)}, u32[]{:S(2)}, u32[]{:S(2)}) collective-permute-start(bf16[256,512]{1,0:T(8,128)(2,1)S(1)} %get-tuple-element.45), channel_id=1, source_target_pairs={{0,8},{4,20},{8,0},{12,28},{16,24},{20,4},{24,16},{28,12},{1,9},{5... | collective-permute-start | bytes 786440 | tf_op jit(solution)/shard_map/ppermute | solution.py:205
  27.7 0.4 shard_map.108
  28.1 0.6 %collective-permute-start.12 = (bf16[256,512]{1,0:T(8,128)(2,1)S(1)}, bf16[256,512]{1,0:T(8,128)(2,1)S(1)}, u32[]{:S(2)}, u32[]{:S(2)}) collective-permute-start(bf16[256,512]{1,0:T(8,128)(2,1)S(1)} %get-tuple-element.46), channel_id=1, source_target_pairs={{0,8},{4,20},{8,0},{12,28},{16,24},{20,4},{24,16},{28,12},{1,9},{5... | collective-permute-start | bytes 786440 | tf_op jit(solution)/shard_map/ppermute | solution.py:205
  28.7 0.5 %collective-permute-start.8 = (bf16[256,512]{1,0:T(8,128)(2,1)S(1)}, bf16[256,512]{1,0:T(8,128)(2,1)S(1)}, u32[]{:S(2)}, u32[]{:S(2)}) collective-permute-start(bf16[256,512]{1,0:T(8,128)(2,1)S(1)} %get-tuple-element.45), channel_id=1, source_target_pairs={{0,4},{4,0},{8,12},{12,8},{16,20},{20,16},{24,28},{28,24},{1,5},{5... | collective-permute-start | bytes 786440 | tf_op jit(solution)/shard_map/ppermute | solution.py:205
  29.3 3.5 %collective-permute-start.11 = (f32[64,512]{1,0:T(8,128)S(1)}, f32[64,512]{1,0:T(8,128)S(1)}, u32[]{:S(2)}, u32[]{:S(2)}) collective-permute-start(f32[64,512]{1,0:T(8,128)S(1)} %get-tuple-element.50), channel_id=1, source_target_pairs={{0,2},{1,3},{2,0},{3,1},{4,6},{5,7},{6,4},{7,5},{8,10},{9,11},{10,... | collective-permute-start | bytes 393224 | tf_op jit(solution)/shard_map/ppermute | solution.py:208
  32.7 2.6 %collective-permute-done.12.refs_6_ = bf16[256,512]{1,0:T(8,128)(2,1)S(1)} collective-permute-done((bf16[256,512]{1,0:T(8,128)(2,1)S(1)}, bf16[256,512]{1,0:T(8,128)(2,1)S(1)}, u32[]{:S(2)}, u32[]{:S(2)}) %collective-permute-start.12) | collective-permute-done | bytes 262176 | tf_op jit(solution)/shard_map/ppermute | solution.py:205
  35.4 3.8 %collective-permute-done.11.refs_15_ = f32[64,512]{1,0:T(8,128)S(1)} collective-permute-done((f32[64,512]{1,0:T(8,128)S(1)}, f32[64,512]{1,0:T(8,128)S(1)}, u32[]{:S(2)}, u32[]{:S(2)}) %collective-permute-start.11) | collective-permute-done | bytes 131104 | tf_op jit(solution)/shard_map/ppermute | solution.py:208
  39.2 3.6 %shard_map.110 = (bf16[2048,512]{1,0:T(8,128)(2,1)}, bf16[256,2048]{1,0:T(8,128)(2,1)}, bf16[2048,512]{1,0:T(8,128)(2,1)}, f32[256,512]{1,0:T(8,128)}, bf16[64,512]{1,0:T(8,128)(2,1)}) custom-call(s32[2]{0:T(128)S(1)} %pad_add_fusion.refs_0_, bf16[256,2048]{1,0:T(8,128)(2,1)S(1)} %copy-done.6, ...), custom_call_target="tpu_custom_call", output_to_operand_aliasing={{0}: (16, {}), {1}: (17, {})} | custom-call | flops 9900000256 | tf_op jit(solution)/shard_map/pallas_call | solution.py:57
  42.8 2.0 %shard_map.111.refs_3_ = bf16[2048,512]{1,0:T(8,128)(2,1)} custom-call(s32[2]{0:T(128)S(1)} %pad_add_fusion.refs_0_, f32[256,512]{1,0:T(8,128)S(1)} %get-tuple-element.41.refs_2_.refs_3_.refs_1_, f32[256,512]{1,0:T(8,128)S(1)} %get-tuple-element.56.refs_2_, f32[256,512]{1,0:T(8,128)S(1)} %get-tuple-element.57.refs_3_, ...), custom_call_target="tpu_custom_call", output_to_operand_aliasing={{}: (7, {})} | custom-call | flops 5939999744 | tf_op jit(solution)/shard_map/pallas_call | solution.py:57
  44.8 1.5 %shard_map.112 = bf16[2048,512]{1,0:T(8,128)(2,1)} custom-call(s32[2]{0:T(128)S(1)} %pad_add_fusion.refs_0_, f32[256,512]{1,0:T(8,128)S(1)} %get-tuple-element.55.refs_1_, bf16[256,512]{1,0:T(8,128)(2,1)S(1)} %collective-permute-done.13.refs_2_, bf16[2048,512]{1,0:T(8,128)(2,1)} %shard_map.111.refs_3_), custom_call_target="tpu_custom_call", output_to_operand_aliasing={{}: (3, {})} | custom-call | flops 5939999744 | tf_op jit(solution)/shard_map/pallas_call | solution.py:57
  (29 shorter events, 0.2 us)
Async XLA Ops:
  0.6 7.4 %collective-permute-start.3 = (bf16[2048,512]{1,0:T(8,128)(2,1)}, bf16[2048,512]{1,0:T(8,128)(2,1)S(1)}, u32[]{:S(2)}, u32[]{:S(2)}) collective-permute-start(bf16[2048,512]{1,0:T(8,128)(2,1)} %bitcast.9), channel_id=1, source_target_pairs={{0,4},{4,0},{8,12},{12,8},{16,20},{20,16},{24,28},{28,24},{1,5},{5... | collective-permute-start | bytes 6291464 | tf_op jit(solution)/shard_map/ppermute | solution.py:205
  1.1 6.8 %collective-permute-start = (bf16[64,512]{1,0:T(8,128)(2,1)}, bf16[64,512]{1,0:T(8,128)(2,1)S(1)}, u32[]{:S(2)}, u32[]{:S(2)}) collective-permute-start(bf16[64,512]{1,0:T(8,128)(2,1)} %refs_6_.3), channel_id=1, source_target_pairs={{0,1},{1,0},{2,3},{3,2},{4,5},{5,4},{6,7},{7,6},{8,9},{9,8},{10,11... | collective-permute-start | bytes 196616 | tf_op jit(solution)/shard_map/ppermute | solution.py:208
  3.9 1.6 %copy-start.2 = (bf16[1,2048,512]{2,1,0:T(8,128)(2,1)S(1)}, bf16[1,2048,512]{2,1,0:T(8,128)(2,1)}, u32[]{:S(2)}) copy-start(bf16[1,2048,512]{2,1,0:T(8,128)(2,1)} %param.7) | copy-start | bytes 6291460
  5.5 1.2 %copy-start.5 = (bf16[256,2048]{1,0:T(8,128)(2,1)S(1)}, bf16[256,2048]{1,0:T(8,128)(2,1)}, u32[]{:S(2)}) copy-start(bf16[256,2048]{1,0:T(8,128)(2,1)} %refs_1_.5) | copy-start | bytes 3145732
  6.7 1.6 %copy-start.4 = (bf16[1,2048,512]{2,1,0:T(8,128)(2,1)S(1)}, bf16[1,2048,512]{2,1,0:T(8,128)(2,1)}, u32[]{:S(2)}) copy-start(bf16[1,2048,512]{2,1,0:T(8,128)(2,1)} %param.11) | copy-start | bytes 6291460
  9.1 6.4 %collective-permute-start.4 = (bf16[256,512]{1,0:T(8,128)(2,1)S(1)}, bf16[256,512]{1,0:T(8,128)(2,1)S(1)}, u32[]{:S(2)}, u32[]{:S(2)}) collective-permute-start(bf16[256,512]{1,0:T(8,128)(2,1)S(1)} %get-tuple-element.35), channel_id=1, source_target_pairs={{0,8},{4,20},{8,0},{12,28},{16,24},{20,4},{24,16},{28,12},{1,9},{5... | collective-permute-start | bytes 786440 | tf_op jit(solution)/shard_map/ppermute | solution.py:205
  10.7 1.5 %copy-start.7 = (bf16[64,512]{1,0:T(8,128)(2,1)S(1)}, bf16[64,512]{1,0:T(8,128)(2,1)}, u32[]{:S(2)}) copy-start(bf16[64,512]{1,0:T(8,128)(2,1)} %refs_6_.3) | copy-start | bytes 196612
  11.6 7.2 %collective-permute-start.6 = (bf16[256,512]{1,0:T(8,128)(2,1)S(1)}, bf16[256,512]{1,0:T(8,128)(2,1)S(1)}, u32[]{:S(2)}, u32[]{:S(2)}) collective-permute-start(bf16[256,512]{1,0:T(8,128)(2,1)S(1)} %get-tuple-element.39), channel_id=1, source_target_pairs={{0,8},{4,20},{8,0},{12,28},{16,24},{20,4},{24,16},{28,12},{1,9},{5... | collective-permute-start | bytes 786440 | tf_op jit(solution)/shard_map/ppermute | solution.py:205
  12.2 8.6 %collective-permute-start.1 = (bf16[64,512]{1,0:T(8,128)(2,1)S(1)}, bf16[64,512]{1,0:T(8,128)(2,1)S(1)}, u32[]{:S(2)}, u32[]{:S(2)}) collective-permute-start(bf16[64,512]{1,0:T(8,128)(2,1)S(1)} %copy-done.7), channel_id=1, source_target_pairs={{0,2},{1,3},{2,0},{3,1},{4,6},{5,7},{6,4},{7,5},{8,10},{9,11},{10,... | collective-permute-start | bytes 196616 | tf_op jit(solution)/shard_map/ppermute | solution.py:208
  14.8 14.5 %collective-permute-start.10 = (f32[128,512]{1,0:T(8,128)S(1)}, f32[128,512]{1,0:T(8,128)S(1)}, u32[]{:S(2)}, u32[]{:S(2)}) collective-permute-start(f32[128,512]{1,0:T(8,128)S(1)} %get-tuple-element.33.refs_3_), channel_id=1, source_target_pairs={{0,1},{1,0},{2,3},{3,2},{4,5},{5,4},{6,7},{7,6},{8,9},{9,8},{10,11... | collective-permute-start | bytes 786440 | tf_op jit(solution)/shard_map/ppermute | solution.py:208
  15.2 7.7 %collective-permute-start.2 = (bf16[64,512]{1,0:T(8,128)(2,1)S(1)}, bf16[64,512]{1,0:T(8,128)(2,1)S(1)}, u32[]{:S(2)}, u32[]{:S(2)}) collective-permute-start(bf16[64,512]{1,0:T(8,128)(2,1)S(1)} %collective-permute-done.refs_4_.refs_7_), channel_id=1, source_target_pairs={{0,2},{1,3},{2,0},{3,1},{4,6},{5,7},{6,4},{7,5},{8,10},{9,11},{10,... | collective-permute-start | bytes 196616 | tf_op jit(solution)/shard_map/ppermute | solution.py:208
  15.6 7.3 %copy-start.1 = (f32[2048,512]{1,0:T(8,128)S(1)}, f32[2048,512]{1,0:T(8,128)}, u32[]{:S(2)}) copy-start(f32[2048,512]{1,0:T(8,128)} %refs_4_.3) | copy-start | bytes 12582916
  15.6 7.3 %copy-start.3 = (bf16[1,2048,512]{2,1,0:T(8,128)(2,1)S(1)}, bf16[1,2048,512]{2,1,0:T(8,128)(2,1)}, u32[]{:S(2)}) copy-start(bf16[1,2048,512]{2,1,0:T(8,128)(2,1)} %param.7) | copy-start | bytes 6291460
  16.0 9.6 %collective-permute-start.5 = (bf16[256,512]{1,0:T(8,128)(2,1)S(1)}, bf16[256,512]{1,0:T(8,128)(2,1)S(1)}, u32[]{:S(2)}, u32[]{:S(2)}) collective-permute-start(bf16[256,512]{1,0:T(8,128)(2,1)S(1)} %get-tuple-element.37), channel_id=1, source_target_pairs={{0,16},{4,12},{8,24},{12,4},{16,0},{20,28},{24,8},{28,20},{1,17},{... | collective-permute-start | bytes 786440 | tf_op jit(solution)/shard_map/ppermute | solution.py:205
  18.7 4.2 %copy-start = (f32[2048,512]{1,0:T(8,128)S(1)}, f32[2048,512]{1,0:T(8,128)}, u32[]{:S(2)}) copy-start(f32[2048,512]{1,0:T(8,128)} %refs_3_.3) | copy-start | bytes 12582916
  18.7 4.2 %copy-start.6 = (bf16[256,2048]{1,0:T(8,128)(2,1)S(1)}, bf16[256,2048]{1,0:T(8,128)(2,1)}, u32[]{:S(2)}) copy-start(bf16[256,2048]{1,0:T(8,128)(2,1)} %refs_1_.5) | copy-start | bytes 3145732
  19.2 8.5 %collective-permute-start.7 = (bf16[256,512]{1,0:T(8,128)(2,1)S(1)}, bf16[256,512]{1,0:T(8,128)(2,1)S(1)}, u32[]{:S(2)}, u32[]{:S(2)}) collective-permute-start(bf16[256,512]{1,0:T(8,128)(2,1)S(1)} %get-tuple-element.43), channel_id=1, source_target_pairs={{0,16},{4,12},{8,24},{12,4},{16,0},{20,28},{24,8},{28,20},{1,17},{... | collective-permute-start | bytes 786440 | tf_op jit(solution)/shard_map/ppermute | solution.py:205
  26.1 6.6 %collective-permute-start.14 = (bf16[256,512]{1,0:T(8,128)(2,1)S(1)}, bf16[256,512]{1,0:T(8,128)(2,1)S(1)}, u32[]{:S(2)}, u32[]{:S(2)}) collective-permute-start(bf16[256,512]{1,0:T(8,128)(2,1)S(1)} %get-tuple-element.45), channel_id=1, source_target_pairs={{0,8},{4,20},{8,0},{12,28},{16,24},{20,4},{24,16},{28,12},{1,9},{5... | collective-permute-start | bytes 786440 | tf_op jit(solution)/shard_map/ppermute | solution.py:205
  28.1 7.2 %collective-permute-start.12 = (bf16[256,512]{1,0:T(8,128)(2,1)S(1)}, bf16[256,512]{1,0:T(8,128)(2,1)S(1)}, u32[]{:S(2)}, u32[]{:S(2)}) collective-permute-start(bf16[256,512]{1,0:T(8,128)(2,1)S(1)} %get-tuple-element.46), channel_id=1, source_target_pairs={{0,8},{4,20},{8,0},{12,28},{16,24},{20,4},{24,16},{28,12},{1,9},{5... | collective-permute-start | bytes 786440 | tf_op jit(solution)/shard_map/ppermute | solution.py:205
  28.7 10.5 %collective-permute-start.9 = (bf16[256,512]{1,0:T(8,128)(2,1)S(1)}, bf16[256,512]{1,0:T(8,128)(2,1)S(1)}, u32[]{:S(2)}, u32[]{:S(2)}) collective-permute-start(bf16[256,512]{1,0:T(8,128)(2,1)S(1)} %get-tuple-element.46), channel_id=1, source_target_pairs={{0,4},{4,0},{8,12},{12,8},{16,20},{20,16},{24,28},{28,24},{1,5},{5... | collective-permute-start | bytes 786440 | tf_op jit(solution)/shard_map/ppermute | solution.py:205
  28.7 10.5 %collective-permute-start.8 = (bf16[256,512]{1,0:T(8,128)(2,1)S(1)}, bf16[256,512]{1,0:T(8,128)(2,1)S(1)}, u32[]{:S(2)}, u32[]{:S(2)}) collective-permute-start(bf16[256,512]{1,0:T(8,128)(2,1)S(1)} %get-tuple-element.45), channel_id=1, source_target_pairs={{0,4},{4,0},{8,12},{12,8},{16,20},{20,16},{24,28},{28,24},{1,5},{5... | collective-permute-start | bytes 786440 | tf_op jit(solution)/shard_map/ppermute | solution.py:205
  29.3 9.9 %collective-permute-start.11 = (f32[64,512]{1,0:T(8,128)S(1)}, f32[64,512]{1,0:T(8,128)S(1)}, u32[]{:S(2)}, u32[]{:S(2)}) collective-permute-start(f32[64,512]{1,0:T(8,128)S(1)} %get-tuple-element.50), channel_id=1, source_target_pairs={{0,2},{1,3},{2,0},{3,1},{4,6},{5,7},{6,4},{7,5},{8,10},{9,11},{10,... | collective-permute-start | bytes 393224 | tf_op jit(solution)/shard_map/ppermute | solution.py:208
  32.7 10.1 %collective-permute-start.15 = (bf16[256,512]{1,0:T(8,128)(2,1)S(1)}, bf16[256,512]{1,0:T(8,128)(2,1)S(1)}, u32[]{:S(2)}, u32[]{:S(2)}) collective-permute-start(bf16[256,512]{1,0:T(8,128)(2,1)S(1)} %collective-permute-done.14.refs_4_), channel_id=1, source_target_pairs={{0,4},{4,0},{8,12},{12,8},{16,20},{20,16},{24,28},{28,24},{1,5},{5... | collective-permute-start | bytes 786440 | tf_op jit(solution)/shard_map/ppermute | solution.py:205
  35.4 9.5 %collective-permute-start.13 = (bf16[256,512]{1,0:T(8,128)(2,1)S(1)}, bf16[256,512]{1,0:T(8,128)(2,1)S(1)}, u32[]{:S(2)}, u32[]{:S(2)}) collective-permute-start(bf16[256,512]{1,0:T(8,128)(2,1)S(1)} %collective-permute-done.12.refs_6_), channel_id=1, source_target_pairs={{0,4},{4,0},{8,12},{12,8},{16,20},{20,16},{24,28},{28,24},{1,5},{5... | collective-permute-start | bytes 786440 | tf_op jit(solution)/shard_map/ppermute | solution.py:205

commit v3 on v2

v3 whole, which is shorter than its diff:
```python
import functools
import math

import jax
import jax.numpy as jnp
from jax import lax
from jax.experimental import pallas as pl
from jax.experimental.pallas import tpu as pltpu
from jax.sharding import PartitionSpec as P

inner_rate = 0.0005
outer_rate = 0.7
outer_momentum = 0.9

stale_bound = 0.29882812
floor = 2.0**-14
power = 250.0 / math.log2(1.0 + stale_bound / floor)


def encode(value, count):
    grown = jnp.log(jnp.abs(value) * (1.0 / (floor * count)) + 1.0)
    code = jnp.exp2(grown * (power / math.log(2.0)) - 125.0)
    return jnp.where(value < 0, -code, code).astype(jnp.bfloat16)


def decode(code, count):
    code = code.astype(jnp.float32)
    grown = jnp.exp2(jnp.log(jnp.abs(code)) * (1.0 / (power * math.log(2.0))) + 125.0 / power)
    value = (grown - 1.0) * (floor * count)
    return jnp.where(code < 0, -value, value)


pace = 3.3e9
cost = {"pair": (0.9, 0.9), "keys": 0.1, "add": (0.5, 0.5), "keys_add": 0.4, "fresh": (0.5, 3.0), "update": (8.0, 8.0), "relay": 0.3}
opt = {"kg_gate": 0, "keys_at": 2, "keys_gate": 1, "fresh_gate": 1, "add_gate": 3}


def place(me):
    core, low, high = me % 2, (me // 2) % 2, me // 4
    return core, jnp.where(core == 0, low, high), jnp.where(core == 0, high, low)


def block(region, half, sub):
    return jnp.where(region == 0, 4 * sub + 2 * half, 4 * half + 2 * sub + 1)


SMEM, VMEM, HBM, ANY = pltpu.SMEM, pltpu.VMEM, pltpu.HBM, pl.ANY


def call(kernel, ins, outs, scratch=(), after=(), aliases=None, micros=1.0, vmem=12):
    late = len(after)

    def body(*refs):
        kernel(*refs[: len(ins)], *refs[len(ins) + late :])

    def placed(array, space):
        return pltpu.with_memory_space_constraint(array, space) if space in (HBM, VMEM) else array

    return pl.pallas_call(
        body,
        in_specs=[pl.BlockSpec(memory_space=s) for _, s in ins] + [pl.BlockSpec(memory_space=ANY)] * late,
        out_specs=[pl.BlockSpec(memory_space=s) for _, _, s in outs],
        out_shape=[s(shape, dtype) for shape, dtype, s in outs],
        scratch_shapes=scratch,
        input_output_aliases=aliases or {},
        cost_estimate=pl.CostEstimate(flops=int(micros * pace), bytes_accessed=0, transcendentals=0),
        compiler_params=pltpu.CompilerParams(vmem_limit_bytes=vmem * 2**20),
    )(*[placed(a, s) for a, s in ins], *after)


def rows(ref, at, size):
    return ref.at[pl.ds(pl.multiple_of(at * size, size), size), :]


def pair_sums(size, own, other, places, code, keep):
    step = 64

    def summed(k, at):
        there = pl.ds(pl.multiple_of(places[k] * size + at, step), step)
        return own[k * size + at : k * size + at + step, :].astype(jnp.float32) + other[there, :].astype(jnp.float32)

    for at in range(0, size, step):
        code[at : at + step, :] = encode(summed(0, at), 2)
        keep[at : at + step, :] = summed(1, at)


def first_pair_kernel(size, stale, other, code, keep, next_own, own, sem):
    core, first, _ = place(lax.axis_index("worker"))
    places = [[block(core, half, sub) for half in (1 - first, first)] for sub in range(2)]
    copies = [
        pltpu.make_async_copy(rows(stale, at, size), target.at[k * size : (k + 1) * size, :], sem.at[2 * sub + k])
        for sub, target in enumerate((own, next_own))
        for k, at in enumerate(places[sub])
    ]
    for copy in copies:
        copy.start()
    for copy in copies[:2]:
        copy.wait()
    pair_sums(size, own, other, places[0], code, keep)
    for copy in copies[2:]:
        copy.wait()


def second_pair_kernel(size, own, other, grad, grad_far, code, keep, both):
    core, first, _ = place(lax.axis_index("worker"))
    places = [block(core, half, 1) for half in (1 - first, first)]
    pair_sums(size, own, other, places, code, keep)
    both[: grad.shape[0], :] = grad[...]
    both[grad.shape[0] :, :] = grad_far[...]


def add_kernel(held, total, value, received, out, code):
    summed = value[...] + decode(received[...], held)
    out[...] = summed
    code[...] = encode(summed, total)


def keys_kernel(tokens, weights, sent, own, later, total):
    total[...] = jnp.dot(tokens[...], weights[...], preferred_element_type=jnp.float32)
    size = own.shape[0]
    shard = lax.axis_index("fsdp")
    sent[:size, :] = rows(total, shard ^ 1, size)[...]
    sent[size:, :] = rows(total, shard ^ 3, size)[...]
    own[...] = rows(total, shard, size)[...]
    later[...] = rows(total, shard ^ 2, size)[...]


def keys_add_kernel(received, own, later, own_out, later_out):
    size = own.shape[0]
    own_out[...] = own[...] + received[:size, :]
    later_out[...] = later[...] + received[size:, :]


def relay_kernel(*refs):
    half = len(refs) // 2
    for source, target in zip(refs[:half], refs[half:], strict=True):
        target[...] = source[...]


def spots(me):
    core, first, last = place(me)
    return {
        "own": (core, first),
        "near": (core, 1 - first),
        "across": (1 - core, last),
        "far": (1 - core, 1 - last),
    }


def span_of(size, kind, sub):
    return pl.ds(pl.multiple_of(block(*spots(lax.axis_index("worker"))[kind], sub) * size, size), size)


def fresh_kernel(workers, kinds, before, tokens, weights, anchor, momentum, stale, near, far, *rest):
    count = len(kinds)
    if before:
        sums, early, rest = rest[:count], rest[count : count + 2], rest[count + 2 :]
        fresh_out, grad_out, fresh_buf, grad_buf, param_buf, moment, portion, sem = rest
    else:
        fresh_buf, grad_buf, bases, portion = rest[0], rest[1], rest[2 : 2 + count], rest[2 + count]
    size = weights.shape[0] // workers
    copies = []
    if before:
        for k, which in enumerate(before):
            span = span_of(size, *which)
            copies.append(pltpu.make_async_copy(early[0].at[k], fresh_out.at[span, :], sem.at[2 * k]))
            copies.append(pltpu.make_async_copy(early[1].at[k], grad_out.at[:, span], sem.at[2 * k + 1]))
        for copy in copies:
            copy.start()
        _, _, last = place(lax.axis_index("worker"))
        average = jnp.where(last == 0, sums[0][...], sums[1][...]) / workers
        moment[...] = outer_momentum * rows(momentum, lax.axis_index("worker"), size)[...] + average
    held = near.shape[0] // 2
    shard = lax.axis_index("fsdp")
    for d, source in ((0, near.at[:held, :]), (2, near.at[held:, :]), (1, far.at[:held, :]), (3, far.at[held:, :])):
        rows(portion, shard ^ d, held)[...] = source[...]
    for k, which in enumerate(kinds):
        span = span_of(size, *which)
        weight = weights[span, :]
        grad_weight = lax.dot_general(
            tokens[:, span], portion[...], (((0,), (0,)), ((), ())), preferred_element_type=jnp.float32
        )
        grad_buf[k] = lax.dot_general(
            portion[...], weight, (((1,), (1,)), ((), ())), preferred_element_type=jnp.float32
        ).astype(jnp.bfloat16)
        value = anchor[span, :]
        fresh = value - (weight.astype(jnp.float32) - inner_rate * grad_weight)
        fresh_buf[k] = fresh.astype(jnp.bfloat16)
        base = value - outer_rate * (
            outer_momentum * outer_momentum * momentum[span, :]
            + (fresh - stale[span, :].astype(jnp.float32)) / workers
        )
        if before:
            param_buf[k] = finished(kinds[k][0], workers, base, sums[k])
        else:
            bases[k][...] = base
    for copy in copies:
        copy.wait()


def finished(kind, workers, base, piece):
    total = piece[...]
    if kind != "own":
        total = decode(total, workers)
    return (base - (outer_rate * (1.0 + outer_momentum) / workers) * total).astype(jnp.bfloat16)


def near_kernel(workers, kinds, done, *rest):
    count = len(kinds)
    bases, pieces, (fresh_buf, grad_buf, param_buf, moment), rest = (
        rest[:count],
        rest[count : 2 * count],
        rest[2 * count : 2 * count + 4],
        rest[2 * count + 6 :],
    )
    fresh_out, grad_out, out, moment_out, out_buf, sem = rest
    size = out.shape[0] // workers
    copies = []

    def send(source, target):
        copies.append(pltpu.make_async_copy(source, target, sem.at[len(copies)]))
        copies[-1].start()

    send(moment, moment_out)
    for k, which in enumerate(done):
        span = span_of(size, *which)
        send(fresh_buf.at[k], fresh_out.at[span, :])
        send(grad_buf.at[k], grad_out.at[:, span])
        send(param_buf.at[k], out.at[span, :])
    for k, which in enumerate(kinds):
        out_buf[k] = finished(which[0], workers, bases[k][...], pieces[k])
        send(out_buf.at[k], out.at[span_of(size, *which), :])
    for copy in copies:
        copy.wait()


def far_kernel(workers, kinds, *rest):
    count = len(kinds)
    bases, pieces, rest = rest[:count], rest[count : 2 * count], rest[2 * count :]
    own, received, _, out, key_out, out_buf, key_buf, sem = rest
    size = out.shape[0] // workers
    key_buf[...] = (own[...] + received[...]).astype(jnp.bfloat16)
    copies = [pltpu.make_async_copy(key_buf, key_out, sem.at[count])]
    copies[0].start()
    for k, which in enumerate(kinds):
        out_buf[k] = finished(which[0], workers, bases[k][...], pieces[k])
        copies.append(
            pltpu.make_async_copy(out_buf.at[k], out.at[span_of(size, *which), :], sem.at[k])
        )
        copies[-1].start()
    for copy in copies:
        copy.wait()


def fast(tokens, inner_weight, key_grad, anchor, momentum, stale_delta):
    workers, shards = lax.axis_size("worker"), lax.axis_size("fsdp")
    f32, bf16 = jnp.float32, jnp.bfloat16
    DMA = pltpu.SemaphoreType.DMA
    weights, stale = inner_weight[0], stale_delta[0]
    height, columns = stale.shape
    batch = tokens.shape[0]
    size = height // workers
    window = (size, columns)

    def swap(value, flips):
        return lax.ppermute(value, "worker", [(i, i ^ flips[i % 2]) for i in range(workers)])

    def across_shards(value, distance):
        return lax.ppermute(value, "fsdp", [(i, i ^ distance) for i in range(shards)])

    beside, first, last = (1, 1), (2, 4), (4, 2)
    chunks = range(2)

    key_rows = batch // shards
    other = swap(stale, beside)
    grad_far = across_shards(key_grad, 2)
    block_of_keys = (key_rows, columns)
    sums = [(window, bf16, VMEM), (window, f32, VMEM)]
    first_code, first_keep, next_own = call(
        functools.partial(first_pair_kernel, size),
        [(stale, HBM), (other, VMEM)],
        [*sums, ((2 * size, columns), bf16, VMEM)],
        scratch=[pltpu.VMEM((2 * size, columns), bf16), DMA((4,))],
        micros=cost["pair"][0],
    )
    second_code, second_keep, both = call(
        functools.partial(second_pair_kernel, size),
        [(next_own, VMEM), (other, VMEM), (key_grad, VMEM), (grad_far, VMEM)],
        [*sums, ((2 * key_grad.shape[0], columns), bf16, VMEM)],
        after=[first_keep],
        micros=cost["pair"][1],
    )
    codes, keeps = [first_code, second_code], [first_keep, second_keep]
    got = [swap(codes[c], first) for c in chunks]

    def keys(after):
        return call(
            keys_kernel,
            [(tokens, VMEM), (weights, VMEM)],
            [((2 * key_rows, columns), f32, VMEM), (block_of_keys, f32, VMEM), (block_of_keys, f32, VMEM)],
            scratch=[pltpu.VMEM((batch, columns), f32)],
            after=after,
            micros=cost["keys"],
        )

    grads = [both, across_shards(both, 1)]
    def added(held, total, gates):
        for c in chunks:
            keeps[c], codes[c] = call(
                functools.partial(add_kernel, held, total),
                [(keeps[c], VMEM), (got[c], VMEM)],
                [(window, f32, VMEM), (window, bf16, VMEM)],
                after=gates[c] if c == 0 else [keeps[0], *gates[c]],
                micros=cost["add"][c],
            )

    blocks = (4, size, columns), (4, batch, size)

    def fresh(kinds, after, sums=(), early=(), before=None):
        ins = [(tokens, VMEM), (weights, VMEM), (anchor, VMEM), (momentum, VMEM), (stale, VMEM)]
        ins += [(g, VMEM) for g in [*grads, *sums, *early]]
        outs = [(blocks[0], bf16, VMEM), (blocks[1], bf16, VMEM)]
        scratch = [pltpu.VMEM((batch, columns), bf16)]
        if before is None:
            outs += [(window, f32, VMEM)] * len(kinds)
        else:
            outs = [((height, columns), bf16, HBM), ((batch, height), bf16, HBM), *outs]
            outs += [(blocks[0], bf16, VMEM), (window, f32, VMEM)]
            scratch.append(DMA((2 * len(before),)))
        return call(
            functools.partial(fresh_kernel, workers, kinds, before),
            ins,
            outs,
            scratch=scratch,
            after=after,
            micros=cost["fresh"][0 if before is None else 1],
        )

    late_kinds = [("near", 0), ("far", 0), ("near", 1), ("far", 1)]
    gates = [[], []]
    if opt["keys_at"] == 0:
        sent, own_keys, later_keys = keys([keeps[1]])
        if opt["keys_gate"]:
            gates[opt["keys_gate"] - 1].append(sent)
    if opt["kg_gate"]:
        gates[opt["kg_gate"] - 1].append(grads[1])
    added(2, 4, gates)
    got = [swap(codes[c], last) for c in chunks]
    if opt["keys_at"]:
        sent, own_keys, later_keys = keys([keeps[opt["keys_at"] - 1]])
    key_near = across_shards(sent, 1)
    own_keys, later_keys = call(
        keys_add_kernel,
        [(key_near, VMEM), (own_keys, VMEM), (later_keys, VMEM)],
        [(block_of_keys, f32, VMEM), (block_of_keys, f32, VMEM)],
        after=[keeps[1]],
        micros=cost["keys_add"],
    )
    key_far = across_shards(later_keys, 2)
    *early, base_a, base_b, base_c, base_d = fresh(late_kinds, [keeps[1]])
    bases = [base_a, base_b, base_c, base_d]
    gates = [[], []]
    if opt["fresh_gate"]:
        gates[opt["fresh_gate"] - 1].append(bases[0])
    if opt["add_gate"] in (1, 2):
        gates[opt["add_gate"] - 1].append(own_keys)
    added(4, 8, gates)
    near = [swap(codes[c], first) for c in chunks]
    across = [swap(codes[c], beside) for c in chunks]
    soon_kinds = [("own", 0), ("own", 1), ("across", 0), ("across", 1)]
    fresh_out, grad_input, *done = fresh(
        soon_kinds, [own_keys] if opt["add_gate"] == 3 else [], [*keeps, *across], early, late_kinds
    )
    relayed = call(
        relay_kernel, [(n, VMEM) for n in near], [(window, bf16, VMEM)] * 2, after=[done[2]], micros=cost["relay"]
    )
    far = [swap(n, beside) for n in relayed]

    ins = [(value, VMEM) for value in (bases[0], bases[2], *near, *done)]
    ins += [(fresh_out, HBM), (grad_input, HBM)]
    fresh_out, grad_input, updated, new_moment = call(
        functools.partial(near_kernel, workers, late_kinds[::2], soon_kinds),
        ins,
        [
            ((height, columns), bf16, HBM),
            ((batch, height), bf16, HBM),
            ((height, columns), bf16, HBM),
            (window, f32, HBM),
        ],
        scratch=[pltpu.VMEM((2, *window), bf16), DMA((3 * len(soon_kinds) + 3,))],
        aliases={len(ins) - 2: 0, len(ins) - 1: 1},
        micros=cost["update"][0],
    )
    ins = [(value, VMEM) for value in (bases[1], bases[3], *far, own_keys, key_far)]
    ins.append((updated, HBM))
    updated, key_out = call(
        functools.partial(far_kernel, workers, late_kinds[1::2]),
        ins,
        [((height, columns), bf16, HBM), ((key_rows, columns), bf16, HBM)],
        scratch=[pltpu.VMEM((2, *window), bf16), pltpu.VMEM((key_rows, columns), bf16), DMA((3,))],
        aliases={len(ins) - 1: 0},
        micros=cost["update"][1],
    )
    return key_out, grad_input, updated[None], new_moment, fresh_out[None]


def plain(tokens, inner_weight, key_grad, anchor, momentum, stale_delta):
    weights = inner_weight[0]
    key_out = lax.psum_scatter(
        jnp.dot(tokens, weights, preferred_element_type=jnp.float32), "fsdp", scatter_dimension=0, tiled=True
    ).astype(jnp.bfloat16)
    portion = lax.all_gather(key_grad, "fsdp", axis=0, tiled=True)
    grad_weight = lax.dot_general(tokens, portion, (((0,), (0,)), ((), ())), preferred_element_type=jnp.float32)
    grad_input = lax.dot_general(portion, weights, (((1,), (1,)), ((), ())), preferred_element_type=jnp.float32)
    fresh_term = anchor - (weights.astype(jnp.float32) - inner_rate * grad_weight)
    stale_value = stale_delta[0].astype(jnp.float32)
    workers = lax.axis_size("worker")
    average = lax.psum(stale_value, "worker") / workers
    moment_full = outer_momentum * momentum + average
    common_term = average + outer_momentum * moment_full
    share_rows = anchor.shape[0] // workers
    new_moment = lax.dynamic_slice_in_dim(moment_full, lax.axis_index("worker") * share_rows, share_rows, 0)
    updated = anchor - outer_rate * (common_term + (fresh_term - stale_value) / workers)
    return (
        key_out,
        grad_input.astype(jnp.bfloat16),
        updated[None].astype(jnp.bfloat16),
        new_moment,
        fresh_term[None].astype(jnp.bfloat16),
    )


def local(*args):
    tokens, inner_weight = args[:2]
    workers, shards = lax.axis_size("worker"), lax.axis_size("fsdp")
    size = inner_weight.shape[1] // workers
    fits = workers == 2**3 and shards == 2**2
    fits = fits and size % 128 == 0 and tokens.shape[0] // shards % 16 == 0
    return (fast if fits else plain)(*args)


def solution(mesh):
    in_specs = (
        P("worker", "fsdp"),
        P("worker", "fsdp", None),
        P(("worker", "fsdp"), None),
        P("fsdp", None),
        P("fsdp", None),
        P("worker", "fsdp", None),
    )
    out_specs = (
        P(("worker", "fsdp"), None),
        P("worker", "fsdp"),
        P("worker", "fsdp", None),
        P(("fsdp", "worker"), None),
        P("worker", "fsdp", None),
    )
    return jax.shard_map(local, mesh=mesh, in_specs=in_specs, out_specs=out_specs, check_vma=False)
```

time: 46.6 us -> 38.1 us (0.82)
  waiting for transfers between devices: 10.1 us -> 4.3 us
  starting transfers between devices: 17.7 us -> 21.5 us
  Pallas kernels: 14.6 us -> 11.3 us
  local copies, waits for them, and re-layouts: 3.12 us -> 0.03 us
    ppermute x5 -> x4, waiting for transfers between devices: 5.98 us -> 0.25 us  [across_shards(): lax.ppermute(value, 'fsdp', [(i, i ^ distance) for i in range(shards)])]
    ppermute x11, starting transfers between devices: 8.52 us -> 12.4 us  [swap(): lax.ppermute(value, 'worker', [(i, i ^ flips[i % 2]) for i in range(worke...]
    pallas_call x12 -> x13, Pallas kernels: 14.6 us -> 11.3 us  [call(): pl.pallas_call(body, in_specs=[pl.BlockSpec(memory_space=s) for _, s in i...]
    unnamed x16 -> x12, local copies, waits for them, and re-layouts: 3.12 us -> 0.03 us
    ppermute x5 -> x4, starting transfers between devices: 9.21 us -> 9.11 us  [across_shards(): lax.ppermute(value, 'fsdp', [(i, i ^ distance) for i in range(shards)])]
  transfers between devices with their start and end apart: 16 -> 15, of which waited for: 5 -> 6; matrix products, arithmetic and copies ran while one was open for 0% -> 0% of each run, Pallas kernels for 26% -> 26%
where the time goes in v3:
time: 38.1 us; the launch traced here: 37.9 us
  starting transfers between devices  21.5 us (56%)
  Pallas kernels  11.3 us (30%)
  waiting for transfers between devices  4.3 us (11%)
  between operations  0.8 us (2%)
    ppermute x11, starting transfers between devices, swap(): lax.ppermute(value, 'worker', [(i, i ^ flips[i % 2]) for i in range(worke...  12.4 us
    pallas_call x13, Pallas kernels, call(): pl.pallas_call(body, in_specs=[pl.BlockSpec(memory_space=s) for _, s in i...  11.3 us
    ppermute x4, starting transfers between devices, across_shards(): lax.ppermute(value, 'fsdp', [(i, i ^ distance) for i in range(shards)])  9.11 us
    ppermute x11, waiting for transfers between devices, swap(): lax.ppermute(value, 'worker', [(i, i ^ flips[i % 2]) for i in range(worke...  4.05 us
  transfers between devices with their start and end apart: 15, of which 6 were waited for; matrix products, arithmetic and copies ran while one was open for 0% of the time, Pallas kernels for 26%

profile of v3, /device:TPU:0, one launch (start us, length us, event | category | flops | bytes accessed | tf_op | source)
XLA Modules:
  0.0 37.9 jit_solution(11783255669969733026)
XLA Ops:
  0.6 0.5 %collective-permute-start = (bf16[2048,512]{1,0:T(8,128)(2,1)}, bf16[2048,512]{1,0:T(8,128)(2,1)S(1)}, u32[]{:S(2)}, u32[]{:S(2)}) collective-permute-start(bf16[2048,512]{1,0:T(8,128)(2,1)} %bitcast.7), channel_id=1, source_target_pairs={{0,4},{4,0},{8,12},{12,8},{16,20},{20,16},{24,28},{28,24},{1,5},{5... | collective-permute-start | bytes 6291464 | tf_op jit(solution)/shard_map/ppermute | solution.py:266
  1.2 3.7 %collective-permute-start.1 = (bf16[64,512]{1,0:T(8,128)(2,1)}, bf16[64,512]{1,0:T(8,128)(2,1)S(1)}, u32[]{:S(2)}, u32[]{:S(2)}) collective-permute-start(bf16[64,512]{1,0:T(8,128)(2,1)} %refs_2_.3), channel_id=1, source_target_pairs={{0,2},{1,3},{2,0},{3,1},{4,6},{5,7},{6,4},{7,5},{8,10},{9,11},{10,... | collective-permute-start | bytes 196616 | tf_op jit(solution)/shard_map/ppermute | solution.py:269
  4.8 0.3 collective-permute-done.refs_1_
  5.2 1.4 %shard_map.101 = (bf16[256,512]{1,0:T(8,128)(2,1)S(1)}, f32[256,512]{1,0:T(8,128)S(1)}, bf16[512,512]{1,0:T(8,128)(2,1)S(1)}) custom-call(bf16[2048,512]{1,0:T(8,128)(2,1)} %bitcast.8, bf16[2048,512]{1,0:T(8,128)(2,1)S(1)} %collective-permute-done.refs_1_), custom_call_target="tpu_custom_call" | custom-call | flops 2969999872 | tf_op jit(solution)/shard_map/pallas_call | solution.py:59
  6.5 2.9 %collective-permute-start.4 = (bf16[256,512]{1,0:T(8,128)(2,1)S(1)}, bf16[256,512]{1,0:T(8,128)(2,1)S(1)}, u32[]{:S(2)}, u32[]{:S(2)}) collective-permute-start(bf16[256,512]{1,0:T(8,128)(2,1)S(1)} %get-tuple-element.49), channel_id=1, source_target_pairs={{0,8},{4,20},{8,0},{12,28},{16,24},{20,4},{24,16},{28,12},{1,9},{5... | collective-permute-start | bytes 786440 | tf_op jit(solution)/shard_map/ppermute | solution.py:266
  9.5 0.3 shard_map.102
  9.8 1.3 %collective-permute-start.3 = (bf16[256,512]{1,0:T(8,128)(2,1)S(1)}, bf16[256,512]{1,0:T(8,128)(2,1)S(1)}, u32[]{:S(2)}, u32[]{:S(2)}) collective-permute-start(bf16[256,512]{1,0:T(8,128)(2,1)S(1)} %get-tuple-element.48), channel_id=1, source_target_pairs={{0,8},{4,20},{8,0},{12,28},{16,24},{20,4},{24,16},{28,12},{1,9},{5... | collective-permute-start | bytes 786440 | tf_op jit(solution)/shard_map/ppermute | solution.py:266
  11.1 0.9 %collective-permute-start.2 = (bf16[128,512]{1,0:T(8,128)(2,1)S(1)}, bf16[128,512]{1,0:T(8,128)(2,1)S(1)}, u32[]{:S(2)}, u32[]{:S(2)}) collective-permute-start(bf16[128,512]{1,0:T(8,128)(2,1)S(1)} %get-tuple-element.46.refs_5_), channel_id=1, source_target_pairs={{0,1},{1,0},{2,3},{3,2},{4,5},{5,4},{6,7},{7,6},{8,9},{9,8},{10,11... | collective-permute-start | bytes 393224 | tf_op jit(solution)/shard_map/ppermute | solution.py:269
  12.0 1.8 %collective-permute-done.4.refs_1_ = bf16[256,512]{1,0:T(8,128)(2,1)S(1)} collective-permute-done((bf16[256,512]{1,0:T(8,128)(2,1)S(1)}, bf16[256,512]{1,0:T(8,128)(2,1)S(1)}, u32[]{:S(2)}, u32[]{:S(2)}) %collective-permute-start.4) | collective-permute-done | bytes 262176 | tf_op jit(solution)/shard_map/ppermute | solution.py:266
  13.8 0.4 %shard_map.103 = (f32[256,512]{1,0:T(8,128)S(1)}, bf16[256,512]{1,0:T(8,128)(2,1)S(1)}) custom-call(f32[256,512]{1,0:T(8,128)S(1)} %get-tuple-element.45.refs_4_.refs_0_, bf16[256,512]{1,0:T(8,128)(2,1)S(1)} %collective-permute-done.4.refs_1_), custom_call_target="tpu_custom_call" | custom-call | flops 1650000000 | tf_op jit(solution)/shard_map/pallas_call | solution.py:59
  14.2 2.1 %collective-permute-start.5 = (bf16[256,512]{1,0:T(8,128)(2,1)S(1)}, bf16[256,512]{1,0:T(8,128)(2,1)S(1)}, u32[]{:S(2)}, u32[]{:S(2)}) collective-permute-start(bf16[256,512]{1,0:T(8,128)(2,1)S(1)} %get-tuple-element.54), channel_id=1, source_target_pairs={{0,16},{4,12},{8,24},{12,4},{16,0},{20,28},{24,8},{28,20},{1,17},{... | collective-permute-start | bytes 786440 | tf_op jit(solution)/shard_map/ppermute | solution.py:266
  16.4 0.3 collective-permute-done.3.refs_1_
  16.7 0.4 %shard_map.104 = (f32[256,512]{1,0:T(8,128)S(1)}, bf16[256,512]{1,0:T(8,128)(2,1)S(1)}) custom-call(f32[256,512]{1,0:T(8,128)S(1)} %get-tuple-element.47.refs_0_, bf16[256,512]{1,0:T(8,128)(2,1)S(1)} %collective-permute-done.3.refs_1_, f32[256,512]{1,0:T(8,128)S(1)} %get-tuple-element.50.refs_2_.refs_0_), custom_call_target="tpu_custom_call" | custom-call | flops 1650000000 | tf_op jit(solution)/shard_map/pallas_call | solution.py:59
  17.1 2.4 %collective-permute-start.7 = (bf16[256,512]{1,0:T(8,128)(2,1)S(1)}, bf16[256,512]{1,0:T(8,128)(2,1)S(1)}, u32[]{:S(2)}, u32[]{:S(2)}) collective-permute-start(bf16[256,512]{1,0:T(8,128)(2,1)S(1)} %get-tuple-element.57), channel_id=1, source_target_pairs={{0,16},{4,12},{8,24},{12,4},{16,0},{20,28},{24,8},{28,20},{1,17},{... | collective-permute-start | bytes 786440 | tf_op jit(solution)/shard_map/ppermute | solution.py:266
  19.5 0.7 %shard_map.108 = (f32[128,512]{1,0:T(8,128)S(1)}, f32[64,512]{1,0:T(8,128)S(1)}, f32[64,512]{1,0:T(8,128)S(1)}) custom-call(bf16[256,2048]{1,0:T(8,128)(2,1)S(1)} %copy-done.3, bf16[2048,512]{1,0:T(8,128)(2,1)S(1)} %bitcast.4, f32[256,512]{1,0:T(8,128)S(1)} %get-tuple-element.51.refs_7_.refs_0_.refs_2_.refs_3_), custom_call_target="tpu_custom_call" | custom-call | flops 330000000 | tf_op jit(solution)/shard_map/pallas_call | solution.py:59
  20.3 1.6 %collective-permute-start.11 = (f32[128,512]{1,0:T(8,128)S(1)}, f32[128,512]{1,0:T(8,128)S(1)}, u32[]{:S(2)}, u32[]{:S(2)}) collective-permute-start(f32[128,512]{1,0:T(8,128)S(1)} %get-tuple-element.63), channel_id=1, source_target_pairs={{0,1},{1,0},{2,3},{3,2},{4,5},{5,4},{6,7},{7,6},{8,9},{9,8},{10,11... | collective-permute-start | bytes 786440 | tf_op jit(solution)/shard_map/ppermute | solution.py:269
  22.0 1.2 %shard_map.105 = (bf16[4,256,512]{2,1,0:T(8,128)(2,1)S(1)}, bf16[4,256,256]{2,1,0:T(8,128)(2,1)S(1)}, f32[256,512]{1,0:T(8,128)S(1)}, f32[256,512]{1,0:T(8,128)S...) custom-call(bf16[256,2048]{1,0:T(8,128)(2,1)S(1)} %copy-done.3, bf16[2048,512]{1,0:T(8,128)(2,1)S(1)} %bitcast.5, ...), custom_call_target="tpu_custom_call" | custom-call | flops 1650000000 | tf_op jit(solution)/shard_map/pallas_call | solution.py:59
  23.2 0.4 %shard_map.106 = (f32[256,512]{1,0:T(8,128)S(1)}, bf16[256,512]{1,0:T(8,128)(2,1)S(1)}) custom-call(f32[256,512]{1,0:T(8,128)S(1)} %get-tuple-element.50.refs_2_.refs_0_, bf16[256,512]{1,0:T(8,128)(2,1)S(1)} %collective-permute-done.5.refs_1_, f32[256,512]{1,0:T(8,128)S(1)} %get-tuple-element.55.refs_2_.refs_0_), custom_call_target="tpu_custom_call" | custom-call | flops 1650000000 | tf_op jit(solution)/shard_map/pallas_call | solution.py:59
  23.6 0.3 collective-permute-done.7.refs_1_
  23.9 0.4 %shard_map.107 = (f32[256,512]{1,0:T(8,128)S(1)}, bf16[256,512]{1,0:T(8,128)(2,1)S(1)}) custom-call(f32[256,512]{1,0:T(8,128)S(1)} %get-tuple-element.51.refs_7_.refs_0_.refs_2_.refs_3_, bf16[256,512]{1,0:T(8,128)(2,1)S(1)} %collective-permute-done.7.refs_1_, f32[256,512]{1,0:T(8,128)S(1)} %get-tuple-element.58.refs_2_.refs_7_), custom_call_target="tpu_custom_call" | custom-call | flops 1650000000 | tf_op jit(solution)/shard_map/pallas_call | solution.py:59
  24.3 0.1 collective-permute-start.10
  24.4 0.5 %collective-permute-start.9 = (bf16[256,512]{1,0:T(8,128)(2,1)S(1)}, bf16[256,512]{1,0:T(8,128)(2,1)S(1)}, u32[]{:S(2)}, u32[]{:S(2)}) collective-permute-start(bf16[256,512]{1,0:T(8,128)(2,1)S(1)} %get-tuple-element.56), channel_id=1, source_target_pairs={{0,4},{4,0},{8,12},{12,8},{16,20},{20,16},{24,28},{28,24},{1,5},{5... | collective-permute-start | bytes 786440 | tf_op jit(solution)/shard_map/ppermute | solution.py:266
  24.9 2.0 %collective-permute-start.8 = (bf16[256,512]{1,0:T(8,128)(2,1)S(1)}, bf16[256,512]{1,0:T(8,128)(2,1)S(1)}, u32[]{:S(2)}, u32[]{:S(2)}) collective-permute-start(bf16[256,512]{1,0:T(8,128)(2,1)S(1)} %get-tuple-element.59), channel_id=1, source_target_pairs={{0,8},{4,20},{8,0},{12,28},{16,24},{20,4},{24,16},{28,12},{1,9},{5... | collective-permute-start | bytes 786440 | tf_op jit(solution)/shard_map/ppermute | solution.py:266
  26.9 0.0 collective-permute-start.6
  26.9 0.2 collective-permute-done.11.refs_0_
  27.2 2.9 %collective-permute-start.14 = (f32[64,512]{1,0:T(8,128)S(1)}, f32[64,512]{1,0:T(8,128)S(1)}, u32[]{:S(2)}, u32[]{:S(2)}) collective-permute-start(f32[64,512]{1,0:T(8,128)S(1)} %get-tuple-element.70), channel_id=1, source_target_pairs={{0,2},{1,3},{2,0},{3,1},{4,6},{5,7},{6,4},{7,5},{8,10},{9,11},{10,... | collective-permute-start | bytes 393224 | tf_op jit(solution)/shard_map/ppermute | solution.py:269
  30.1 2.7 %shard_map.110 = (bf16[2048,512]{1,0:T(8,128)(2,1)}, bf16[256,2048]{1,0:T(8,128)(2,1)}, bf16[4,256,512]{2,1,0:T(8,128)(2,1)S(1)}, bf16[4,256,256]{2,1,0:T(8,128)...) custom-call(bf16[256,2048]{1,0:T(8,128)(2,1)S(1)} %copy-done.3, bf16[2048,512]{1,0:T(8,128)(2,1)S(1)} %bitcast.6, ...), custom_call_target="tpu_custom_call" | custom-call | flops 9900000256 | tf_op jit(solution)/shard_map/pallas_call | solution.py:59
  32.8 1.3 %collective-permute-done.6.refs_0_.refs_2_ = bf16[256,512]{1,0:T(8,128)(2,1)S(1)} collective-permute-done((bf16[256,512]{1,0:T(8,128)(2,1)S(1)}, bf16[256,512]{1,0:T(8,128)(2,1)S(1)}, u32[]{:S(2)}, u32[]{:S(2)}) %collective-permute-start.6) | collective-permute-done | bytes 262176 | tf_op jit(solution)/shard_map/ppermute | solution.py:266
  34.1 0.1 collective-permute-start.12
  34.2 0.5 %collective-permute-start.13 = (bf16[256,512]{1,0:T(8,128)(2,1)S(1)}, bf16[256,512]{1,0:T(8,128)(2,1)S(1)}, u32[]{:S(2)}, u32[]{:S(2)}) collective-permute-start(bf16[256,512]{1,0:T(8,128)(2,1)S(1)} %get-tuple-element.69), channel_id=1, source_target_pairs={{0,4},{4,0},{8,12},{12,8},{16,20},{20,16},{24,28},{28,24},{1,5},{5... | collective-permute-start | bytes 786440 | tf_op jit(solution)/shard_map/ppermute | solution.py:266
  34.7 2.0 %shard_map.112 = (bf16[2048,512]{1,0:T(8,128)(2,1)}, bf16[256,2048]{1,0:T(8,128)(2,1)}, bf16[2048,512]{1,0:T(8,128)(2,1)}, f32[256,512]{1,0:T(8,128)}) custom-call(f32[256,512]{1,0:T(8,128)S(1)} %get-tuple-element.55.refs_2_.refs_0_, f32[256,512]{1,0:T(8,128)S(1)} %get-tuple-element.71.refs_1_, ...), custom_call_target="tpu_custom_call", output_to_operand_aliasing={{0}: (8, {}), {1}: (9, {})} | custom-call | flops 26400000000 | tf_op jit(solution)/shard_map/pallas_call | solution.py:59
  36.7 1.2 %shard_map.113 = (bf16[2048,512]{1,0:T(8,128)(2,1)}, bf16[64,512]{1,0:T(8,128)(2,1)}) custom-call(f32[256,512]{1,0:T(8,128)S(1)} %get-tuple-element.52.refs_0_, f32[256,512]{1,0:T(8,128)S(1)} %get-tuple-element.53.refs_1_, bf16[256,512]{1,0:T(8,128)(2,1)S(1)} %collective-permute-done.12.refs_2_, ...), custom_call_target="tpu_custom_call", output_to_operand_aliasing={{0}: (6, {})} | custom-call | flops 26400000000 | tf_op jit(solution)/shard_map/pallas_call | solution.py:59
  (23 shorter events, 0.1 us)
Async XLA Ops:
  0.6 8.8 %copy-start.5 = (bf16[64,512]{1,0:T(8,128)(2,1)S(1)}, bf16[64,512]{1,0:T(8,128)(2,1)}, u32[]{:S(2)}) copy-start(bf16[64,512]{1,0:T(8,128)(2,1)} %refs_2_.3) | copy-start | bytes 196612
  0.6 4.5 %collective-permute-start = (bf16[2048,512]{1,0:T(8,128)(2,1)}, bf16[2048,512]{1,0:T(8,128)(2,1)S(1)}, u32[]{:S(2)}, u32[]{:S(2)}) collective-permute-start(bf16[2048,512]{1,0:T(8,128)(2,1)} %bitcast.7), channel_id=1, source_target_pairs={{0,4},{4,0},{8,12},{12,8},{16,20},{20,16},{24,28},{28,24},{1,5},{5... | collective-permute-start | bytes 6291464 | tf_op jit(solution)/shard_map/ppermute | solution.py:266
  1.2 8.3 %collective-permute-start.1 = (bf16[64,512]{1,0:T(8,128)(2,1)}, bf16[64,512]{1,0:T(8,128)(2,1)S(1)}, u32[]{:S(2)}, u32[]{:S(2)}) collective-permute-start(bf16[64,512]{1,0:T(8,128)(2,1)} %refs_2_.3), channel_id=1, source_target_pairs={{0,2},{1,3},{2,0},{3,1},{4,6},{5,7},{6,4},{7,5},{8,10},{9,11},{10,... | collective-permute-start | bytes 196616 | tf_op jit(solution)/shard_map/ppermute | solution.py:269
  6.5 7.3 %collective-permute-start.4 = (bf16[256,512]{1,0:T(8,128)(2,1)S(1)}, bf16[256,512]{1,0:T(8,128)(2,1)S(1)}, u32[]{:S(2)}, u32[]{:S(2)}) collective-permute-start(bf16[256,512]{1,0:T(8,128)(2,1)S(1)} %get-tuple-element.49), channel_id=1, source_target_pairs={{0,8},{4,20},{8,0},{12,28},{16,24},{20,4},{24,16},{28,12},{1,9},{5... | collective-permute-start | bytes 786440 | tf_op jit(solution)/shard_map/ppermute | solution.py:266
  9.8 6.9 %collective-permute-start.3 = (bf16[256,512]{1,0:T(8,128)(2,1)S(1)}, bf16[256,512]{1,0:T(8,128)(2,1)S(1)}, u32[]{:S(2)}, u32[]{:S(2)}) collective-permute-start(bf16[256,512]{1,0:T(8,128)(2,1)S(1)} %get-tuple-element.48), channel_id=1, source_target_pairs={{0,8},{4,20},{8,0},{12,28},{16,24},{20,4},{24,16},{28,12},{1,9},{5... | collective-permute-start | bytes 786440 | tf_op jit(solution)/shard_map/ppermute | solution.py:266
  11.1 10.9 %collective-permute-start.2 = (bf16[128,512]{1,0:T(8,128)(2,1)S(1)}, bf16[128,512]{1,0:T(8,128)(2,1)S(1)}, u32[]{:S(2)}, u32[]{:S(2)}) collective-permute-start(bf16[128,512]{1,0:T(8,128)(2,1)S(1)} %get-tuple-element.46.refs_5_), channel_id=1, source_target_pairs={{0,1},{1,0},{2,3},{3,2},{4,5},{5,4},{6,7},{7,6},{8,9},{9,8},{10,11... | collective-permute-start | bytes 393224 | tf_op jit(solution)/shard_map/ppermute | solution.py:269
  13.8 5.7 %copy-start.3 = (bf16[256,2048]{1,0:T(8,128)(2,1)S(1)}, bf16[256,2048]{1,0:T(8,128)(2,1)}, u32[]{:S(2)}) copy-start(bf16[256,2048]{1,0:T(8,128)(2,1)} %refs_0_.5) | copy-start | bytes 3145732
  13.8 8.1 %copy-start.2 = (f32[2048,512]{1,0:T(8,128)S(1)}, f32[2048,512]{1,0:T(8,128)}, u32[]{:S(2)}) copy-start(f32[2048,512]{1,0:T(8,128)} %refs_3_.3) | copy-start | bytes 12582916
  14.2 8.9 %collective-permute-start.5 = (bf16[256,512]{1,0:T(8,128)(2,1)S(1)}, bf16[256,512]{1,0:T(8,128)(2,1)S(1)}, u32[]{:S(2)}, u32[]{:S(2)}) collective-permute-start(bf16[256,512]{1,0:T(8,128)(2,1)S(1)} %get-tuple-element.54), channel_id=1, source_target_pairs={{0,16},{4,12},{8,24},{12,4},{16,0},{20,28},{24,8},{28,20},{1,17},{... | collective-permute-start | bytes 786440 | tf_op jit(solution)/shard_map/ppermute | solution.py:266
  16.7 2.9 %copy-start = (bf16[1,2048,512]{2,1,0:T(8,128)(2,1)S(1)}, bf16[1,2048,512]{2,1,0:T(8,128)(2,1)}, u32[]{:S(2)}) copy-start(bf16[1,2048,512]{2,1,0:T(8,128)(2,1)} %param.7) | copy-start | bytes 6291460
  16.7 5.3 %copy-start.1 = (f32[2048,512]{1,0:T(8,128)S(1)}, f32[2048,512]{1,0:T(8,128)}, u32[]{:S(2)}) copy-start(f32[2048,512]{1,0:T(8,128)} %refs_2_.5) | copy-start | bytes 12582916
  17.1 4.8 %copy-start.4 = (bf16[1,2048,512]{2,1,0:T(8,128)(2,1)S(1)}, bf16[1,2048,512]{2,1,0:T(8,128)(2,1)}, u32[]{:S(2)}) copy-start(bf16[1,2048,512]{2,1,0:T(8,128)(2,1)} %param.11) | copy-start | bytes 6291460
  17.1 6.8 %collective-permute-start.7 = (bf16[256,512]{1,0:T(8,128)(2,1)S(1)}, bf16[256,512]{1,0:T(8,128)(2,1)S(1)}, u32[]{:S(2)}, u32[]{:S(2)}) collective-permute-start(bf16[256,512]{1,0:T(8,128)(2,1)S(1)} %get-tuple-element.57), channel_id=1, source_target_pairs={{0,16},{4,12},{8,24},{12,4},{16,0},{20,28},{24,8},{28,20},{1,17},{... | collective-permute-start | bytes 786440 | tf_op jit(solution)/shard_map/ppermute | solution.py:266
  20.3 6.9 %collective-permute-start.11 = (f32[128,512]{1,0:T(8,128)S(1)}, f32[128,512]{1,0:T(8,128)S(1)}, u32[]{:S(2)}, u32[]{:S(2)}) collective-permute-start(f32[128,512]{1,0:T(8,128)S(1)} %get-tuple-element.63), channel_id=1, source_target_pairs={{0,1},{1,0},{2,3},{3,2},{4,5},{5,4},{6,7},{7,6},{8,9},{9,8},{10,11... | collective-permute-start | bytes 786440 | tf_op jit(solution)/shard_map/ppermute | solution.py:269
  24.3 5.8 %collective-permute-start.10 = (bf16[256,512]{1,0:T(8,128)(2,1)S(1)}, bf16[256,512]{1,0:T(8,128)(2,1)S(1)}, u32[]{:S(2)}, u32[]{:S(2)}) collective-permute-start(bf16[256,512]{1,0:T(8,128)(2,1)S(1)} %get-tuple-element.59), channel_id=1, source_target_pairs={{0,4},{4,0},{8,12},{12,8},{16,20},{20,16},{24,28},{28,24},{1,5},{5... | collective-permute-start | bytes 786440 | tf_op jit(solution)/shard_map/ppermute | solution.py:266
  24.4 5.7 %collective-permute-start.9 = (bf16[256,512]{1,0:T(8,128)(2,1)S(1)}, bf16[256,512]{1,0:T(8,128)(2,1)S(1)}, u32[]{:S(2)}, u32[]{:S(2)}) collective-permute-start(bf16[256,512]{1,0:T(8,128)(2,1)S(1)} %get-tuple-element.56), channel_id=1, source_target_pairs={{0,4},{4,0},{8,12},{12,8},{16,20},{20,16},{24,28},{28,24},{1,5},{5... | collective-permute-start | bytes 786440 | tf_op jit(solution)/shard_map/ppermute | solution.py:266
  24.9 7.9 %collective-permute-start.8 = (bf16[256,512]{1,0:T(8,128)(2,1)S(1)}, bf16[256,512]{1,0:T(8,128)(2,1)S(1)}, u32[]{:S(2)}, u32[]{:S(2)}) collective-permute-start(bf16[256,512]{1,0:T(8,128)(2,1)S(1)} %get-tuple-element.59), channel_id=1, source_target_pairs={{0,8},{4,20},{8,0},{12,28},{16,24},{20,4},{24,16},{28,12},{1,9},{5... | collective-permute-start | bytes 786440 | tf_op jit(solution)/shard_map/ppermute | solution.py:266
  26.9 7.2 %collective-permute-start.6 = (bf16[256,512]{1,0:T(8,128)(2,1)S(1)}, bf16[256,512]{1,0:T(8,128)(2,1)S(1)}, u32[]{:S(2)}, u32[]{:S(2)}) collective-permute-start(bf16[256,512]{1,0:T(8,128)(2,1)S(1)} %get-tuple-element.56), channel_id=1, source_target_pairs={{0,8},{4,20},{8,0},{12,28},{16,24},{20,4},{24,16},{28,12},{1,9},{5... | collective-permute-start | bytes 786440 | tf_op jit(solution)/shard_map/ppermute | solution.py:266
  27.2 9.4 %collective-permute-start.14 = (f32[64,512]{1,0:T(8,128)S(1)}, f32[64,512]{1,0:T(8,128)S(1)}, u32[]{:S(2)}, u32[]{:S(2)}) collective-permute-start(f32[64,512]{1,0:T(8,128)S(1)} %get-tuple-element.70), channel_id=1, source_target_pairs={{0,2},{1,3},{2,0},{3,1},{4,6},{5,7},{6,4},{7,5},{8,10},{9,11},{10,... | collective-permute-start | bytes 393224 | tf_op jit(solution)/shard_map/ppermute | solution.py:269
  34.1 2.5 %collective-permute-start.12 = (bf16[256,512]{1,0:T(8,128)(2,1)S(1)}, bf16[256,512]{1,0:T(8,128)(2,1)S(1)}, u32[]{:S(2)}, u32[]{:S(2)}) collective-permute-start(bf16[256,512]{1,0:T(8,128)(2,1)S(1)} %get-tuple-element.68), channel_id=1, source_target_pairs={{0,4},{4,0},{8,12},{12,8},{16,20},{20,16},{24,28},{28,24},{1,5},{5... | collective-permute-start | bytes 786440 | tf_op jit(solution)/shard_map/ppermute | solution.py:266
  34.2 2.5 %collective-permute-start.13 = (bf16[256,512]{1,0:T(8,128)(2,1)S(1)}, bf16[256,512]{1,0:T(8,128)(2,1)S(1)}, u32[]{:S(2)}, u32[]{:S(2)}) collective-permute-start(bf16[256,512]{1,0:T(8,128)(2,1)S(1)} %get-tuple-element.69), channel_id=1, source_target_pairs={{0,4},{4,0},{8,12},{12,8},{16,20},{20,16},{24,28},{28,24},{1,5},{5... | collective-permute-start | bytes 786440 | tf_op jit(solution)/shard_map/ppermute | solution.py:266

commit v4 on v3

v4 whole, which is shorter than its diff:
```python
import functools
import math

import jax
import jax.numpy as jnp
from jax import lax
from jax.experimental import pallas as pl
from jax.experimental.pallas import tpu as pltpu
from jax.sharding import PartitionSpec as P

inner_rate = 0.0005
outer_rate = 0.7
outer_momentum = 0.9

stale_bound = 0.29882812
floor = 2.0**-14
power = 250.0 / math.log2(1.0 + stale_bound / floor)


def encode(value, count):
    grown = jnp.log(jnp.abs(value) * (1.0 / (floor * count)) + 1.0)
    code = jnp.exp2(grown * (power / math.log(2.0)) - 125.0)
    return jnp.where(value < 0, -code, code).astype(jnp.bfloat16)


def decode(code, count):
    code = code.astype(jnp.float32)
    grown = jnp.exp2(jnp.log(jnp.abs(code)) * (1.0 / (power * math.log(2.0))) + 125.0 / power)
    value = (grown - 1.0) * (floor * count)
    return jnp.where(code < 0, -value, value)


pace = 3.3e9
cost = {"pair": (0.9, 0.9), "keys": 0.1, "add": (0.5, 0.5), "keys_add": 0.4, "fresh": 0.3, "update": (8.0, 8.0), "relay": 0.3, "fetch": 0.5}
opt = {"kg_gate": 0, "keys_gate": 2, "add_gate": 1}


def place(me):
    core, low, high = me % 2, (me // 2) % 2, me // 4
    return core, jnp.where(core == 0, low, high), jnp.where(core == 0, high, low)


def block(region, half, sub):
    return jnp.where(region == 0, 4 * sub + 2 * half, 4 * half + 2 * sub + 1)


SMEM, VMEM, HBM, ANY = pltpu.SMEM, pltpu.VMEM, pltpu.HBM, pl.ANY


def call(kernel, ins, outs, scratch=(), after=(), aliases=None, micros=1.0, vmem=12):
    late = len(after)

    def body(*refs):
        kernel(*refs[: len(ins)], *refs[len(ins) + late :])

    def placed(array, space):
        return pltpu.with_memory_space_constraint(array, space) if space in (HBM, VMEM) else array

    return pl.pallas_call(
        body,
        in_specs=[pl.BlockSpec(memory_space=s) for _, s in ins] + [pl.BlockSpec(memory_space=ANY)] * late,
        out_specs=[pl.BlockSpec(memory_space=s) for _, _, s in outs],
        out_shape=[s(shape, dtype) for shape, dtype, s in outs],
        scratch_shapes=scratch,
        input_output_aliases=aliases or {},
        cost_estimate=pl.CostEstimate(flops=int(micros * pace), bytes_accessed=0, transcendentals=0),
        compiler_params=pltpu.CompilerParams(vmem_limit_bytes=vmem * 2**20),
    )(*[placed(a, s) for a, s in ins], *after)


def rows(ref, at, size):
    return ref.at[pl.ds(pl.multiple_of(at * size, size), size), :]


def pair_sums(size, own, other, places, code, keep):
    step = 64

    def summed(k, at):
        there = pl.ds(pl.multiple_of(places[k] * size + at, step), step)
        return own[k * size + at : k * size + at + step, :].astype(jnp.float32) + other[there, :].astype(jnp.float32)

    for at in range(0, size, step):
        code[at : at + step, :] = encode(summed(0, at), 2)
        keep[at : at + step, :] = summed(1, at)


def fetch_kernel(size, stale, grad, first_own, second_own, grad_out, sem):
    core, first, _ = place(lax.axis_index("worker"))
    copies = [
        pltpu.make_async_copy(
            rows(stale, block(core, half, sub), size), own.at[k * size : (k + 1) * size, :], sem.at[2 * sub + k]
        )
        for sub, own in enumerate((first_own, second_own))
        for k, half in enumerate((1 - first, first))
    ]
    copies.append(pltpu.make_async_copy(grad, grad_out, sem.at[4]))
    for copy in copies:
        copy.start()
    for copy in copies:
        copy.wait()


def pair_kernel(size, sub, own, other, code, keep):
    core, first, _ = place(lax.axis_index("worker"))
    places = [block(core, half, sub) for half in (1 - first, first)]
    pair_sums(size, own, other, places, code, keep)


def add_kernel(held, total, value, received, out, code):
    summed = value[...] + decode(received[...], held)
    out[...] = summed
    code[...] = encode(summed, total)


def keys_kernel(tokens, weights, grad, grad_far, packed, own, later, total):
    total[...] = jnp.dot(tokens[...], weights[...], preferred_element_type=jnp.float32)
    size = own.shape[0]
    shard = lax.axis_index("fsdp")
    packed[:size, :] = grad[...]
    packed[size : 2 * size, :] = grad_far[...]
    for k, d in enumerate((1, 3)):
        value = rows(total, shard ^ d, size)[...]
        high = value.astype(jnp.bfloat16)
        packed[(2 + k) * size : (3 + k) * size, :] = high
        packed[(4 + k) * size : (5 + k) * size, :] = (value - high.astype(jnp.float32)).astype(jnp.bfloat16)
    own[...] = rows(total, shard, size)[...]
    later[...] = rows(total, shard ^ 2, size)[...]


def keys_add_kernel(received, own, later, own_out, later_out):
    size = own.shape[0]

    def arrived(k):
        high, low = (received[at * size : (at + 1) * size, :].astype(jnp.float32) for at in (2 + k, 4 + k))
        return high + low

    own_out[...] = own[...] + arrived(0)
    later_out[...] = later[...] + arrived(1)


def relay_kernel(*refs):
    half = len(refs) // 2
    for source, target in zip(refs[:half], refs[half:], strict=True):
        target[...] = source[...]


def spots(me):
    core, first, last = place(me)
    return {
        "own": (core, first),
        "near": (core, 1 - first),
        "across": (1 - core, last),
        "far": (1 - core, 1 - last),
    }


def span_of(size, kind, sub):
    return pl.ds(pl.multiple_of(block(*spots(lax.axis_index("worker"))[kind], sub) * size, size), size)


def fresh_kernel(workers, soon, late, tokens, weights, anchor, momentum, stale, near, far, *rest):
    sums, rest = rest[: len(soon)], rest[len(soon) :]
    fresh_out, grad_out, param_out, moment_out, rest = *rest[:4], rest[4:]
    bases, rest = rest[: len(late)], rest[len(late) :]
    fresh_buf, grad_buf, param_buf, moment, portion, sem = rest
    size = weights.shape[0] // workers
    copies = []

    def send(source, target):
        copies.append(pltpu.make_async_copy(source, target, sem.at[len(copies)]))
        copies[-1].start()

    held = portion.shape[0] // 4
    shard = lax.axis_index("fsdp")
    for d, source, k in ((0, near, 0), (2, near, 1), (1, far, 0), (3, far, 1)):
        rows(portion, shard ^ d, held)[...] = source[k * held : (k + 1) * held, :]
    for k, which in enumerate([*late, *soon]):
        span = span_of(size, *which)
        weight = weights[span, :]
        grad_weight = lax.dot_general(
            tokens[:, span], portion[...], (((0,), (0,)), ((), ())), preferred_element_type=jnp.float32
        )
        grad_buf[k] = lax.dot_general(
            portion[...], weight, (((1,), (1,)), ((), ())), preferred_element_type=jnp.float32
        ).astype(jnp.bfloat16)
        send(grad_buf.at[k], grad_out.at[:, span])
        value = anchor[span, :]
        fresh = value - (weight.astype(jnp.float32) - inner_rate * grad_weight)
        fresh_buf[k] = fresh.astype(jnp.bfloat16)
        send(fresh_buf.at[k], fresh_out.at[span, :])
        base = value - outer_rate * (
            outer_momentum * outer_momentum * momentum[span, :]
            + (fresh - stale[span, :].astype(jnp.float32)) / workers
        )
        if k < len(late):
            bases[k][...] = base
        else:
            k -= len(late)
            param_buf[k] = finished(which[0], workers, base, sums[k])
            send(param_buf.at[k], param_out.at[span, :])
        if which is late[-1]:
            _, _, last = place(lax.axis_index("worker"))
            average = jnp.where(last == 0, sums[0][...], sums[1][...]) / workers
            moment[...] = outer_momentum * rows(momentum, lax.axis_index("worker"), size)[...] + average
            send(moment, moment_out)
    for copy in copies:
        copy.wait()


def finished(kind, workers, base, piece):
    total = piece[...]
    if kind != "own":
        total = decode(total, workers)
    return (base - (outer_rate * (1.0 + outer_momentum) / workers) * total).astype(jnp.bfloat16)


def update_kernel(workers, kinds, keys, *rest):
    count = len(kinds)
    bases, pieces, rest = rest[:count], rest[count : 2 * count], rest[2 * count :]
    if keys:
        own, received, _, out, key_out, out_buf, key_buf, sem = rest
    else:
        _, out, out_buf, sem = rest
    size = out.shape[0] // workers
    copies = []
    if keys:
        key_buf[...] = (own[...] + received[...]).astype(jnp.bfloat16)
        copies.append(pltpu.make_async_copy(key_buf, key_out, sem.at[count]))
        copies[0].start()
    for k, which in enumerate(kinds):
        out_buf[k] = finished(which[0], workers, bases[k][...], pieces[k])
        copies.append(pltpu.make_async_copy(out_buf.at[k], out.at[span_of(size, *which), :], sem.at[k]))
        copies[-1].start()
    for copy in copies:
        copy.wait()


def fast(tokens, inner_weight, key_grad, anchor, momentum, stale_delta):
    workers, shards = lax.axis_size("worker"), lax.axis_size("fsdp")
    f32, bf16 = jnp.float32, jnp.bfloat16
    DMA = pltpu.SemaphoreType.DMA
    weights, stale = inner_weight[0], stale_delta[0]
    height, columns = stale.shape
    batch = tokens.shape[0]
    size = height // workers
    window = (size, columns)

    def swap(value, flips):
        return lax.ppermute(value, "worker", [(i, i ^ flips[i % 2]) for i in range(workers)])

    def across_shards(value, distance):
        return lax.ppermute(value, "fsdp", [(i, i ^ distance) for i in range(shards)])

    beside, first, last = (1, 1), (2, 4), (4, 2)
    chunks = range(2)

    key_rows = batch // shards
    other = swap(stale, beside)
    block_of_keys = (key_rows, columns)
    *owns, grad = call(
        functools.partial(fetch_kernel, size),
        [(stale, HBM), (key_grad, HBM)],
        [((2 * size, columns), bf16, VMEM)] * 2 + [(key_grad.shape, bf16, VMEM)],
        scratch=[DMA((5,))],
        micros=cost["fetch"],
    )
    grad_far = across_shards(grad, 2)

    codes, keeps = [], []
    for c in chunks:
        code, keep = call(
            functools.partial(pair_kernel, size, c),
            [(owns[c], VMEM), (other, VMEM)],
            [(window, bf16, VMEM), (window, f32, VMEM)],
            after=keeps + [grad_far] * (c == 1 and opt["kg_gate"]),
            micros=cost["pair"][c],
        )
        codes.append(code)
        keeps.append(keep)
    got = [swap(codes[c], first) for c in chunks]

    packed, own_keys, later_keys = call(
        keys_kernel,
        [(tokens, VMEM), (weights, VMEM), (grad, VMEM), (grad_far, VMEM)],
        [((6 * key_rows, columns), bf16, VMEM), (block_of_keys, f32, VMEM), (block_of_keys, f32, VMEM)],
        scratch=[pltpu.VMEM((batch, columns), f32)],
        after=[keeps[1]],
        micros=cost["keys"],
    )
    arrived = across_shards(packed, 1)
    grads = [packed, arrived]

    def added(held, total, gates):
        for c in chunks:
            keeps[c], codes[c] = call(
                functools.partial(add_kernel, held, total),
                [(keeps[c], VMEM), (got[c], VMEM)],
                [(window, f32, VMEM), (window, bf16, VMEM)],
                after=gates[c] if c == 0 else [keeps[0], *gates[c]],
                micros=cost["add"][c],
            )

    late_kinds = [("near", 0), ("far", 0), ("near", 1), ("far", 1)]
    gates = [[], []]
    if opt["keys_gate"]:
        gates[opt["keys_gate"] - 1].append(packed)
    added(2, 4, gates)
    got = [swap(codes[c], last) for c in chunks]
    own_keys, later_keys = call(
        keys_add_kernel,
        [(arrived, VMEM), (own_keys, VMEM), (later_keys, VMEM)],
        [(block_of_keys, f32, VMEM), (block_of_keys, f32, VMEM)],
        after=[keeps[1]],
        micros=cost["keys_add"],
    )
    key_far = across_shards(later_keys, 2)
    gates = [[], []]
    if opt["add_gate"] in (1, 2):
        gates[opt["add_gate"] - 1].append(own_keys)
    added(4, 8, gates)
    near = [swap(codes[c], first) for c in chunks]
    across = [swap(codes[c], beside) for c in chunks]
    soon_kinds = [("own", 0), ("own", 1), ("across", 0), ("across", 1)]
    late_kinds = [("near", 0), ("near", 1), ("far", 0), ("far", 1)]
    n = len(soon_kinds)
    ins = [tokens, weights, anchor, momentum, stale, packed, arrived, *keeps, *across]
    fresh_out, grad_input, updated, new_moment, *bases = call(
        functools.partial(fresh_kernel, workers, soon_kinds, late_kinds),
        [(value, VMEM) for value in ins],
        [
            ((height, columns), bf16, HBM),
            ((batch, height), bf16, HBM),
            ((height, columns), bf16, HBM),
            (window, f32, HBM),
        ]
        + [(window, f32, VMEM)] * n,
        scratch=[
            pltpu.VMEM((2 * n, *window), bf16),
            pltpu.VMEM((2 * n, batch, size), bf16),
            pltpu.VMEM((n, *window), bf16),
            pltpu.VMEM(window, f32),
            pltpu.VMEM((batch, columns), bf16),
            DMA((5 * n + 1,)),
        ],
        after=[own_keys] if opt["add_gate"] == 3 else [],
        micros=cost["fresh"],
    )
    relayed = call(
        relay_kernel, [(v, VMEM) for v in near], [(window, bf16, VMEM)] * 2, after=[bases[0]], micros=cost["relay"]
    )
    far = [swap(v, beside) for v in relayed]

    pieces = [*near, *far]
    for which, with_keys in (((0, 1), False), ((2, 3), True)):
        ins = [(bases[w], VMEM) for w in which] + [(pieces[w], VMEM) for w in which]
        outs = [((height, columns), bf16, HBM)]
        scratch = [pltpu.VMEM((len(which), *window), bf16)]
        if with_keys:
            ins += [(own_keys, VMEM), (key_far, VMEM)]
            outs.append(((key_rows, columns), bf16, HBM))
            scratch.append(pltpu.VMEM((key_rows, columns), bf16))
        ins.append((updated, HBM))
        updated, *key_out = call(
            functools.partial(update_kernel, workers, [late_kinds[w] for w in which], with_keys),
            ins,
            outs,
            scratch=[*scratch, DMA((len(which) + 1,))],
            aliases={len(ins) - 1: 0},
            micros=cost["update"][with_keys],
        )
    return key_out[0], grad_input, updated[None], new_moment, fresh_out[None]


def plain(tokens, inner_weight, key_grad, anchor, momentum, stale_delta):
    weights = inner_weight[0]
    key_out = lax.psum_scatter(
        jnp.dot(tokens, weights, preferred_element_type=jnp.float32), "fsdp", scatter_dimension=0, tiled=True
    ).astype(jnp.bfloat16)
    portion = lax.all_gather(key_grad, "fsdp", axis=0, tiled=True)
    grad_weight = lax.dot_general(tokens, portion, (((0,), (0,)), ((), ())), preferred_element_type=jnp.float32)
    grad_input = lax.dot_general(portion, weights, (((1,), (1,)), ((), ())), preferred_element_type=jnp.float32)
    fresh_term = anchor - (weights.astype(jnp.float32) - inner_rate * grad_weight)
    stale_value = stale_delta[0].astype(jnp.float32)
    workers = lax.axis_size("worker")
    average = lax.psum(stale_value, "worker") / workers
    moment_full = outer_momentum * momentum + average
    common_term = average + outer_momentum * moment_full
    share_rows = anchor.shape[0] // workers
    new_moment = lax.dynamic_slice_in_dim(moment_full, lax.axis_index("worker") * share_rows, share_rows, 0)
    updated = anchor - outer_rate * (common_term + (fresh_term - stale_value) / workers)
    return (
        key_out,
        grad_input.astype(jnp.bfloat16),
        updated[None].astype(jnp.bfloat16),
        new_moment,
        fresh_term[None].astype(jnp.bfloat16),
    )


def local(*args):
    tokens, inner_weight = args[:2]
    workers, shards = lax.axis_size("worker"), lax.axis_size("fsdp")
    size = inner_weight.shape[1] // workers
    fits = workers == 2**3 and shards == 2**2
    fits = fits and size % 128 == 0 and tokens.shape[0] // shards % 16 == 0
    return (fast if fits else plain)(*args)


def solution(mesh):
    in_specs = (
        P("worker", "fsdp"),
        P("worker", "fsdp", None),
        P(("worker", "fsdp"), None),
        P("fsdp", None),
        P("fsdp", None),
        P("worker", "fsdp", None),
    )
    out_specs = (
        P(("worker", "fsdp"), None),
        P("worker", "fsdp"),
        P("worker", "fsdp", None),
        P(("fsdp", "worker"), None),
        P("worker", "fsdp", None),
    )
    return jax.shard_map(local, mesh=mesh, in_specs=in_specs, out_specs=out_specs, check_vma=False)
```

time: 38.1 us -> 36.4 us (0.955)
  starting transfers between devices: 21.5 us -> 18.5 us
  waiting for transfers between devices: 4.3 us -> 6.11 us
  Pallas kernels: 11.3 us -> 10.8 us
    ppermute x4 -> x3, waiting for transfers between devices: 0.25 us -> 4.92 us  [across_shards(): lax.ppermute(value, 'fsdp', [(i, i ^ distance) for i in range(shards)])]
    ppermute x11, waiting for transfers between devices: 4.05 us -> 1.19 us  [swap(): lax.ppermute(value, 'worker', [(i, i ^ flips[i % 2]) for i in range(worke...]
    ppermute x11, starting transfers between devices: 12.4 us -> 10.1 us  [swap(): lax.ppermute(value, 'worker', [(i, i ^ flips[i % 2]) for i in range(worke...]
    ppermute x4 -> x3, starting transfers between devices: 9.11 us -> 8.41 us  [across_shards(): lax.ppermute(value, 'fsdp', [(i, i ^ distance) for i in range(shards)])]
    pallas_call x13, Pallas kernels: 11.3 us -> 10.8 us  [call(): pl.pallas_call(body, in_specs=[pl.BlockSpec(memory_space=s) for _, s in i...]
  transfers between devices with their start and end apart: 15 -> 14, of which waited for: 6 -> 8; matrix products, arithmetic and copies ran while one was open for 0% -> 0% of each run, Pallas kernels for 26% -> 25%
where the time goes in v4:
time: 36.4 us; the launch traced here: 36.3 us
  starting transfers between devices  18.5 us (51%)
  Pallas kernels  10.8 us (30%)
  waiting for transfers between devices  6.11 us (17%)
  between operations  0.78 us (2%)
    pallas_call x13, Pallas kernels, call(): pl.pallas_call(body, in_specs=[pl.BlockSpec(memory_space=s) for _, s in i...  10.8 us
    ppermute x11, starting transfers between devices, swap(): lax.ppermute(value, 'worker', [(i, i ^ flips[i % 2]) for i in range(worke...  10.1 us
    ppermute x3, starting transfers between devices, across_shards(): lax.ppermute(value, 'fsdp', [(i, i ^ distance) for i in range(shards)])  8.41 us
    ppermute x3, waiting for transfers between devices, across_shards(): lax.ppermute(value, 'fsdp', [(i, i ^ distance) for i in range(shards)])  4.92 us
    ppermute x11, waiting for transfers between devices, swap(): lax.ppermute(value, 'worker', [(i, i ^ flips[i % 2]) for i in range(worke...  1.19 us
  transfers between devices with their start and end apart: 14, of which 8 were waited for; matrix products, arithmetic and copies ran while one was open for 0% of the time, Pallas kernels for 25%

profile of v4, /device:TPU:0, one launch (start us, length us, event | category | flops | bytes accessed | tf_op | source)
XLA Modules:
  0.0 36.3 jit_solution(15534571603046114451)
XLA Ops:
  0.6 0.5 %collective-permute-start.1 = (bf16[2048,512]{1,0:T(8,128)(2,1)}, bf16[2048,512]{1,0:T(8,128)(2,1)S(1)}, u32[]{:S(2)}, u32[]{:S(2)}) collective-permute-start(bf16[2048,512]{1,0:T(8,128)(2,1)} %bitcast.6), channel_id=1, source_target_pairs={{0,4},{4,0},{8,12},{12,8},{16,20},{20,16},{24,28},{28,24},{1,5},{5... | collective-permute-start | bytes 6291464 | tf_op jit(solution)/shard_map/ppermute | solution.py:249
  1.1 1.2 %shard_map.101 = (bf16[512,512]{1,0:T(8,128)(2,1)S(1)}, bf16[512,512]{1,0:T(8,128)(2,1)S(1)}, bf16[64,512]{1,0:T(8,128)(2,1)S(1)}) custom-call(bf16[2048,512]{1,0:T(8,128)(2,1)} %bitcast.7, bf16[64,512]{1,0:T(8,128)(2,1)} %refs_1_.1), custom_call_target="tpu_custom_call" | custom-call | flops 1650000000 | tf_op jit(solution)/shard_map/pallas_call | solution.py:59
  2.4 3.7 %collective-permute-start = (bf16[64,512]{1,0:T(8,128)(2,1)S(1)}, bf16[64,512]{1,0:T(8,128)(2,1)S(1)}, u32[]{:S(2)}, u32[]{:S(2)}) collective-permute-start(bf16[64,512]{1,0:T(8,128)(2,1)S(1)} %get-tuple-element.37.refs_2_), channel_id=1, source_target_pairs={{0,2},{1,3},{2,0},{3,1},{4,6},{5,7},{6,4},{7,5},{8,10},{9,11},{10,... | collective-permute-start | bytes 196616 | tf_op jit(solution)/shard_map/ppermute | solution.py:252
  6.1 0.3 shard_map.102
  6.4 2.0 %collective-permute-start.3 = (bf16[256,512]{1,0:T(8,128)(2,1)S(1)}, bf16[256,512]{1,0:T(8,128)(2,1)S(1)}, u32[]{:S(2)}, u32[]{:S(2)}) collective-permute-start(bf16[256,512]{1,0:T(8,128)(2,1)S(1)} %get-tuple-element.43), channel_id=1, source_target_pairs={{0,8},{4,20},{8,0},{12,28},{16,24},{20,4},{24,16},{28,12},{1,9},{5... | collective-permute-start | bytes 786440 | tf_op jit(solution)/shard_map/ppermute | solution.py:249
  8.4 0.3 shard_map.103
  8.7 0.2 collective-permute-start.5
  8.9 1.3 %collective-permute-done.refs_3_ = bf16[64,512]{1,0:T(8,128)(2,1)S(1)} collective-permute-done((bf16[64,512]{1,0:T(8,128)(2,1)S(1)}, bf16[64,512]{1,0:T(8,128)(2,1)S(1)}, u32[]{:S(2)}, u32[]{:S(2)}) %collective-permute-start) | collective-permute-done | bytes 65568 | tf_op jit(solution)/shard_map/ppermute | solution.py:252
  10.2 0.8 %shard_map.104 = (bf16[384,512]{1,0:T(8,128)(2,1)S(1)}, f32[64,512]{1,0:T(8,128)S(1)}, f32[64,512]{1,0:T(8,128)S(1)}) custom-call(bf16[256,2048]{1,0:T(8,128)(2,1)S(1)} %copy-done.3, bf16[2048,512]{1,0:T(8,128)(2,1)S(1)} %bitcast.4, bf16[64,512]{1,0:T(8,128)(2,1)S(1)} %get-tuple-element.37.refs_2_, bf16[64,512]{1,0:T(8,128)(2,1)S(1)} %collective-permute-done.refs_3_, ...), custom_call_target="tpu_custom_call" | custom-call | flops 330000000 | tf_op jit(solution)/shard_map/pallas_call | solution.py:59
  11.0 1.6 %collective-permute-start.2 = (bf16[384,512]{1,0:T(8,128)(2,1)S(1)}, bf16[384,512]{1,0:T(8,128)(2,1)S(1)}, u32[]{:S(2)}, u32[]{:S(2)}) collective-permute-start(bf16[384,512]{1,0:T(8,128)(2,1)S(1)} %get-tuple-element.42.refs_3_.refs_5_), channel_id=1, source_target_pairs={{0,1},{1,0},{2,3},{3,2},{4,5},{5,4},{6,7},{7,6},{8,9},{9,8},{10,11... | collective-permute-start | bytes 1179656 | tf_op jit(solution)/shard_map/ppermute | solution.py:252
  12.6 0.2 collective-permute-done.3.refs_1_
  12.8 0.4 %shard_map.105 = (f32[256,512]{1,0:T(8,128)S(1)}, bf16[256,512]{1,0:T(8,128)(2,1)S(1)}) custom-call(f32[256,512]{1,0:T(8,128)S(1)} %get-tuple-element.40.refs_2_.refs_0_, bf16[256,512]{1,0:T(8,128)(2,1)S(1)} %collective-permute-done.3.refs_1_), custom_call_target="tpu_custom_call" | custom-call | flops 1650000000 | tf_op jit(solution)/shard_map/pallas_call | solution.py:59
  13.3 2.0 %collective-permute-start.4 = (bf16[256,512]{1,0:T(8,128)(2,1)S(1)}, bf16[256,512]{1,0:T(8,128)(2,1)S(1)}, u32[]{:S(2)}, u32[]{:S(2)}) collective-permute-start(bf16[256,512]{1,0:T(8,128)(2,1)S(1)} %get-tuple-element.45), channel_id=1, source_target_pairs={{0,16},{4,12},{8,24},{12,4},{16,0},{20,28},{24,8},{28,20},{1,17},{... | collective-permute-start | bytes 786440 | tf_op jit(solution)/shard_map/ppermute | solution.py:249
  15.3 0.5 %collective-permute-done.5.refs_1_ = bf16[256,512]{1,0:T(8,128)(2,1)S(1)} collective-permute-done((bf16[256,512]{1,0:T(8,128)(2,1)S(1)}, bf16[256,512]{1,0:T(8,128)(2,1)S(1)}, u32[]{:S(2)}, u32[]{:S(2)}) %collective-permute-start.5) | collective-permute-done | bytes 262176 | tf_op jit(solution)/shard_map/ppermute | solution.py:249
  15.8 0.4 %shard_map.106 = (f32[256,512]{1,0:T(8,128)S(1)}, bf16[256,512]{1,0:T(8,128)(2,1)S(1)}) custom-call(f32[256,512]{1,0:T(8,128)S(1)} %get-tuple-element.41.refs_4_.refs_0_, bf16[256,512]{1,0:T(8,128)(2,1)S(1)} %collective-permute-done.5.refs_1_, f32[256,512]{1,0:T(8,128)S(1)} %get-tuple-element.44.refs_2_.refs_0_, ...), custom_call_target="tpu_custom_call" | custom-call | flops 1650000000 | tf_op jit(solution)/shard_map/pallas_call | solution.py:59
  16.2 2.2 %collective-permute-start.6 = (bf16[256,512]{1,0:T(8,128)(2,1)S(1)}, bf16[256,512]{1,0:T(8,128)(2,1)S(1)}, u32[]{:S(2)}, u32[]{:S(2)}) collective-permute-start(bf16[256,512]{1,0:T(8,128)(2,1)S(1)} %get-tuple-element.52), channel_id=1, source_target_pairs={{0,16},{4,12},{8,24},{12,4},{16,0},{20,28},{24,8},{28,20},{1,17},{... | collective-permute-start | bytes 786440 | tf_op jit(solution)/shard_map/ppermute | solution.py:249
  18.4 3.5 %collective-permute-done.2.refs_0_.refs_6_ = bf16[384,512]{1,0:T(8,128)(2,1)S(1)} collective-permute-done((bf16[384,512]{1,0:T(8,128)(2,1)S(1)}, bf16[384,512]{1,0:T(8,128)(2,1)S(1)}, u32[]{:S(2)}, u32[]{:S(2)}) %collective-permute-start.2) | collective-permute-done | bytes 393248 | tf_op jit(solution)/shard_map/ppermute | solution.py:252
  22.0 0.4 %shard_map.108 = (f32[256,512]{1,0:T(8,128)S(1)}, bf16[256,512]{1,0:T(8,128)(2,1)S(1)}) custom-call(f32[256,512]{1,0:T(8,128)S(1)} %get-tuple-element.44.refs_2_.refs_0_, bf16[256,512]{1,0:T(8,128)(2,1)S(1)} %collective-permute-done.4.refs_1_, f32[64,512]{1,0:T(8,128)S(1)} %get-tuple-element.50.refs_2_.refs_4_), custom_call_target="tpu_custom_call" | custom-call | flops 1650000000 | tf_op jit(solution)/shard_map/pallas_call | solution.py:59
  22.5 0.3 collective-permute-done.6.refs_1_
  22.8 0.4 %shard_map.109 = (f32[256,512]{1,0:T(8,128)S(1)}, bf16[256,512]{1,0:T(8,128)(2,1)S(1)}) custom-call(f32[256,512]{1,0:T(8,128)S(1)} %get-tuple-element.49.refs_3_.refs_0_, bf16[256,512]{1,0:T(8,128)(2,1)S(1)} %collective-permute-done.6.refs_1_, f32[256,512]{1,0:T(8,128)S(1)} %get-tuple-element.51.refs_2_.refs_7_), custom_call_target="tpu_custom_call" | custom-call | flops 1650000000 | tf_op jit(solution)/shard_map/pallas_call | solution.py:59
  23.2 0.1 collective-permute-start.8
  23.3 0.5 %collective-permute-start.7 = (bf16[256,512]{1,0:T(8,128)(2,1)S(1)}, bf16[256,512]{1,0:T(8,128)(2,1)S(1)}, u32[]{:S(2)}, u32[]{:S(2)}) collective-permute-start(bf16[256,512]{1,0:T(8,128)(2,1)S(1)} %get-tuple-element.54), channel_id=1, source_target_pairs={{0,4},{4,0},{8,12},{12,8},{16,20},{20,16},{24,28},{28,24},{1,5},{5... | collective-permute-start | bytes 786440 | tf_op jit(solution)/shard_map/ppermute | solution.py:249
  23.8 2.0 %collective-permute-start.10 = (bf16[256,512]{1,0:T(8,128)(2,1)S(1)}, bf16[256,512]{1,0:T(8,128)(2,1)S(1)}, u32[]{:S(2)}, u32[]{:S(2)}) collective-permute-start(bf16[256,512]{1,0:T(8,128)(2,1)S(1)} %get-tuple-element.55), channel_id=1, source_target_pairs={{0,8},{4,20},{8,0},{12,28},{16,24},{20,4},{24,16},{28,12},{1,9},{5... | collective-permute-start | bytes 786440 | tf_op jit(solution)/shard_map/ppermute | solution.py:249
  25.9 3.1 %collective-permute-start.13 = (f32[64,512]{1,0:T(8,128)S(1)}, f32[64,512]{1,0:T(8,128)S(1)}, u32[]{:S(2)}, u32[]{:S(2)}) collective-permute-start(f32[64,512]{1,0:T(8,128)S(1)} %get-tuple-element.61), channel_id=1, source_target_pairs={{0,2},{1,3},{2,0},{3,1},{4,6},{5,7},{6,4},{7,5},{8,10},{9,11},{10,... | collective-permute-start | bytes 393224 | tf_op jit(solution)/shard_map/ppermute | solution.py:252
  29.0 3.9 %shard_map.110 = (bf16[2048,512]{1,0:T(8,128)(2,1)}, bf16[256,2048]{1,0:T(8,128)(2,1)}, bf16[2048,512]{1,0:T(8,128)(2,1)}, f32[256,512]{1,0:T(8,128)}, f32[256,5...) custom-call(bf16[256,2048]{1,0:T(8,128)(2,1)S(1)} %copy-done.3, ...), custom_call_target="tpu_custom_call" | custom-call | flops 990000000 | tf_op jit(solution)/shard_map/pallas_call | solution.py:59
  32.9 0.1 collective-permute-done.9.refs_0_.refs_2_
  33.0 0.1 collective-permute-start.11
  33.1 0.5 %collective-permute-start.12 = (bf16[256,512]{1,0:T(8,128)(2,1)S(1)}, bf16[256,512]{1,0:T(8,128)(2,1)S(1)}, u32[]{:S(2)}, u32[]{:S(2)}) collective-permute-start(bf16[256,512]{1,0:T(8,128)(2,1)S(1)} %get-tuple-element.60), channel_id=1, source_target_pairs={{0,4},{4,0},{8,12},{12,8},{16,20},{20,16},{24,28},{28,24},{1,5},{5... | collective-permute-start | bytes 786440 | tf_op jit(solution)/shard_map/ppermute | solution.py:249
  33.6 1.2 %shard_map.112.refs_6_ = bf16[2048,512]{1,0:T(8,128)(2,1)} custom-call(f32[256,512]{1,0:T(8,128)S(1)} %get-tuple-element.58.refs_2_.refs_0_, f32[256,512]{1,0:T(8,128)S(1)} %get-tuple-element.62.refs_1_, bf16[256,512]{1,0:T(8,128)(2,1)S(1)} %collective-permute-done.9.refs_0_.refs_2_, ...), custom_call_target="tpu_custom_call", output_to_operand_aliasing={{}: (4, {})} | custom-call | flops 26400000000 | tf_op jit(solution)/shard_map/pallas_call | solution.py:59
  34.9 0.1 collective-permute-done.13.refs_5_
  34.9 0.1 collective-permute-done.12.refs_3_
  35.0 1.2 %shard_map.113 = (bf16[2048,512]{1,0:T(8,128)(2,1)}, bf16[64,512]{1,0:T(8,128)(2,1)}) custom-call(f32[256,512]{1,0:T(8,128)S(1)} %get-tuple-element.56.refs_0_, f32[256,512]{1,0:T(8,128)S(1)} %get-tuple-element.57.refs_1_, bf16[256,512]{1,0:T(8,128)(2,1)S(1)} %collective-permute-done.11.refs_2_, ...), custom_call_target="tpu_custom_call", output_to_operand_aliasing={{0}: (6, {})} | custom-call | flops 26400000000 | tf_op jit(solution)/shard_map/pallas_call | solution.py:59
  (19 shorter events, 0.2 us)
Async XLA Ops:
  0.6 5.5 %collective-permute-start.1 = (bf16[2048,512]{1,0:T(8,128)(2,1)}, bf16[2048,512]{1,0:T(8,128)(2,1)S(1)}, u32[]{:S(2)}, u32[]{:S(2)}) collective-permute-start(bf16[2048,512]{1,0:T(8,128)(2,1)} %bitcast.6), channel_id=1, source_target_pairs={{0,4},{4,0},{8,12},{12,8},{16,20},{20,16},{24,28},{28,24},{1,5},{5... | collective-permute-start | bytes 6291464 | tf_op jit(solution)/shard_map/ppermute | solution.py:249
  2.4 7.8 %collective-permute-start = (bf16[64,512]{1,0:T(8,128)(2,1)S(1)}, bf16[64,512]{1,0:T(8,128)(2,1)S(1)}, u32[]{:S(2)}, u32[]{:S(2)}) collective-permute-start(bf16[64,512]{1,0:T(8,128)(2,1)S(1)} %get-tuple-element.37.refs_2_), channel_id=1, source_target_pairs={{0,2},{1,3},{2,0},{3,1},{4,6},{5,7},{6,4},{7,5},{8,10},{9,11},{10,... | collective-permute-start | bytes 196616 | tf_op jit(solution)/shard_map/ppermute | solution.py:252
  6.4 6.4 %collective-permute-start.3 = (bf16[256,512]{1,0:T(8,128)(2,1)S(1)}, bf16[256,512]{1,0:T(8,128)(2,1)S(1)}, u32[]{:S(2)}, u32[]{:S(2)}) collective-permute-start(bf16[256,512]{1,0:T(8,128)(2,1)S(1)} %get-tuple-element.43), channel_id=1, source_target_pairs={{0,8},{4,20},{8,0},{12,28},{16,24},{20,4},{24,16},{28,12},{1,9},{5... | collective-permute-start | bytes 786440 | tf_op jit(solution)/shard_map/ppermute | solution.py:249
  8.4 1.8 %copy-start = (bf16[1,2048,512]{2,1,0:T(8,128)(2,1)S(1)}, bf16[1,2048,512]{2,1,0:T(8,128)(2,1)}, u32[]{:S(2)}) copy-start(bf16[1,2048,512]{2,1,0:T(8,128)(2,1)} %param.7) | copy-start | bytes 6291460
  8.4 1.9 %copy-start.3 = (bf16[256,2048]{1,0:T(8,128)(2,1)S(1)}, bf16[256,2048]{1,0:T(8,128)(2,1)}, u32[]{:S(2)}) copy-start(bf16[256,2048]{1,0:T(8,128)(2,1)} %refs_0_.3) | copy-start | bytes 3145732
  8.7 7.1 %collective-permute-start.5 = (bf16[256,512]{1,0:T(8,128)(2,1)S(1)}, bf16[256,512]{1,0:T(8,128)(2,1)S(1)}, u32[]{:S(2)}, u32[]{:S(2)}) collective-permute-start(bf16[256,512]{1,0:T(8,128)(2,1)S(1)} %get-tuple-element.48), channel_id=1, source_target_pairs={{0,8},{4,20},{8,0},{12,28},{16,24},{20,4},{24,16},{28,12},{1,9},{5... | collective-permute-start | bytes 786440 | tf_op jit(solution)/shard_map/ppermute | solution.py:249
  11.0 11.0 %collective-permute-start.2 = (bf16[384,512]{1,0:T(8,128)(2,1)S(1)}, bf16[384,512]{1,0:T(8,128)(2,1)S(1)}, u32[]{:S(2)}, u32[]{:S(2)}) collective-permute-start(bf16[384,512]{1,0:T(8,128)(2,1)S(1)} %get-tuple-element.42.refs_3_.refs_5_), channel_id=1, source_target_pairs={{0,1},{1,0},{2,3},{3,2},{4,5},{5,4},{6,7},{7,6},{8,9},{9,8},{10,11... | collective-permute-start | bytes 1179656 | tf_op jit(solution)/shard_map/ppermute | solution.py:252
  13.3 8.7 %collective-permute-start.4 = (bf16[256,512]{1,0:T(8,128)(2,1)S(1)}, bf16[256,512]{1,0:T(8,128)(2,1)S(1)}, u32[]{:S(2)}, u32[]{:S(2)}) collective-permute-start(bf16[256,512]{1,0:T(8,128)(2,1)S(1)} %get-tuple-element.45), channel_id=1, source_target_pairs={{0,16},{4,12},{8,24},{12,4},{16,0},{20,28},{24,8},{28,20},{1,17},{... | collective-permute-start | bytes 786440 | tf_op jit(solution)/shard_map/ppermute | solution.py:249
  16.2 6.6 %collective-permute-start.6 = (bf16[256,512]{1,0:T(8,128)(2,1)S(1)}, bf16[256,512]{1,0:T(8,128)(2,1)S(1)}, u32[]{:S(2)}, u32[]{:S(2)}) collective-permute-start(bf16[256,512]{1,0:T(8,128)(2,1)S(1)} %get-tuple-element.52), channel_id=1, source_target_pairs={{0,16},{4,12},{8,24},{12,4},{16,0},{20,28},{24,8},{28,20},{1,17},{... | collective-permute-start | bytes 786440 | tf_op jit(solution)/shard_map/ppermute | solution.py:249
  22.0 6.9 %copy-start.2 = (f32[2048,512]{1,0:T(8,128)S(1)}, f32[2048,512]{1,0:T(8,128)}, u32[]{:S(2)}) copy-start(f32[2048,512]{1,0:T(8,128)} %refs_3_.1) | copy-start | bytes 12582916
  22.0 6.9 %copy-start.4 = (bf16[1,2048,512]{2,1,0:T(8,128)(2,1)S(1)}, bf16[1,2048,512]{2,1,0:T(8,128)(2,1)}, u32[]{:S(2)}) copy-start(bf16[1,2048,512]{2,1,0:T(8,128)(2,1)} %param.11) | copy-start | bytes 6291460
  22.8 6.2 %copy-start.1 = (f32[2048,512]{1,0:T(8,128)S(1)}, f32[2048,512]{1,0:T(8,128)}, u32[]{:S(2)}) copy-start(f32[2048,512]{1,0:T(8,128)} %refs_2_.1) | copy-start | bytes 12582916
  23.2 5.7 %collective-permute-start.8 = (bf16[256,512]{1,0:T(8,128)(2,1)S(1)}, bf16[256,512]{1,0:T(8,128)(2,1)S(1)}, u32[]{:S(2)}, u32[]{:S(2)}) collective-permute-start(bf16[256,512]{1,0:T(8,128)(2,1)S(1)} %get-tuple-element.55), channel_id=1, source_target_pairs={{0,4},{4,0},{8,12},{12,8},{16,20},{20,16},{24,28},{28,24},{1,5},{5... | collective-permute-start | bytes 786440 | tf_op jit(solution)/shard_map/ppermute | solution.py:249
  23.3 5.6 %collective-permute-start.7 = (bf16[256,512]{1,0:T(8,128)(2,1)S(1)}, bf16[256,512]{1,0:T(8,128)(2,1)S(1)}, u32[]{:S(2)}, u32[]{:S(2)}) collective-permute-start(bf16[256,512]{1,0:T(8,128)(2,1)S(1)} %get-tuple-element.54), channel_id=1, source_target_pairs={{0,4},{4,0},{8,12},{12,8},{16,20},{20,16},{24,28},{28,24},{1,5},{5... | collective-permute-start | bytes 786440 | tf_op jit(solution)/shard_map/ppermute | solution.py:249
  23.8 9.1 %collective-permute-start.10 = (bf16[256,512]{1,0:T(8,128)(2,1)S(1)}, bf16[256,512]{1,0:T(8,128)(2,1)S(1)}, u32[]{:S(2)}, u32[]{:S(2)}) collective-permute-start(bf16[256,512]{1,0:T(8,128)(2,1)S(1)} %get-tuple-element.55), channel_id=1, source_target_pairs={{0,8},{4,20},{8,0},{12,28},{16,24},{20,4},{24,16},{28,12},{1,9},{5... | collective-permute-start | bytes 786440 | tf_op jit(solution)/shard_map/ppermute | solution.py:249
  25.8 7.2 %collective-permute-start.9 = (bf16[256,512]{1,0:T(8,128)(2,1)S(1)}, bf16[256,512]{1,0:T(8,128)(2,1)S(1)}, u32[]{:S(2)}, u32[]{:S(2)}) collective-permute-start(bf16[256,512]{1,0:T(8,128)(2,1)S(1)} %get-tuple-element.54), channel_id=1, source_target_pairs={{0,8},{4,20},{8,0},{12,28},{16,24},{20,4},{24,16},{28,12},{1,9},{5... | collective-permute-start | bytes 786440 | tf_op jit(solution)/shard_map/ppermute | solution.py:249
  25.9 9.1 %collective-permute-start.13 = (f32[64,512]{1,0:T(8,128)S(1)}, f32[64,512]{1,0:T(8,128)S(1)}, u32[]{:S(2)}, u32[]{:S(2)}) collective-permute-start(f32[64,512]{1,0:T(8,128)S(1)} %get-tuple-element.61), channel_id=1, source_target_pairs={{0,2},{1,3},{2,0},{3,1},{4,6},{5,7},{6,4},{7,5},{8,10},{9,11},{10,... | collective-permute-start | bytes 393224 | tf_op jit(solution)/shard_map/ppermute | solution.py:252
  33.0 1.9 %collective-permute-start.11 = (bf16[256,512]{1,0:T(8,128)(2,1)S(1)}, bf16[256,512]{1,0:T(8,128)(2,1)S(1)}, u32[]{:S(2)}, u32[]{:S(2)}) collective-permute-start(bf16[256,512]{1,0:T(8,128)(2,1)S(1)} %get-tuple-element.59), channel_id=1, source_target_pairs={{0,4},{4,0},{8,12},{12,8},{16,20},{20,16},{24,28},{28,24},{1,5},{5... | collective-permute-start | bytes 786440 | tf_op jit(solution)/shard_map/ppermute | solution.py:249
  33.1 1.9 %collective-permute-start.12 = (bf16[256,512]{1,0:T(8,128)(2,1)S(1)}, bf16[256,512]{1,0:T(8,128)(2,1)S(1)}, u32[]{:S(2)}, u32[]{:S(2)}) collective-permute-start(bf16[256,512]{1,0:T(8,128)(2,1)S(1)} %get-tuple-element.60), channel_id=1, source_target_pairs={{0,4},{4,0},{8,12},{12,8},{16,20},{20,16},{24,28},{28,24},{1,5},{5... | collective-permute-start | bytes 786440 | tf_op jit(solution)/shard_map/ppermute | solution.py:249

commit v5 on v4

--- a/solution.py
+++ b/solution.py
@@ -30,9 +30,17 @@
     return jnp.where(code < 0, -value, value)
 
 
-pace = 3.3e9
-cost = {"pair": (0.9, 0.9), "keys": 0.1, "add": (0.5, 0.5), "keys_add": 0.4, "fresh": 0.3, "update": (8.0, 8.0), "relay": 0.3, "fetch": 0.5}
-opt = {"kg_gate": 0, "keys_gate": 2, "add_gate": 1}
+pace = 2e9
+cost = {
+    "fetch": 0.5,
+    "pair": (0.9, 0.9),
+    "keys": 0.1,
+    "add": (0.5, 0.5),
+    "keys_add": 0.4,
+    "fresh": 0.3,
+    "relay": 0.3,
+    "update": (8.0, 8.0),
+}
 
 
 def place(me):
@@ -272,7 +280,7 @@
             functools.partial(pair_kernel, size, c),
             [(owns[c], VMEM), (other, VMEM)],
             [(window, bf16, VMEM), (window, f32, VMEM)],
-            after=keeps + [grad_far] * (c == 1 and opt["kg_gate"]),
+            after=keeps,
             micros=cost["pair"][c],
         )
         codes.append(code)
@@ -290,21 +298,18 @@
     arrived = across_shards(packed, 1)
     grads = [packed, arrived]
 
-    def added(held, total, gates):
+    def added(held, total, before_second):
         for c in chunks:
             keeps[c], codes[c] = call(
                 functools.partial(add_kernel, held, total),
                 [(keeps[c], VMEM), (got[c], VMEM)],
                 [(window, f32, VMEM), (window, bf16, VMEM)],
-                after=gates[c] if c == 0 else [keeps[0], *gates[c]],
+                after=[] if c == 0 else [keeps[0], *before_second],
                 micros=cost["add"][c],
             )
 
     late_kinds = [("near", 0), ("far", 0), ("near", 1), ("far", 1)]
-    gates = [[], []]
-    if opt["keys_gate"]:
-        gates[opt["keys_gate"] - 1].append(packed)
-    added(2, 4, gates)
+    added(2, 4, [packed])
     got = [swap(codes[c], last) for c in chunks]
     own_keys, later_keys = call(
         keys_add_kernel,
@@ -314,10 +319,7 @@
         micros=cost["keys_add"],
     )
     key_far = across_shards(later_keys, 2)
-    gates = [[], []]
-    if opt["add_gate"] in (1, 2):
-        gates[opt["add_gate"] - 1].append(own_keys)
-    added(4, 8, gates)
+    added(4, 8, [own_keys])
     near = [swap(codes[c], first) for c in chunks]
     across = [swap(codes[c], beside) for c in chunks]
     soon_kinds = [("own", 0), ("own", 1), ("across", 0), ("across", 1)]
@@ -342,7 +344,6 @@
             pltpu.VMEM((batch, columns), bf16),
             DMA((5 * n + 1,)),
         ],
-        after=[own_keys] if opt["add_gate"] == 3 else [],
         micros=cost["fresh"],
     )
     relayed = call(

time: 36.4 us -> 36.4 us (level)
  no operation moved by 1% of the time
where the time goes in v5:
time: 36.4 us; the launch traced here: 36.3 us
  starting transfers between devices  18.5 us (51%)
  Pallas kernels  10.8 us (30%)
  waiting for transfers between devices  6.12 us (17%)
  between operations  0.77 us (2%)
    pallas_call x13, Pallas kernels, call(): pl.pallas_call(body, in_specs=[pl.BlockSpec(memory_space=s) for _, s in i...  10.8 us
    ppermute x11, starting transfers between devices, swap(): lax.ppermute(value, 'worker', [(i, i ^ flips[i % 2]) for i in range(worke...  10.1 us
    ppermute x3, starting transfers between devices, across_shards(): lax.ppermute(value, 'fsdp', [(i, i ^ distance) for i in range(shards)])  8.41 us
    ppermute x3, waiting for transfers between devices, across_shards(): lax.ppermute(value, 'fsdp', [(i, i ^ distance) for i in range(shards)])  4.92 us
    ppermute x11, waiting for transfers between devices, swap(): lax.ppermute(value, 'worker', [(i, i ^ flips[i % 2]) for i in range(worke...  1.2 us
  transfers between devices with their start and end apart: 14, of which 8 were waited for; matrix products, arithmetic and copies ran while one was open for 0% of the time, Pallas kernels for 25%

profile of v5, /device:TPU:0, one launch (start us, length us, event | category | flops | bytes accessed | tf_op | source)
XLA Modules:
  0.0 36.3 jit_solution(1140240959992350878)
XLA Ops:
  0.6 0.5 %collective-permute-start.1 = (bf16[2048,512]{1,0:T(8,128)(2,1)}, bf16[2048,512]{1,0:T(8,128)(2,1)S(1)}, u32[]{:S(2)}, u32[]{:S(2)}) collective-permute-start(bf16[2048,512]{1,0:T(8,128)(2,1)} %bitcast.6), channel_id=1, source_target_pairs={{0,4},{4,0},{8,12},{12,8},{16,20},{20,16},{24,28},{28,24},{1,5},{5... | collective-permute-start | bytes 6291464 | tf_op jit(solution)/shard_map/ppermute | solution.py:257
  1.1 1.2 %shard_map.101 = (bf16[512,512]{1,0:T(8,128)(2,1)S(1)}, bf16[512,512]{1,0:T(8,128)(2,1)S(1)}, bf16[64,512]{1,0:T(8,128)(2,1)S(1)}) custom-call(bf16[2048,512]{1,0:T(8,128)(2,1)} %bitcast.7, bf16[64,512]{1,0:T(8,128)(2,1)} %refs_1_.1), custom_call_target="tpu_custom_call" | custom-call | flops 1000000000 | tf_op jit(solution)/shard_map/pallas_call | solution.py:67
  2.4 3.7 %collective-permute-start = (bf16[64,512]{1,0:T(8,128)(2,1)S(1)}, bf16[64,512]{1,0:T(8,128)(2,1)S(1)}, u32[]{:S(2)}, u32[]{:S(2)}) collective-permute-start(bf16[64,512]{1,0:T(8,128)(2,1)S(1)} %get-tuple-element.37.refs_2_), channel_id=1, source_target_pairs={{0,2},{1,3},{2,0},{3,1},{4,6},{5,7},{6,4},{7,5},{8,10},{9,11},{10,... | collective-permute-start | bytes 196616 | tf_op jit(solution)/shard_map/ppermute | solution.py:260
  6.1 0.3 shard_map.102
  6.4 2.0 %collective-permute-start.3 = (bf16[256,512]{1,0:T(8,128)(2,1)S(1)}, bf16[256,512]{1,0:T(8,128)(2,1)S(1)}, u32[]{:S(2)}, u32[]{:S(2)}) collective-permute-start(bf16[256,512]{1,0:T(8,128)(2,1)S(1)} %get-tuple-element.43), channel_id=1, source_target_pairs={{0,8},{4,20},{8,0},{12,28},{16,24},{20,4},{24,16},{28,12},{1,9},{5... | collective-permute-start | bytes 786440 | tf_op jit(solution)/shard_map/ppermute | solution.py:257
  8.4 0.3 shard_map.103
  8.7 0.2 collective-permute-start.5
  8.9 1.3 %collective-permute-done.refs_3_ = bf16[64,512]{1,0:T(8,128)(2,1)S(1)} collective-permute-done((bf16[64,512]{1,0:T(8,128)(2,1)S(1)}, bf16[64,512]{1,0:T(8,128)(2,1)S(1)}, u32[]{:S(2)}, u32[]{:S(2)}) %collective-permute-start) | collective-permute-done | bytes 65568 | tf_op jit(solution)/shard_map/ppermute | solution.py:260
  10.2 0.8 %shard_map.104 = (bf16[384,512]{1,0:T(8,128)(2,1)S(1)}, f32[64,512]{1,0:T(8,128)S(1)}, f32[64,512]{1,0:T(8,128)S(1)}) custom-call(bf16[256,2048]{1,0:T(8,128)(2,1)S(1)} %copy-done.3, bf16[2048,512]{1,0:T(8,128)(2,1)S(1)} %bitcast.4, bf16[64,512]{1,0:T(8,128)(2,1)S(1)} %get-tuple-element.37.refs_2_, bf16[64,512]{1,0:T(8,128)(2,1)S(1)} %collective-permute-done.refs_3_, ...), custom_call_target="tpu_custom_call" | custom-call | flops 200000000 | tf_op jit(solution)/shard_map/pallas_call | solution.py:67
  11.0 1.6 %collective-permute-start.2 = (bf16[384,512]{1,0:T(8,128)(2,1)S(1)}, bf16[384,512]{1,0:T(8,128)(2,1)S(1)}, u32[]{:S(2)}, u32[]{:S(2)}) collective-permute-start(bf16[384,512]{1,0:T(8,128)(2,1)S(1)} %get-tuple-element.42.refs_3_.refs_5_), channel_id=1, source_target_pairs={{0,1},{1,0},{2,3},{3,2},{4,5},{5,4},{6,7},{7,6},{8,9},{9,8},{10,11... | collective-permute-start | bytes 1179656 | tf_op jit(solution)/shard_map/ppermute | solution.py:260
  12.6 0.2 collective-permute-done.3.refs_1_
  12.8 0.4 %shard_map.105 = (f32[256,512]{1,0:T(8,128)S(1)}, bf16[256,512]{1,0:T(8,128)(2,1)S(1)}) custom-call(f32[256,512]{1,0:T(8,128)S(1)} %get-tuple-element.40.refs_2_.refs_0_, bf16[256,512]{1,0:T(8,128)(2,1)S(1)} %collective-permute-done.3.refs_1_), custom_call_target="tpu_custom_call" | custom-call | flops 1000000000 | tf_op jit(solution)/shard_map/pallas_call | solution.py:67
  13.3 2.0 %collective-permute-start.4 = (bf16[256,512]{1,0:T(8,128)(2,1)S(1)}, bf16[256,512]{1,0:T(8,128)(2,1)S(1)}, u32[]{:S(2)}, u32[]{:S(2)}) collective-permute-start(bf16[256,512]{1,0:T(8,128)(2,1)S(1)} %get-tuple-element.45), channel_id=1, source_target_pairs={{0,16},{4,12},{8,24},{12,4},{16,0},{20,28},{24,8},{28,20},{1,17},{... | collective-permute-start | bytes 786440 | tf_op jit(solution)/shard_map/ppermute | solution.py:257
  15.3 0.5 %collective-permute-done.5.refs_1_ = bf16[256,512]{1,0:T(8,128)(2,1)S(1)} collective-permute-done((bf16[256,512]{1,0:T(8,128)(2,1)S(1)}, bf16[256,512]{1,0:T(8,128)(2,1)S(1)}, u32[]{:S(2)}, u32[]{:S(2)}) %collective-permute-start.5) | collective-permute-done | bytes 262176 | tf_op jit(solution)/shard_map/ppermute | solution.py:257
  15.8 0.4 %shard_map.107 = (f32[256,512]{1,0:T(8,128)S(1)}, bf16[256,512]{1,0:T(8,128)(2,1)S(1)}) custom-call(f32[256,512]{1,0:T(8,128)S(1)} %get-tuple-element.41.refs_4_.refs_0_, bf16[256,512]{1,0:T(8,128)(2,1)S(1)} %collective-permute-done.5.refs_1_, f32[256,512]{1,0:T(8,128)S(1)} %get-tuple-element.44.refs_0_.refs_2_, ...), custom_call_target="tpu_custom_call" | custom-call | flops 1000000000 | tf_op jit(solution)/shard_map/pallas_call | solution.py:67
  16.2 2.2 %collective-permute-start.6 = (bf16[256,512]{1,0:T(8,128)(2,1)S(1)}, bf16[256,512]{1,0:T(8,128)(2,1)S(1)}, u32[]{:S(2)}, u32[]{:S(2)}) collective-permute-start(bf16[256,512]{1,0:T(8,128)(2,1)S(1)} %get-tuple-element.49), channel_id=1, source_target_pairs={{0,16},{4,12},{8,24},{12,4},{16,0},{20,28},{24,8},{28,20},{1,17},{... | collective-permute-start | bytes 786440 | tf_op jit(solution)/shard_map/ppermute | solution.py:257
  18.5 3.5 %collective-permute-done.2.refs_0_.refs_6_ = bf16[384,512]{1,0:T(8,128)(2,1)S(1)} collective-permute-done((bf16[384,512]{1,0:T(8,128)(2,1)S(1)}, bf16[384,512]{1,0:T(8,128)(2,1)S(1)}, u32[]{:S(2)}, u32[]{:S(2)}) %collective-permute-start.2) | collective-permute-done | bytes 393248 | tf_op jit(solution)/shard_map/ppermute | solution.py:260
  22.0 0.4 %shard_map.106 = (f32[256,512]{1,0:T(8,128)S(1)}, bf16[256,512]{1,0:T(8,128)(2,1)S(1)}) custom-call(f32[256,512]{1,0:T(8,128)S(1)} %get-tuple-element.44.refs_0_.refs_2_, bf16[256,512]{1,0:T(8,128)(2,1)S(1)} %collective-permute-done.4.refs_1_), custom_call_target="tpu_custom_call" | custom-call | flops 1000000000 | tf_op jit(solution)/shard_map/pallas_call | solution.py:67
  22.5 0.3 collective-permute-done.6.refs_1_
  22.8 0.4 %shard_map.109 = (f32[256,512]{1,0:T(8,128)S(1)}, bf16[256,512]{1,0:T(8,128)(2,1)S(1)}) custom-call(f32[256,512]{1,0:T(8,128)S(1)} %get-tuple-element.48.refs_3_.refs_0_, bf16[256,512]{1,0:T(8,128)(2,1)S(1)} %collective-permute-done.6.refs_1_, f32[256,512]{1,0:T(8,128)S(1)} %get-tuple-element.46.refs_2_.refs_7_, f32[64,512]{1,0:T(8,128)S(1)} %get-tuple-element.52.refs_3_.refs_4_), custom_call_target="tpu_custom_call" | custom-call | flops 1000000000 | tf_op jit(solution)/shard_map/pallas_call | solution.py:67
  23.2 0.1 collective-permute-start.8
  23.3 0.5 %collective-permute-start.7 = (bf16[256,512]{1,0:T(8,128)(2,1)S(1)}, bf16[256,512]{1,0:T(8,128)(2,1)S(1)}, u32[]{:S(2)}, u32[]{:S(2)}) collective-permute-start(bf16[256,512]{1,0:T(8,128)(2,1)S(1)} %get-tuple-element.54), channel_id=1, source_target_pairs={{0,4},{4,0},{8,12},{12,8},{16,20},{20,16},{24,28},{28,24},{1,5},{5... | collective-permute-start | bytes 786440 | tf_op jit(solution)/shard_map/ppermute | solution.py:257
  23.8 2.0 %collective-permute-start.10 = (bf16[256,512]{1,0:T(8,128)(2,1)S(1)}, bf16[256,512]{1,0:T(8,128)(2,1)S(1)}, u32[]{:S(2)}, u32[]{:S(2)}) collective-permute-start(bf16[256,512]{1,0:T(8,128)(2,1)S(1)} %get-tuple-element.55), channel_id=1, source_target_pairs={{0,8},{4,20},{8,0},{12,28},{16,24},{20,4},{24,16},{28,12},{1,9},{5... | collective-permute-start | bytes 786440 | tf_op jit(solution)/shard_map/ppermute | solution.py:257
  25.9 3.1 %collective-permute-start.13 = (f32[64,512]{1,0:T(8,128)S(1)}, f32[64,512]{1,0:T(8,128)S(1)}, u32[]{:S(2)}, u32[]{:S(2)}) collective-permute-start(f32[64,512]{1,0:T(8,128)S(1)} %get-tuple-element.61), channel_id=1, source_target_pairs={{0,2},{1,3},{2,0},{3,1},{4,6},{5,7},{6,4},{7,5},{8,10},{9,11},{10,... | collective-permute-start | bytes 393224 | tf_op jit(solution)/shard_map/ppermute | solution.py:260
  29.0 3.9 %shard_map.110 = (bf16[2048,512]{1,0:T(8,128)(2,1)}, bf16[256,2048]{1,0:T(8,128)(2,1)}, bf16[2048,512]{1,0:T(8,128)(2,1)}, f32[256,512]{1,0:T(8,128)}, f32[256,5...) custom-call(bf16[256,2048]{1,0:T(8,128)(2,1)S(1)} %copy-done.3, ...), custom_call_target="tpu_custom_call" | custom-call | flops 600000000 | tf_op jit(solution)/shard_map/pallas_call | solution.py:67
  32.9 0.1 collective-permute-done.9.refs_0_.refs_2_
  33.0 0.1 collective-permute-start.11
  33.1 0.5 %collective-permute-start.12 = (bf16[256,512]{1,0:T(8,128)(2,1)S(1)}, bf16[256,512]{1,0:T(8,128)(2,1)S(1)}, u32[]{:S(2)}, u32[]{:S(2)}) collective-permute-start(bf16[256,512]{1,0:T(8,128)(2,1)S(1)} %get-tuple-element.60), channel_id=1, source_target_pairs={{0,4},{4,0},{8,12},{12,8},{16,20},{20,16},{24,28},{28,24},{1,5},{5... | collective-permute-start | bytes 786440 | tf_op jit(solution)/shard_map/ppermute | solution.py:257
  33.6 1.2 %shard_map.112.refs_6_ = bf16[2048,512]{1,0:T(8,128)(2,1)} custom-call(f32[256,512]{1,0:T(8,128)S(1)} %get-tuple-element.58.refs_2_.refs_0_, f32[256,512]{1,0:T(8,128)S(1)} %get-tuple-element.62.refs_1_, bf16[256,512]{1,0:T(8,128)(2,1)S(1)} %collective-permute-done.9.refs_0_.refs_2_, ...), custom_call_target="tpu_custom_call", output_to_operand_aliasing={{}: (4, {})} | custom-call | flops 16000000000 | tf_op jit(solution)/shard_map/pallas_call | solution.py:67
  34.9 0.1 collective-permute-done.13.refs_5_
  34.9 0.1 collective-permute-done.12.refs_3_
  35.0 1.2 %shard_map.113 = (bf16[2048,512]{1,0:T(8,128)(2,1)}, bf16[64,512]{1,0:T(8,128)(2,1)}) custom-call(f32[256,512]{1,0:T(8,128)S(1)} %get-tuple-element.56.refs_0_, f32[256,512]{1,0:T(8,128)S(1)} %get-tuple-element.57.refs_1_, bf16[256,512]{1,0:T(8,128)(2,1)S(1)} %collective-permute-done.11.refs_2_, ...), custom_call_target="tpu_custom_call", output_to_operand_aliasing={{0}: (6, {})} | custom-call | flops 16000000000 | tf_op jit(solution)/shard_map/pallas_call | solution.py:67
  (19 shorter events, 0.2 us)
Async XLA Ops:
  0.6 5.5 %collective-permute-start.1 = (bf16[2048,512]{1,0:T(8,128)(2,1)}, bf16[2048,512]{1,0:T(8,128)(2,1)S(1)}, u32[]{:S(2)}, u32[]{:S(2)}) collective-permute-start(bf16[2048,512]{1,0:T(8,128)(2,1)} %bitcast.6), channel_id=1, source_target_pairs={{0,4},{4,0},{8,12},{12,8},{16,20},{20,16},{24,28},{28,24},{1,5},{5... | collective-permute-start | bytes 6291464 | tf_op jit(solution)/shard_map/ppermute | solution.py:257
  2.4 7.8 %collective-permute-start = (bf16[64,512]{1,0:T(8,128)(2,1)S(1)}, bf16[64,512]{1,0:T(8,128)(2,1)S(1)}, u32[]{:S(2)}, u32[]{:S(2)}) collective-permute-start(bf16[64,512]{1,0:T(8,128)(2,1)S(1)} %get-tuple-element.37.refs_2_), channel_id=1, source_target_pairs={{0,2},{1,3},{2,0},{3,1},{4,6},{5,7},{6,4},{7,5},{8,10},{9,11},{10,... | collective-permute-start | bytes 196616 | tf_op jit(solution)/shard_map/ppermute | solution.py:260
  6.4 6.4 %collective-permute-start.3 = (bf16[256,512]{1,0:T(8,128)(2,1)S(1)}, bf16[256,512]{1,0:T(8,128)(2,1)S(1)}, u32[]{:S(2)}, u32[]{:S(2)}) collective-permute-start(bf16[256,512]{1,0:T(8,128)(2,1)S(1)} %get-tuple-element.43), channel_id=1, source_target_pairs={{0,8},{4,20},{8,0},{12,28},{16,24},{20,4},{24,16},{28,12},{1,9},{5... | collective-permute-start | bytes 786440 | tf_op jit(solution)/shard_map/ppermute | solution.py:257
  8.4 1.8 %copy-start = (bf16[1,2048,512]{2,1,0:T(8,128)(2,1)S(1)}, bf16[1,2048,512]{2,1,0:T(8,128)(2,1)}, u32[]{:S(2)}) copy-start(bf16[1,2048,512]{2,1,0:T(8,128)(2,1)} %param.7) | copy-start | bytes 6291460
  8.4 1.9 %copy-start.3 = (bf16[256,2048]{1,0:T(8,128)(2,1)S(1)}, bf16[256,2048]{1,0:T(8,128)(2,1)}, u32[]{:S(2)}) copy-start(bf16[256,2048]{1,0:T(8,128)(2,1)} %refs_0_.3) | copy-start | bytes 3145732
  8.7 7.1 %collective-permute-start.5 = (bf16[256,512]{1,0:T(8,128)(2,1)S(1)}, bf16[256,512]{1,0:T(8,128)(2,1)S(1)}, u32[]{:S(2)}, u32[]{:S(2)}) collective-permute-start(bf16[256,512]{1,0:T(8,128)(2,1)S(1)} %get-tuple-element.47), channel_id=1, source_target_pairs={{0,8},{4,20},{8,0},{12,28},{16,24},{20,4},{24,16},{28,12},{1,9},{5... | collective-permute-start | bytes 786440 | tf_op jit(solution)/shard_map/ppermute | solution.py:257
  11.0 11.0 %collective-permute-start.2 = (bf16[384,512]{1,0:T(8,128)(2,1)S(1)}, bf16[384,512]{1,0:T(8,128)(2,1)S(1)}, u32[]{:S(2)}, u32[]{:S(2)}) collective-permute-start(bf16[384,512]{1,0:T(8,128)(2,1)S(1)} %get-tuple-element.42.refs_3_.refs_5_), channel_id=1, source_target_pairs={{0,1},{1,0},{2,3},{3,2},{4,5},{5,4},{6,7},{7,6},{8,9},{9,8},{10,11... | collective-permute-start | bytes 1179656 | tf_op jit(solution)/shard_map/ppermute | solution.py:260
  13.3 8.8 %collective-permute-start.4 = (bf16[256,512]{1,0:T(8,128)(2,1)S(1)}, bf16[256,512]{1,0:T(8,128)(2,1)S(1)}, u32[]{:S(2)}, u32[]{:S(2)}) collective-permute-start(bf16[256,512]{1,0:T(8,128)(2,1)S(1)} %get-tuple-element.45), channel_id=1, source_target_pairs={{0,16},{4,12},{8,24},{12,4},{16,0},{20,28},{24,8},{28,20},{1,17},{... | collective-permute-start | bytes 786440 | tf_op jit(solution)/shard_map/ppermute | solution.py:257
  15.8 13.2 %copy-start.4 = (bf16[1,2048,512]{2,1,0:T(8,128)(2,1)S(1)}, bf16[1,2048,512]{2,1,0:T(8,128)(2,1)}, u32[]{:S(2)}) copy-start(bf16[1,2048,512]{2,1,0:T(8,128)(2,1)} %param.11) | copy-start | bytes 6291460
  16.2 6.6 %collective-permute-start.6 = (bf16[256,512]{1,0:T(8,128)(2,1)S(1)}, bf16[256,512]{1,0:T(8,128)(2,1)S(1)}, u32[]{:S(2)}, u32[]{:S(2)}) collective-permute-start(bf16[256,512]{1,0:T(8,128)(2,1)S(1)} %get-tuple-element.49), channel_id=1, source_target_pairs={{0,16},{4,12},{8,24},{12,4},{16,0},{20,28},{24,8},{28,20},{1,17},{... | collective-permute-start | bytes 786440 | tf_op jit(solution)/shard_map/ppermute | solution.py:257
  22.0 7.0 %copy-start.2 = (f32[2048,512]{1,0:T(8,128)S(1)}, f32[2048,512]{1,0:T(8,128)}, u32[]{:S(2)}) copy-start(f32[2048,512]{1,0:T(8,128)} %refs_3_.1) | copy-start | bytes 12582916
  22.0 6.9 %copy-start.1 = (f32[2048,512]{1,0:T(8,128)S(1)}, f32[2048,512]{1,0:T(8,128)}, u32[]{:S(2)}) copy-start(f32[2048,512]{1,0:T(8,128)} %refs_2_.1) | copy-start | bytes 12582916
  23.2 5.7 %collective-permute-start.8 = (bf16[256,512]{1,0:T(8,128)(2,1)S(1)}, bf16[256,512]{1,0:T(8,128)(2,1)S(1)}, u32[]{:S(2)}, u32[]{:S(2)}) collective-permute-start(bf16[256,512]{1,0:T(8,128)(2,1)S(1)} %get-tuple-element.55), channel_id=1, source_target_pairs={{0,4},{4,0},{8,12},{12,8},{16,20},{20,16},{24,28},{28,24},{1,5},{5... | collective-permute-start | bytes 786440 | tf_op jit(solution)/shard_map/ppermute | solution.py:257
  23.3 5.6 %collective-permute-start.7 = (bf16[256,512]{1,0:T(8,128)(2,1)S(1)}, bf16[256,512]{1,0:T(8,128)(2,1)S(1)}, u32[]{:S(2)}, u32[]{:S(2)}) collective-permute-start(bf16[256,512]{1,0:T(8,128)(2,1)S(1)} %get-tuple-element.54), channel_id=1, source_target_pairs={{0,4},{4,0},{8,12},{12,8},{16,20},{20,16},{24,28},{28,24},{1,5},{5... | collective-permute-start | bytes 786440 | tf_op jit(solution)/shard_map/ppermute | solution.py:257
  23.8 9.1 %collective-permute-start.10 = (bf16[256,512]{1,0:T(8,128)(2,1)S(1)}, bf16[256,512]{1,0:T(8,128)(2,1)S(1)}, u32[]{:S(2)}, u32[]{:S(2)}) collective-permute-start(bf16[256,512]{1,0:T(8,128)(2,1)S(1)} %get-tuple-element.55), channel_id=1, source_target_pairs={{0,8},{4,20},{8,0},{12,28},{16,24},{20,4},{24,16},{28,12},{1,9},{5... | collective-permute-start | bytes 786440 | tf_op jit(solution)/shard_map/ppermute | solution.py:257
  25.8 7.2 %collective-permute-start.9 = (bf16[256,512]{1,0:T(8,128)(2,1)S(1)}, bf16[256,512]{1,0:T(8,128)(2,1)S(1)}, u32[]{:S(2)}, u32[]{:S(2)}) collective-permute-start(bf16[256,512]{1,0:T(8,128)(2,1)S(1)} %get-tuple-element.54), channel_id=1, source_target_pairs={{0,8},{4,20},{8,0},{12,28},{16,24},{20,4},{24,16},{28,12},{1,9},{5... | collective-permute-start | bytes 786440 | tf_op jit(solution)/shard_map/ppermute | solution.py:257
  25.9 9.1 %collective-permute-start.13 = (f32[64,512]{1,0:T(8,128)S(1)}, f32[64,512]{1,0:T(8,128)S(1)}, u32[]{:S(2)}, u32[]{:S(2)}) collective-permute-start(f32[64,512]{1,0:T(8,128)S(1)} %get-tuple-element.61), channel_id=1, source_target_pairs={{0,2},{1,3},{2,0},{3,1},{4,6},{5,7},{6,4},{7,5},{8,10},{9,11},{10,... | collective-permute-start | bytes 393224 | tf_op jit(solution)/shard_map/ppermute | solution.py:260
  33.0 1.9 %collective-permute-start.11 = (bf16[256,512]{1,0:T(8,128)(2,1)S(1)}, bf16[256,512]{1,0:T(8,128)(2,1)S(1)}, u32[]{:S(2)}, u32[]{:S(2)}) collective-permute-start(bf16[256,512]{1,0:T(8,128)(2,1)S(1)} %get-tuple-element.59), channel_id=1, source_target_pairs={{0,4},{4,0},{8,12},{12,8},{16,20},{20,16},{24,28},{28,24},{1,5},{5... | collective-permute-start | bytes 786440 | tf_op jit(solution)/shard_map/ppermute | solution.py:257
  33.1 1.9 %collective-permute-start.12 = (bf16[256,512]{1,0:T(8,128)(2,1)S(1)}, bf16[256,512]{1,0:T(8,128)(2,1)S(1)}, u32[]{:S(2)}, u32[]{:S(2)}) collective-permute-start(bf16[256,512]{1,0:T(8,128)(2,1)S(1)} %get-tuple-element.60), channel_id=1, source_target_pairs={{0,4},{4,0},{8,12},{12,8},{16,20},{20,16},{24,28},{28,24},{1,5},{5... | collective-permute-start | bytes 786440 | tf_op jit(solution)/shard_map/ppermute | solution.py:257

commit v6 on v5

--- a/solution.py
+++ b/solution.py
@@ -182,7 +182,7 @@
     shard = lax.axis_index("fsdp")
     for d, source, k in ((0, near, 0), (2, near, 1), (1, far, 0), (3, far, 1)):
         rows(portion, shard ^ d, held)[...] = source[k * held : (k + 1) * held, :]
-    for k, which in enumerate([*late, *soon]):
+    for k, which in enumerate([*soon, *late]):
         span = span_of(size, *which)
         weight = weights[span, :]
         grad_weight = lax.dot_general(
@@ -200,13 +200,12 @@
             outer_momentum * outer_momentum * momentum[span, :]
             + (fresh - stale[span, :].astype(jnp.float32)) / workers
         )
-        if k < len(late):
-            bases[k][...] = base
+        if k >= len(soon):
+            bases[k - len(soon)][...] = base
         else:
-            k -= len(late)
             param_buf[k] = finished(which[0], workers, base, sums[k])
             send(param_buf.at[k], param_out.at[span, :])
-        if which is late[-1]:
+        if k == 0:
             _, _, last = place(lax.axis_index("worker"))
             average = jnp.where(last == 0, sums[0][...], sums[1][...]) / workers
             moment[...] = outer_momentum * rows(momentum, lax.axis_index("worker"), size)[...] + average
@@ -233,12 +232,15 @@
     copies = []
     if keys:
         key_buf[...] = (own[...] + received[...]).astype(jnp.bfloat16)
-        copies.append(pltpu.make_async_copy(key_buf, key_out, sem.at[count]))
+        copies.append(pltpu.make_async_copy(key_buf, key_out, sem.at[2 * count]))
         copies[0].start()
     for k, which in enumerate(kinds):
-        out_buf[k] = finished(which[0], workers, bases[k][...], pieces[k])
-        copies.append(pltpu.make_async_copy(out_buf.at[k], out.at[span_of(size, *which), :], sem.at[k]))
-        copies[-1].start()
+        for part in range(2):
+            some = pl.ds(part * (size // 2), size // 2)
+            out_buf[k, some, :] = finished(which[0], workers, bases[k][some, :], pieces[k].at[some, :])
+            there = pl.ds(pl.multiple_of(block(*spots(lax.axis_index("worker"))[which[0]], which[1]) * size + part * (size // 2), size // 2), size // 2)
+            copies.append(pltpu.make_async_copy(out_buf.at[k, some, :], out.at[there, :], sem.at[2 * k + part]))
+            copies[-1].start()
     for copy in copies:
         copy.wait()
 
@@ -365,7 +367,7 @@
             functools.partial(update_kernel, workers, [late_kinds[w] for w in which], with_keys),
             ins,
             outs,
-            scratch=[*scratch, DMA((len(which) + 1,))],
+            scratch=[*scratch, DMA((2 * len(which) + 1,))],
             aliases={len(ins) - 1: 0},
             micros=cost["update"][with_keys],
         )

time: 36.4 us -> 36.4 us (level)
  no operation moved by 1% of the time
where the time goes in v6:
time: 36.4 us; the launch traced here: 36.2 us
  starting transfers between devices  18.5 us (51%)
  Pallas kernels  10.7 us (29%)
  waiting for transfers between devices  6.21 us (17%)
  between operations  0.77 us (2%)
    pallas_call x13, Pallas kernels, call(): pl.pallas_call(body, in_specs=[pl.BlockSpec(memory_space=s) for _, s in i...  10.7 us
    ppermute x11, starting transfers between devices, swap(): lax.ppermute(value, 'worker', [(i, i ^ flips[i % 2]) for i in range(worke...  10.1 us
    ppermute x3, starting transfers between devices, across_shards(): lax.ppermute(value, 'fsdp', [(i, i ^ distance) for i in range(shards)])  8.41 us
    ppermute x3, waiting for transfers between devices, across_shards(): lax.ppermute(value, 'fsdp', [(i, i ^ distance) for i in range(shards)])  4.95 us
    ppermute x11, waiting for transfers between devices, swap(): lax.ppermute(value, 'worker', [(i, i ^ flips[i % 2]) for i in range(worke...  1.26 us
  transfers between devices with their start and end apart: 14, of which 8 were waited for; matrix products, arithmetic and copies ran while one was open for 0% of the time, Pallas kernels for 25%

profile of v6, /device:TPU:0, one launch (start us, length us, event | category | flops | bytes accessed | tf_op | source)
XLA Modules:
  0.0 36.2 jit_solution(15990145128679019127)
XLA Ops:
  0.6 0.5 %collective-permute-start.1 = (bf16[2048,512]{1,0:T(8,128)(2,1)}, bf16[2048,512]{1,0:T(8,128)(2,1)S(1)}, u32[]{:S(2)}, u32[]{:S(2)}) collective-permute-start(bf16[2048,512]{1,0:T(8,128)(2,1)} %bitcast.6), channel_id=1, source_target_pairs={{0,4},{4,0},{8,12},{12,8},{16,20},{20,16},{24,28},{28,24},{1,5},{5... | collective-permute-start | bytes 6291464 | tf_op jit(solution)/shard_map/ppermute | solution.py:259
  1.1 1.2 %shard_map.101 = (bf16[512,512]{1,0:T(8,128)(2,1)S(1)}, bf16[512,512]{1,0:T(8,128)(2,1)S(1)}, bf16[64,512]{1,0:T(8,128)(2,1)S(1)}) custom-call(bf16[2048,512]{1,0:T(8,128)(2,1)} %bitcast.7, bf16[64,512]{1,0:T(8,128)(2,1)} %refs_1_.1), custom_call_target="tpu_custom_call" | custom-call | flops 1000000000 | tf_op jit(solution)/shard_map/pallas_call | solution.py:67
  2.4 3.7 %collective-permute-start = (bf16[64,512]{1,0:T(8,128)(2,1)S(1)}, bf16[64,512]{1,0:T(8,128)(2,1)S(1)}, u32[]{:S(2)}, u32[]{:S(2)}) collective-permute-start(bf16[64,512]{1,0:T(8,128)(2,1)S(1)} %get-tuple-element.37.refs_2_), channel_id=1, source_target_pairs={{0,2},{1,3},{2,0},{3,1},{4,6},{5,7},{6,4},{7,5},{8,10},{9,11},{10,... | collective-permute-start | bytes 196616 | tf_op jit(solution)/shard_map/ppermute | solution.py:262
  6.1 0.3 shard_map.102
  6.4 2.0 %collective-permute-start.3 = (bf16[256,512]{1,0:T(8,128)(2,1)S(1)}, bf16[256,512]{1,0:T(8,128)(2,1)S(1)}, u32[]{:S(2)}, u32[]{:S(2)}) collective-permute-start(bf16[256,512]{1,0:T(8,128)(2,1)S(1)} %get-tuple-element.43), channel_id=1, source_target_pairs={{0,8},{4,20},{8,0},{12,28},{16,24},{20,4},{24,16},{28,12},{1,9},{5... | collective-permute-start | bytes 786440 | tf_op jit(solution)/shard_map/ppermute | solution.py:259
  8.4 0.3 shard_map.103
  8.7 0.2 collective-permute-start.5
  8.9 1.3 %collective-permute-done.refs_3_ = bf16[64,512]{1,0:T(8,128)(2,1)S(1)} collective-permute-done((bf16[64,512]{1,0:T(8,128)(2,1)S(1)}, bf16[64,512]{1,0:T(8,128)(2,1)S(1)}, u32[]{:S(2)}, u32[]{:S(2)}) %collective-permute-start) | collective-permute-done | bytes 65568 | tf_op jit(solution)/shard_map/ppermute | solution.py:262
  10.2 0.8 %shard_map.104 = (bf16[384,512]{1,0:T(8,128)(2,1)S(1)}, f32[64,512]{1,0:T(8,128)S(1)}, f32[64,512]{1,0:T(8,128)S(1)}) custom-call(bf16[256,2048]{1,0:T(8,128)(2,1)S(1)} %copy-done.3, bf16[2048,512]{1,0:T(8,128)(2,1)S(1)} %bitcast.4, bf16[64,512]{1,0:T(8,128)(2,1)S(1)} %get-tuple-element.37.refs_2_, bf16[64,512]{1,0:T(8,128)(2,1)S(1)} %collective-permute-done.refs_3_, ...), custom_call_target="tpu_custom_call" | custom-call | flops 200000000 | tf_op jit(solution)/shard_map/pallas_call | solution.py:67
  11.0 1.6 %collective-permute-start.2 = (bf16[384,512]{1,0:T(8,128)(2,1)S(1)}, bf16[384,512]{1,0:T(8,128)(2,1)S(1)}, u32[]{:S(2)}, u32[]{:S(2)}) collective-permute-start(bf16[384,512]{1,0:T(8,128)(2,1)S(1)} %get-tuple-element.42.refs_3_.refs_5_), channel_id=1, source_target_pairs={{0,1},{1,0},{2,3},{3,2},{4,5},{5,4},{6,7},{7,6},{8,9},{9,8},{10,11... | collective-permute-start | bytes 1179656 | tf_op jit(solution)/shard_map/ppermute | solution.py:262
  12.6 0.2 collective-permute-done.3.refs_1_
  12.8 0.4 %shard_map.105 = (f32[256,512]{1,0:T(8,128)S(1)}, bf16[256,512]{1,0:T(8,128)(2,1)S(1)}) custom-call(f32[256,512]{1,0:T(8,128)S(1)} %get-tuple-element.40.refs_2_.refs_0_, bf16[256,512]{1,0:T(8,128)(2,1)S(1)} %collective-permute-done.3.refs_1_), custom_call_target="tpu_custom_call" | custom-call | flops 1000000000 | tf_op jit(solution)/shard_map/pallas_call | solution.py:67
  13.3 2.0 %collective-permute-start.4 = (bf16[256,512]{1,0:T(8,128)(2,1)S(1)}, bf16[256,512]{1,0:T(8,128)(2,1)S(1)}, u32[]{:S(2)}, u32[]{:S(2)}) collective-permute-start(bf16[256,512]{1,0:T(8,128)(2,1)S(1)} %get-tuple-element.45), channel_id=1, source_target_pairs={{0,16},{4,12},{8,24},{12,4},{16,0},{20,28},{24,8},{28,20},{1,17},{... | collective-permute-start | bytes 786440 | tf_op jit(solution)/shard_map/ppermute | solution.py:259
  15.3 0.5 %collective-permute-done.5.refs_1_ = bf16[256,512]{1,0:T(8,128)(2,1)S(1)} collective-permute-done((bf16[256,512]{1,0:T(8,128)(2,1)S(1)}, bf16[256,512]{1,0:T(8,128)(2,1)S(1)}, u32[]{:S(2)}, u32[]{:S(2)}) %collective-permute-start.5) | collective-permute-done | bytes 262176 | tf_op jit(solution)/shard_map/ppermute | solution.py:259
  15.8 0.4 %shard_map.107 = (f32[256,512]{1,0:T(8,128)S(1)}, bf16[256,512]{1,0:T(8,128)(2,1)S(1)}) custom-call(f32[256,512]{1,0:T(8,128)S(1)} %get-tuple-element.41.refs_4_.refs_0_, bf16[256,512]{1,0:T(8,128)(2,1)S(1)} %collective-permute-done.5.refs_1_, f32[256,512]{1,0:T(8,128)S(1)} %get-tuple-element.44.refs_0_.refs_2_, ...), custom_call_target="tpu_custom_call" | custom-call | flops 1000000000 | tf_op jit(solution)/shard_map/pallas_call | solution.py:67
  16.2 2.2 %collective-permute-start.6 = (bf16[256,512]{1,0:T(8,128)(2,1)S(1)}, bf16[256,512]{1,0:T(8,128)(2,1)S(1)}, u32[]{:S(2)}, u32[]{:S(2)}) collective-permute-start(bf16[256,512]{1,0:T(8,128)(2,1)S(1)} %get-tuple-element.49), channel_id=1, source_target_pairs={{0,16},{4,12},{8,24},{12,4},{16,0},{20,28},{24,8},{28,20},{1,17},{... | collective-permute-start | bytes 786440 | tf_op jit(solution)/shard_map/ppermute | solution.py:259
  18.5 3.5 %collective-permute-done.2.refs_0_.refs_6_ = bf16[384,512]{1,0:T(8,128)(2,1)S(1)} collective-permute-done((bf16[384,512]{1,0:T(8,128)(2,1)S(1)}, bf16[384,512]{1,0:T(8,128)(2,1)S(1)}, u32[]{:S(2)}, u32[]{:S(2)}) %collective-permute-start.2) | collective-permute-done | bytes 393248 | tf_op jit(solution)/shard_map/ppermute | solution.py:262
  22.0 0.4 %shard_map.106 = (f32[256,512]{1,0:T(8,128)S(1)}, bf16[256,512]{1,0:T(8,128)(2,1)S(1)}) custom-call(f32[256,512]{1,0:T(8,128)S(1)} %get-tuple-element.44.refs_0_.refs_2_, bf16[256,512]{1,0:T(8,128)(2,1)S(1)} %collective-permute-done.4.refs_1_), custom_call_target="tpu_custom_call" | custom-call | flops 1000000000 | tf_op jit(solution)/shard_map/pallas_call | solution.py:67
  22.5 0.3 collective-permute-done.6.refs_1_
  22.8 0.4 %shard_map.109 = (f32[256,512]{1,0:T(8,128)S(1)}, bf16[256,512]{1,0:T(8,128)(2,1)S(1)}) custom-call(f32[256,512]{1,0:T(8,128)S(1)} %get-tuple-element.48.refs_3_.refs_0_, bf16[256,512]{1,0:T(8,128)(2,1)S(1)} %collective-permute-done.6.refs_1_, f32[256,512]{1,0:T(8,128)S(1)} %get-tuple-element.46.refs_2_.refs_7_, f32[64,512]{1,0:T(8,128)S(1)} %get-tuple-element.52.refs_3_.refs_4_), custom_call_target="tpu_custom_call" | custom-call | flops 1000000000 | tf_op jit(solution)/shard_map/pallas_call | solution.py:67
  23.2 0.1 collective-permute-start.8
  23.3 0.5 %collective-permute-start.7 = (bf16[256,512]{1,0:T(8,128)(2,1)S(1)}, bf16[256,512]{1,0:T(8,128)(2,1)S(1)}, u32[]{:S(2)}, u32[]{:S(2)}) collective-permute-start(bf16[256,512]{1,0:T(8,128)(2,1)S(1)} %get-tuple-element.54), channel_id=1, source_target_pairs={{0,4},{4,0},{8,12},{12,8},{16,20},{20,16},{24,28},{28,24},{1,5},{5... | collective-permute-start | bytes 786440 | tf_op jit(solution)/shard_map/ppermute | solution.py:259
  23.8 2.0 %collective-permute-start.10 = (bf16[256,512]{1,0:T(8,128)(2,1)S(1)}, bf16[256,512]{1,0:T(8,128)(2,1)S(1)}, u32[]{:S(2)}, u32[]{:S(2)}) collective-permute-start(bf16[256,512]{1,0:T(8,128)(2,1)S(1)} %get-tuple-element.55), channel_id=1, source_target_pairs={{0,8},{4,20},{8,0},{12,28},{16,24},{20,4},{24,16},{28,12},{1,9},{5... | collective-permute-start | bytes 786440 | tf_op jit(solution)/shard_map/ppermute | solution.py:259
  25.9 3.1 %collective-permute-start.13 = (f32[64,512]{1,0:T(8,128)S(1)}, f32[64,512]{1,0:T(8,128)S(1)}, u32[]{:S(2)}, u32[]{:S(2)}) collective-permute-start(f32[64,512]{1,0:T(8,128)S(1)} %get-tuple-element.61), channel_id=1, source_target_pairs={{0,2},{1,3},{2,0},{3,1},{4,6},{5,7},{6,4},{7,5},{8,10},{9,11},{10,... | collective-permute-start | bytes 393224 | tf_op jit(solution)/shard_map/ppermute | solution.py:262
  29.0 3.9 %shard_map.110 = (bf16[2048,512]{1,0:T(8,128)(2,1)}, bf16[256,2048]{1,0:T(8,128)(2,1)}, bf16[2048,512]{1,0:T(8,128)(2,1)}, f32[256,512]{1,0:T(8,128)}, f32[256,5...) custom-call(bf16[256,2048]{1,0:T(8,128)(2,1)S(1)} %copy-done.3, ...), custom_call_target="tpu_custom_call" | custom-call | flops 600000000 | tf_op jit(solution)/shard_map/pallas_call | solution.py:67
  32.9 0.1 collective-permute-done.9.refs_0_.refs_2_
  33.0 0.1 collective-permute-start.11
  33.1 0.5 %collective-permute-start.12 = (bf16[256,512]{1,0:T(8,128)(2,1)S(1)}, bf16[256,512]{1,0:T(8,128)(2,1)S(1)}, u32[]{:S(2)}, u32[]{:S(2)}) collective-permute-start(bf16[256,512]{1,0:T(8,128)(2,1)S(1)} %get-tuple-element.60), channel_id=1, source_target_pairs={{0,4},{4,0},{8,12},{12,8},{16,20},{20,16},{24,28},{28,24},{1,5},{5... | collective-permute-start | bytes 786440 | tf_op jit(solution)/shard_map/ppermute | solution.py:259
  33.6 1.2 %shard_map.112.refs_6_ = bf16[2048,512]{1,0:T(8,128)(2,1)} custom-call(f32[256,512]{1,0:T(8,128)S(1)} %get-tuple-element.58.refs_2_.refs_0_, f32[256,512]{1,0:T(8,128)S(1)} %get-tuple-element.62.refs_1_, bf16[256,512]{1,0:T(8,128)(2,1)S(1)} %collective-permute-done.9.refs_0_.refs_2_, ...), custom_call_target="tpu_custom_call", output_to_operand_aliasing={{}: (4, {})} | custom-call | flops 16000000000 | tf_op jit(solution)/shard_map/pallas_call | solution.py:67
  34.8 0.1 collective-permute-done.13.refs_5_
  34.9 0.1 collective-permute-done.12.refs_3_
  35.0 1.2 %shard_map.113 = (bf16[2048,512]{1,0:T(8,128)(2,1)}, bf16[64,512]{1,0:T(8,128)(2,1)}) custom-call(f32[256,512]{1,0:T(8,128)S(1)} %get-tuple-element.56.refs_0_, f32[256,512]{1,0:T(8,128)S(1)} %get-tuple-element.57.refs_1_, bf16[256,512]{1,0:T(8,128)(2,1)S(1)} %collective-permute-done.11.refs_2_, ...), custom_call_target="tpu_custom_call", output_to_operand_aliasing={{0}: (6, {})} | custom-call | flops 16000000000 | tf_op jit(solution)/shard_map/pallas_call | solution.py:67
  (19 shorter events, 0.2 us)
Async XLA Ops:
  0.6 5.5 %collective-permute-start.1 = (bf16[2048,512]{1,0:T(8,128)(2,1)}, bf16[2048,512]{1,0:T(8,128)(2,1)S(1)}, u32[]{:S(2)}, u32[]{:S(2)}) collective-permute-start(bf16[2048,512]{1,0:T(8,128)(2,1)} %bitcast.6), channel_id=1, source_target_pairs={{0,4},{4,0},{8,12},{12,8},{16,20},{20,16},{24,28},{28,24},{1,5},{5... | collective-permute-start | bytes 6291464 | tf_op jit(solution)/shard_map/ppermute | solution.py:259
  2.4 7.8 %collective-permute-start = (bf16[64,512]{1,0:T(8,128)(2,1)S(1)}, bf16[64,512]{1,0:T(8,128)(2,1)S(1)}, u32[]{:S(2)}, u32[]{:S(2)}) collective-permute-start(bf16[64,512]{1,0:T(8,128)(2,1)S(1)} %get-tuple-element.37.refs_2_), channel_id=1, source_target_pairs={{0,2},{1,3},{2,0},{3,1},{4,6},{5,7},{6,4},{7,5},{8,10},{9,11},{10,... | collective-permute-start | bytes 196616 | tf_op jit(solution)/shard_map/ppermute | solution.py:262
  6.4 6.4 %collective-permute-start.3 = (bf16[256,512]{1,0:T(8,128)(2,1)S(1)}, bf16[256,512]{1,0:T(8,128)(2,1)S(1)}, u32[]{:S(2)}, u32[]{:S(2)}) collective-permute-start(bf16[256,512]{1,0:T(8,128)(2,1)S(1)} %get-tuple-element.43), channel_id=1, source_target_pairs={{0,8},{4,20},{8,0},{12,28},{16,24},{20,4},{24,16},{28,12},{1,9},{5... | collective-permute-start | bytes 786440 | tf_op jit(solution)/shard_map/ppermute | solution.py:259
  8.4 1.8 %copy-start = (bf16[1,2048,512]{2,1,0:T(8,128)(2,1)S(1)}, bf16[1,2048,512]{2,1,0:T(8,128)(2,1)}, u32[]{:S(2)}) copy-start(bf16[1,2048,512]{2,1,0:T(8,128)(2,1)} %param.7) | copy-start | bytes 6291460
  8.4 1.9 %copy-start.3 = (bf16[256,2048]{1,0:T(8,128)(2,1)S(1)}, bf16[256,2048]{1,0:T(8,128)(2,1)}, u32[]{:S(2)}) copy-start(bf16[256,2048]{1,0:T(8,128)(2,1)} %refs_0_.3) | copy-start | bytes 3145732
  8.7 7.1 %collective-permute-start.5 = (bf16[256,512]{1,0:T(8,128)(2,1)S(1)}, bf16[256,512]{1,0:T(8,128)(2,1)S(1)}, u32[]{:S(2)}, u32[]{:S(2)}) collective-permute-start(bf16[256,512]{1,0:T(8,128)(2,1)S(1)} %get-tuple-element.47), channel_id=1, source_target_pairs={{0,8},{4,20},{8,0},{12,28},{16,24},{20,4},{24,16},{28,12},{1,9},{5... | collective-permute-start | bytes 786440 | tf_op jit(solution)/shard_map/ppermute | solution.py:259
  11.0 11.0 %collective-permute-start.2 = (bf16[384,512]{1,0:T(8,128)(2,1)S(1)}, bf16[384,512]{1,0:T(8,128)(2,1)S(1)}, u32[]{:S(2)}, u32[]{:S(2)}) collective-permute-start(bf16[384,512]{1,0:T(8,128)(2,1)S(1)} %get-tuple-element.42.refs_3_.refs_5_), channel_id=1, source_target_pairs={{0,1},{1,0},{2,3},{3,2},{4,5},{5,4},{6,7},{7,6},{8,9},{9,8},{10,11... | collective-permute-start | bytes 1179656 | tf_op jit(solution)/shard_map/ppermute | solution.py:262
  13.3 8.8 %collective-permute-start.4 = (bf16[256,512]{1,0:T(8,128)(2,1)S(1)}, bf16[256,512]{1,0:T(8,128)(2,1)S(1)}, u32[]{:S(2)}, u32[]{:S(2)}) collective-permute-start(bf16[256,512]{1,0:T(8,128)(2,1)S(1)} %get-tuple-element.45), channel_id=1, source_target_pairs={{0,16},{4,12},{8,24},{12,4},{16,0},{20,28},{24,8},{28,20},{1,17},{... | collective-permute-start | bytes 786440 | tf_op jit(solution)/shard_map/ppermute | solution.py:259
  15.8 13.2 %copy-start.4 = (bf16[1,2048,512]{2,1,0:T(8,128)(2,1)S(1)}, bf16[1,2048,512]{2,1,0:T(8,128)(2,1)}, u32[]{:S(2)}) copy-start(bf16[1,2048,512]{2,1,0:T(8,128)(2,1)} %param.11) | copy-start | bytes 6291460
  16.2 6.6 %collective-permute-start.6 = (bf16[256,512]{1,0:T(8,128)(2,1)S(1)}, bf16[256,512]{1,0:T(8,128)(2,1)S(1)}, u32[]{:S(2)}, u32[]{:S(2)}) collective-permute-start(bf16[256,512]{1,0:T(8,128)(2,1)S(1)} %get-tuple-element.49), channel_id=1, source_target_pairs={{0,16},{4,12},{8,24},{12,4},{16,0},{20,28},{24,8},{28,20},{1,17},{... | collective-permute-start | bytes 786440 | tf_op jit(solution)/shard_map/ppermute | solution.py:259
  22.0 7.0 %copy-start.2 = (f32[2048,512]{1,0:T(8,128)S(1)}, f32[2048,512]{1,0:T(8,128)}, u32[]{:S(2)}) copy-start(f32[2048,512]{1,0:T(8,128)} %refs_3_.1) | copy-start | bytes 12582916
  22.0 6.9 %copy-start.1 = (f32[2048,512]{1,0:T(8,128)S(1)}, f32[2048,512]{1,0:T(8,128)}, u32[]{:S(2)}) copy-start(f32[2048,512]{1,0:T(8,128)} %refs_2_.1) | copy-start | bytes 12582916
  23.2 5.7 %collective-permute-start.8 = (bf16[256,512]{1,0:T(8,128)(2,1)S(1)}, bf16[256,512]{1,0:T(8,128)(2,1)S(1)}, u32[]{:S(2)}, u32[]{:S(2)}) collective-permute-start(bf16[256,512]{1,0:T(8,128)(2,1)S(1)} %get-tuple-element.55), channel_id=1, source_target_pairs={{0,4},{4,0},{8,12},{12,8},{16,20},{20,16},{24,28},{28,24},{1,5},{5... | collective-permute-start | bytes 786440 | tf_op jit(solution)/shard_map/ppermute | solution.py:259
  23.3 5.6 %collective-permute-start.7 = (bf16[256,512]{1,0:T(8,128)(2,1)S(1)}, bf16[256,512]{1,0:T(8,128)(2,1)S(1)}, u32[]{:S(2)}, u32[]{:S(2)}) collective-permute-start(bf16[256,512]{1,0:T(8,128)(2,1)S(1)} %get-tuple-element.54), channel_id=1, source_target_pairs={{0,4},{4,0},{8,12},{12,8},{16,20},{20,16},{24,28},{28,24},{1,5},{5... | collective-permute-start | bytes 786440 | tf_op jit(solution)/shard_map/ppermute | solution.py:259
  23.8 9.0 %collective-permute-start.10 = (bf16[256,512]{1,0:T(8,128)(2,1)S(1)}, bf16[256,512]{1,0:T(8,128)(2,1)S(1)}, u32[]{:S(2)}, u32[]{:S(2)}) collective-permute-start(bf16[256,512]{1,0:T(8,128)(2,1)S(1)} %get-tuple-element.55), channel_id=1, source_target_pairs={{0,8},{4,20},{8,0},{12,28},{16,24},{20,4},{24,16},{28,12},{1,9},{5... | collective-permute-start | bytes 786440 | tf_op jit(solution)/shard_map/ppermute | solution.py:259
  25.8 7.2 %collective-permute-start.9 = (bf16[256,512]{1,0:T(8,128)(2,1)S(1)}, bf16[256,512]{1,0:T(8,128)(2,1)S(1)}, u32[]{:S(2)}, u32[]{:S(2)}) collective-permute-start(bf16[256,512]{1,0:T(8,128)(2,1)S(1)} %get-tuple-element.54), channel_id=1, source_target_pairs={{0,8},{4,20},{8,0},{12,28},{16,24},{20,4},{24,16},{28,12},{1,9},{5... | collective-permute-start | bytes 786440 | tf_op jit(solution)/shard_map/ppermute | solution.py:259
  25.9 9.1 %collective-permute-start.13 = (f32[64,512]{1,0:T(8,128)S(1)}, f32[64,512]{1,0:T(8,128)S(1)}, u32[]{:S(2)}, u32[]{:S(2)}) collective-permute-start(f32[64,512]{1,0:T(8,128)S(1)} %get-tuple-element.61), channel_id=1, source_target_pairs={{0,2},{1,3},{2,0},{3,1},{4,6},{5,7},{6,4},{7,5},{8,10},{9,11},{10,... | collective-permute-start | bytes 393224 | tf_op jit(solution)/shard_map/ppermute | solution.py:262
  33.0 1.9 %collective-permute-start.11 = (bf16[256,512]{1,0:T(8,128)(2,1)S(1)}, bf16[256,512]{1,0:T(8,128)(2,1)S(1)}, u32[]{:S(2)}, u32[]{:S(2)}) collective-permute-start(bf16[256,512]{1,0:T(8,128)(2,1)S(1)} %get-tuple-element.59), channel_id=1, source_target_pairs={{0,4},{4,0},{8,12},{12,8},{16,20},{20,16},{24,28},{28,24},{1,5},{5... | collective-permute-start | bytes 786440 | tf_op jit(solution)/shard_map/ppermute | solution.py:259
  33.1 1.9 %collective-permute-start.12 = (bf16[256,512]{1,0:T(8,128)(2,1)S(1)}, bf16[256,512]{1,0:T(8,128)(2,1)S(1)}, u32[]{:S(2)}, u32[]{:S(2)}) collective-permute-start(bf16[256,512]{1,0:T(8,128)(2,1)S(1)} %get-tuple-element.60), channel_id=1, source_target_pairs={{0,4},{4,0},{8,12},{12,8},{16,20},{20,16},{24,28},{28,24},{1,5},{5... | collective-permute-start | bytes 786440 | tf_op jit(solution)/shard_map/ppermute | solution.py:259
